TPU v7x, 128 devices: a whole 4x4x4 slice. The times are simulated.
128 devices in a mesh: cells: 128 (over x, y, z, core).
Axes of the slice: x: 4, y: 4, z: 4, core: 2. Of those that a mesh axis runs over, the one named last changes fastest.
Arguments:
- state_deviation: bfloat16 [540, 262144], P(None, 'cells'), may hold values from -6 to 6
- forcing: bfloat16 [90, 262144], P(None, 'cells'), may hold values from -6 to 6
- trajectory: bfloat16 [540, 65536], P(None, 'cells'), may hold values from -6 to 6
- w_in: bfloat16 [540, 256], replicated, may hold values from -0.25 to 0.25
- w_hidden: bfloat16 [2, 256, 256], replicated, may hold values from -0.375 to 0.375
- w_out: bfloat16 [256, 90], replicated, may hold values from -0.375 to 0.375
- biases: float32 [3, 256], replicated, may hold values from -3 to 3
- fine_order: int32 [128, 2048], P('cells'), may hold values from 0 to 2047, each once within a row
- group_parent: int32 [128, 512], P('cells'), may hold values from 0 to 65535, as said below
- daylit_counts: int32 [128], replicated, may hold values from 0 to 512, as said below
- sun_rank: int32 [128, 512], P('cells'), may hold values from 0 to 511, each once within a row
- adjacent_source_slots: int32 [6, 262144], P(None, 'cells'), may hold values from 0 to 2559, as said below
- outgoing_local_lists: int32 [128, 2, 256], P('cells'), may hold values from 0 to 2047, as said below
Outputs:
- tl_temperature: float32 [90, 262144], P(None, 'cells')
- forcing_sensitivity_vector: bfloat16 [540, 262144], P(None, 'cells')
Inputs may be any that keep to these rules, and one draw needn't show every extreme that they name: `fine_order`: each row is a permutation of the fine cells of one device. `group_parent`: every radiation column is the parent of exactly one group; at most 8 groups of one device have their columns on any one device, and in every draw 8 do for every device. `daylit_counts`: the counts of device i and of device i xor (half the number of devices) sum to 512 or less, to exactly 512 for some pair. `sun_rank`: each row is a permutation. `adjacent_source_slots`: entries below 2048 are own cells, 2048 to 2303 the cells received from the device below, the rest those from the device above; within one of the six rows, the cells of one device never name the same entry twice. `outgoing_local_lists`: each list holds 256 distinct local cells.
All inputs are finite; a program needn't handle non-finite values.
Results may differ from a plain program's by a relative error of at most 0.01.
Values may be sent and summed in bfloat16 or wider, within the bound.
No kernel may reach another device: no remote copies, remote signals or barrier semaphores. Data moves between devices by JAX's collectives and lax.ppermute only.
A program may use at most 128 MiB of HBM per device.

v0:
```python
import jax
import jax.numpy as jnp
from jax import lax
from jax.sharding import PartitionSpec as P

SUBSTEPS = 3


spreading_coefficient = 0.125


def extended(x, sides, width):
    for axis, dim in sides:
        size, length = (lax.axis_size(axis), x.shape[dim])
        up = [(i, (i + 1) % size) for i in range(size)]
        down = [(j, i) for i, j in up]
        last = lax.slice_in_dim(x, length - width, length, axis=dim)
        initial = lax.slice_in_dim(x, 0, width, axis=dim)
        before = lax.ppermute(last, axis, up)
        after = lax.ppermute(initial, axis, down)
        x = jnp.concatenate([before, x, after], axis=dim)
    return x


def contract(weight, operand):
    return lax.dot_general(
        weight, operand, (((0,), (0,)), ((), ())), preferred_element_type=jnp.float32
    )


def network_pass(inputs, daylit, tangent, adjoint, w_in, w_hidden, w_out, biases):
    act_one = jnp.tanh(contract(w_in, inputs) + biases[0][:, None])
    act_two = jnp.tanh(contract(w_hidden[0], act_one.astype(jnp.bfloat16)) + biases[1][:, None])
    act_three = jnp.tanh(contract(w_hidden[1], act_two.astype(jnp.bfloat16)) + biases[2][:, None])
    slope_one = 1.0 - act_one * act_one
    slope_two = 1.0 - act_two * act_two
    slope_three = 1.0 - act_three * act_three
    forward = (slope_one * contract(w_in, tangent)).astype(jnp.bfloat16)
    forward = (slope_two * contract(w_hidden[0], forward)).astype(jnp.bfloat16)
    forward = (slope_three * contract(w_hidden[1], forward)).astype(jnp.bfloat16)
    heating = (daylit[None, :] * contract(w_out, forward)).astype(jnp.bfloat16)
    backward = (slope_three * jnp.dot(w_out, adjoint, preferred_element_type=jnp.float32)).astype(
        jnp.bfloat16
    )
    backward = (
        slope_two * jnp.dot(w_hidden[1], backward, preferred_element_type=jnp.float32)
    ).astype(jnp.bfloat16)
    backward = (
        slope_one * jnp.dot(w_hidden[0], backward, preferred_element_type=jnp.float32)
    ).astype(jnp.bfloat16)
    sensitivity = jnp.dot(w_in, backward, preferred_element_type=jnp.float32).astype(jnp.bfloat16)
    return (heating, sensitivity)


def pick_columns(values, index):
    return jnp.take(values.T, index, axis=0, mode="fill", fill_value=0).T


def gather_groups(values, children):
    rows = values.T
    overall_reduction_sum = rows[children[:, 0]].astype(jnp.float32)
    for member in range(1, 4):
        overall_reduction_sum = overall_reduction_sum + rows[children[:, member]].astype(
            jnp.float32
        )
    return overall_reduction_sum.T


def local(
    state_deviation,
    forcing,
    trajectory,
    w_in,
    w_hidden,
    w_out,
    biases,
    fine_order,
    group_parent,
    daylit_counts,
    sun_rank,
    adjacent_source_slots,
    outgoing_local_lists,
):
    column_layer_count, fine_cells = forcing.shape
    features, coarse_cells = trajectory.shape
    devices = lax.axis_size("cells")
    capacity = 2 * coarse_cells // devices
    my_index = lax.axis_index("cells")
    order_local = fine_order[0]
    inverse = (
        jnp.zeros((fine_cells,), jnp.int32)
        .at[order_local]
        .set(jnp.arange(fine_cells, dtype=jnp.int32))
    )
    children = inverse.reshape(coarse_cells, 4)
    group_of = order_local // 4
    parents = group_parent[0]
    target = parents // coarse_cells
    matches = (target[:, None] == jnp.arange(devices, dtype=jnp.int32)[None, :]).astype(jnp.int32)
    earlier = jnp.cumsum(matches, axis=0) - matches
    send_slot = target * capacity + jnp.sum(earlier * matches, axis=1)
    route_table = (
        jnp.full((devices * capacity,), coarse_cells, jnp.int32)
        .at[send_slot]
        .set(parents % coarse_cells)
    )
    slot_group = (
        jnp.full((devices * capacity,), coarse_cells, jnp.int32)
        .at[send_slot]
        .set(jnp.arange(coarse_cells, dtype=jnp.int32))
    )
    arrived = lax.all_to_all(route_table, "cells", split_axis=0, concat_axis=0, tiled=True)
    daylit = (sun_rank[0] < daylit_counts[my_index]).astype(jnp.float32)
    borrowed_slot_number = jnp.concatenate([outgoing_local_lists[0, 0], outgoing_local_lists[0, 1]])
    padding_breadth = outgoing_local_lists.shape[2]
    extended_count = fine_cells + 2 * padding_breadth
    cell_numbers = jnp.arange(fine_cells, dtype=jnp.int32)
    reverse_links = [
        jnp.full((extended_count,), fine_cells, jnp.int32)
        .at[adjacent_source_slots[link_index]]
        .set(cell_numbers)
        for link_index in range(6)
    ]
    adjoint = forcing.astype(jnp.float32)
    heat_back = adjoint
    for substep in range(SUBSTEPS):
        scaled = spreading_coefficient * adjoint
        scaled_rows = jnp.concatenate(
            [scaled.T, jnp.zeros((1, column_layer_count), jnp.float32)], axis=0
        )
        spread_rows = scaled_rows[reverse_links[0]]
        for spread_link_index in range(1, 6):
            spread_rows = spread_rows + scaled_rows[reverse_links[spread_link_index]]
        spread = spread_rows.T
        returned = extended(
            spread[:, fine_cells:].astype(jnp.bfloat16), (("cells", 1),), padding_breadth
        ).astype(jnp.float32)
        result = adjoint - 6.0 * scaled + spread[:, :fine_cells]
        incoming_sums = jnp.concatenate(
            [returned[:, :padding_breadth], returned[:, 3 * padding_breadth :]], axis=1
        )
        adjoint = result.T.at[borrowed_slot_number].add(incoming_sums.T).T
        if substep + 1 < SUBSTEPS:
            heat_back = heat_back + adjoint
    tangent_group = (gather_groups(state_deviation, children) * 0.25).astype(jnp.bfloat16)
    back_group = gather_groups(heat_back, children).astype(jnp.bfloat16)

    def pack_fine(values):
        return pick_columns(values, slot_group)

    def unpack_fine(values):
        return pick_columns(values, send_slot)

    def pack_coarse(values):
        return pick_columns(values, arrived)

    lifted = (
        lax.all_to_all(pack_fine(tangent_group), "cells", split_axis=1, concat_axis=1, tiled=True),
        lax.all_to_all(pack_fine(back_group), "cells", split_axis=1, concat_axis=1, tiled=True),
    )
    arrival_slot = (
        jnp.zeros((coarse_cells,), jnp.int32)
        .at[arrived]
        .set(jnp.arange(devices * capacity, dtype=jnp.int32), mode="drop")
    )
    tangent_in = pick_columns(lifted[0], arrival_slot)
    back_in = (daylit[None, :] * pick_columns(lifted[1], arrival_slot).astype(jnp.float32)).astype(
        jnp.bfloat16
    )
    heating, sensitivity = network_pass(
        trajectory, daylit, tangent_in, back_in, w_in, w_hidden, w_out, biases
    )
    lowered = (
        lax.all_to_all(pack_coarse(heating), "cells", split_axis=1, concat_axis=1, tiled=True),
        lax.all_to_all(pack_coarse(sensitivity), "cells", split_axis=1, concat_axis=1, tiled=True),
    )
    heat_group = unpack_fine(lowered[0])
    sens_group = unpack_fine(lowered[1])
    warming_detailed_sites = pick_columns(heat_group, group_of).astype(jnp.float32)
    atmospheric_warmth = state_deviation[:column_layer_count].astype(jnp.float32)
    for substep in range(SUBSTEPS):
        padding_sites = pick_columns(atmospheric_warmth, borrowed_slot_number)
        edge_sites_list = extended(
            padding_sites.astype(jnp.bfloat16), (("cells", 1),), padding_breadth
        ).astype(padding_sites.dtype)
        extended_rows = jnp.concatenate(
            [
                atmospheric_warmth.T,
                edge_sites_list[:, :padding_breadth].T,
                edge_sites_list[:, 3 * padding_breadth :].T,
            ],
            axis=0,
        )
        overall_reduction_sum = extended_rows[adjacent_source_slots[0]]
        for spreading_link_index in range(1, 6):
            overall_reduction_sum = (
                overall_reduction_sum + extended_rows[adjacent_source_slots[spreading_link_index]]
            )
        atmospheric_warmth = (
            atmospheric_warmth
            + spreading_coefficient * (overall_reduction_sum.T - 6.0 * atmospheric_warmth)
            + warming_detailed_sites
        )
    forcing_sensitivity_vector = pick_columns(sens_group, group_of).astype(jnp.float32) * 0.25
    forcing_sensitivity_vector = forcing_sensitivity_vector.at[:column_layer_count].add(adjoint)
    return (atmospheric_warmth, forcing_sensitivity_vector.astype(jnp.bfloat16))


def solution(mesh):
    return jax.shard_map(
        local,
        mesh=mesh,
        in_specs=(
            P(None, "cells"),
            P(None, "cells"),
            P(None, "cells"),
            P(),
            P(),
            P(),
            P(),
            P("cells", None),
            P("cells", None),
            P(),
            P("cells", None),
            P(None, "cells"),
            P("cells", None, None),
        ),
        out_specs=(P(None, "cells"), P(None, "cells")),
        check_vma=False,
    )
```

profile of v0, /device:TPU:0, one launch (start us, length us, event | category | flops | bytes accessed | tf_op | source)
XLA Modules:
  0.0 580.2 jit_solution(11226162748066900816)
XLA Ops:
  10.7 8.2 %collective-permute-start.1 = (bf16[90,256]{0,1:T(8,128)(2,1)}, bf16[90,256]{0,1:T(8,128)(2,1)}, u32[]{:S(2)}, u32[]{:S(2)}) collective-permute-start(bf16[90,256]{0,1:T(8,128)(2,1)} %get-tuple-element.62), channel_id=1, source_target_pairs={{1,0},{2,1},{3,2},{4,3},{5,4},{6,5},{7,6},{8,7},{9,8},{10,9},{11,1... | collective-permute-start | bytes 138248 | tf_op jit(solution)/shard_map/ppermute | solution.py:20
  22.8 9.1 %all-to-all-start.1 = ((s32[128,8,1]{1,2,0:T(1,128)}), s32[128,8,1]{1,2,0:T(1,128)S(1)}, u32[]{:S(2)}, u32[]{:S(2)}) async-start(s32[128,8,1]{1,2,0:T(1,128)} %bitcast.28), calls=%async_computation.1 | async-start | bytes 131072 | tf_op jit(solution)/shard_map/all_to_all | solution.py:112
  32.4 8.1 %scatter_custom_fusion.9 = s32[2560]{0:T(1024)S(1)} fusion(s32[2048]{0:T(1024)S(1)} %bitcast.256, s32[2048]{0:T(1024)S(1)} %iota.38, s32[]{:T(128)} %constant.177.clone.1), kind=kCustom, calls=%fused_computation.266 | custom fusion | bytes 10244 | tf_op jit(solution)/shard_map/scatter | solution.py:121
  40.5 8.1 %scatter_custom_fusion.8 = s32[2560]{0:T(1024)S(1)} fusion(s32[2048]{0:T(1024)S(1)} %bitcast.254, s32[2048]{0:T(1024)S(1)} %iota.37, s32[]{:T(128)} %constant.177.clone.1), kind=kCustom, calls=%fused_computation.268 | custom fusion | bytes 10244 | tf_op jit(solution)/shard_map/scatter | solution.py:121
  58.5 8.1 %scatter_custom_fusion.7 = s32[2560]{0:T(1024)S(1)} fusion(s32[2048]{0:T(1024)S(1)} %bitcast.252, s32[2048]{0:T(1024)S(1)} %iota.36, s32[]{:T(128)} %constant.177.clone.1), kind=kCustom, calls=%fused_computation.270 | custom fusion | bytes 10244 | tf_op jit(solution)/shard_map/scatter | solution.py:121
  72.2 8.1 %scatter_custom_fusion.6 = s32[2560]{0:T(1024)S(1)} fusion(s32[2048]{0:T(1024)S(1)} %bitcast.250, s32[2048]{0:T(1024)S(1)} %iota.35, s32[]{:T(128)} %constant.177.clone.1), kind=kCustom, calls=%fused_computation.272 | custom fusion | bytes 10244 | tf_op jit(solution)/shard_map/scatter | solution.py:121
  86.0 8.1 %scatter_custom_fusion.4 = s32[2560]{0:T(1024)S(1)} fusion(s32[2048]{0:T(1024)S(1)} %bitcast.248, s32[2048]{0:T(1024)S(1)} %iota.33, s32[]{:T(128)} %constant.177.clone.1), kind=kCustom, calls=%fused_computation.276 | custom fusion | bytes 10244 | tf_op jit(solution)/shard_map/scatter | solution.py:121
  99.7 8.2 %scatter_custom_fusion.5 = s32[2560]{0:T(1024)S(1)} fusion(s32[2048]{0:T(1024)S(1)} %bitcast.246, s32[2048]{0:T(1024)S(1)} %iota.34, s32[]{:T(128)} %constant.177.clone.1), kind=kCustom, calls=%fused_computation.274 | custom fusion | bytes 10244 | tf_op jit(solution)/shard_map/scatter | solution.py:121
  135.7 8.0 %scatter_custom_fusion = s32[2048]{0:T(1024)S(1)} fusion(s32[2048]{0:T(1024)S(1)} %bitcast.269, s32[2048]{0:T(1024)S(1)} %iota.30, s32[]{:T(128)} %constant.164.clone.1), kind=kCustom, calls=%fused_computation.298 | custom fusion | bytes 8196 | tf_op jit(solution)/shard_map/scatter | solution.py:93
  301.8 10.9 %all-to-all-done.3 = bf16[90,128,8]{0,2,1:T(8,128)(2,1)S(1)} async-done(((bf16[90,128,8]{0,2,1:T(8,128)(2,1)}), bf16[90,128,8]{0,2,1:T(8,128)(2,1)S(1)}, u32[]{:S(2)}, u32[]{:S(2)}) %all-to-all-start.3) | async-done | bytes 184352 | tf_op jit(solution)/shard_map/all_to_all | solution.py:159
  327.7 7.6 %gather_fusion.5 = f32[2048,90]{1,0:T(8,128)} fusion(f32[2560,90]{1,0:T(8,128)S(1)} %pad_maximum_fusion, s32[2048]{0:T(1024)S(1)} %copy-done.38), kind=kCustom, calls=%fused_computation.16 | custom fusion | bytes 1482752 | tf_op jit(solution)/shard_map/gather | solution.py:197
  335.3 7.6 %gather_fusion.4 = f32[2048,90]{1,0:T(8,128)} fusion(f32[2560,90]{1,0:T(8,128)S(1)} %pad_maximum_fusion, s32[2048]{0:T(1024)S(1)} %copy-done.39), kind=kCustom, calls=%fused_computation.15 | custom fusion | bytes 1482752 | tf_op jit(solution)/shard_map/gather | solution.py:197
  342.9 7.6 %gather_fusion.3 = f32[2048,90]{1,0:T(8,128)} fusion(f32[2560,90]{1,0:T(8,128)S(1)} %pad_maximum_fusion, s32[2048]{0:T(1024)S(1)} %copy-done.40), kind=kCustom, calls=%fused_computation.14 | custom fusion | bytes 1482752 | tf_op jit(solution)/shard_map/gather | solution.py:197
  350.6 7.6 %gather_fusion.2 = f32[2048,90]{1,0:T(8,128)} fusion(f32[2560,90]{1,0:T(8,128)S(1)} %pad_maximum_fusion, s32[2048]{0:T(1024)S(1)} %copy-done.41), kind=kCustom, calls=%fused_computation.13 | custom fusion | bytes 1482752 | tf_op jit(solution)/shard_map/gather | solution.py:197
  358.2 7.6 %gather_fusion = f32[2048,90]{1,0:T(8,128)} fusion(f32[2560,90]{1,0:T(8,128)S(1)} %pad_maximum_fusion, s32[2048]{0:T(1024)S(1)} %copy-done.42), kind=kCustom, calls=%fused_computation.11 | custom fusion | bytes 1482752 | tf_op jit(solution)/shard_map/gather | solution.py:194
  365.8 7.6 %gather_fusion.1 = f32[2048,90]{1,0:T(8,128)} fusion(f32[2560,90]{1,0:T(8,128)S(1)} %pad_maximum_fusion, s32[2048]{0:T(1024)S(1)} %copy-done.43), kind=kCustom, calls=%fused_computation.12 | custom fusion | bytes 1482752 | tf_op jit(solution)/shard_map/gather | solution.py:197
  390.6 9.1 %all-to-all-start.2 = ((bf16[90,128,8]{0,2,1:T(8,128)(2,1)}), bf16[90,128,8]{0,2,1:T(8,128)(2,1)S(1)}, u32[]{:S(2)}, u32[]{:S(2)}) async-start(bf16[90,128,8]{0,2,1:T(8,128)(2,1)} %select_bitcast_fusion.3), calls=%async_computation.2 | async-start | bytes 524288 | tf_op jit(solution)/shard_map/all_to_all | solution.py:174
  400.2 10.5 %all-to-all-done.2 = bf16[90,128,8]{0,2,1:T(8,128)(2,1)S(1)} async-done(((bf16[90,128,8]{0,2,1:T(8,128)(2,1)}), bf16[90,128,8]{0,2,1:T(8,128)(2,1)S(1)}, u32[]{:S(2)}, u32[]{:S(2)}) %all-to-all-start.2) | async-done | bytes 184352 | tf_op jit(solution)/shard_map/all_to_all | solution.py:174
  434.1 7.6 %gather_fusion.16 = f32[2048,90]{1,0:T(8,128)} fusion(f32[2560,90]{1,0:T(8,128)S(1)} %pad_maximum_fusion.1, s32[2048]{0:T(1024)S(1)} %copy-done.38), kind=kCustom, calls=%fused_computation.27 | custom fusion | bytes 1482752 | tf_op jit(solution)/shard_map/gather | solution.py:197
  441.7 7.6 %gather_fusion.15 = f32[2048,90]{1,0:T(8,128)} fusion(f32[2560,90]{1,0:T(8,128)S(1)} %pad_maximum_fusion.1, s32[2048]{0:T(1024)S(1)} %copy-done.39), kind=kCustom, calls=%fused_computation.26 | custom fusion | bytes 1482752 | tf_op jit(solution)/shard_map/gather | solution.py:197
  449.3 7.6 %gather_fusion.14 = f32[2048,90]{1,0:T(8,128)} fusion(f32[2560,90]{1,0:T(8,128)S(1)} %pad_maximum_fusion.1, s32[2048]{0:T(1024)S(1)} %copy-done.40), kind=kCustom, calls=%fused_computation.25 | custom fusion | bytes 1482752 | tf_op jit(solution)/shard_map/gather | solution.py:197
  457.0 7.6 %gather_fusion.13 = f32[2048,90]{1,0:T(8,128)} fusion(f32[2560,90]{1,0:T(8,128)S(1)} %pad_maximum_fusion.1, s32[2048]{0:T(1024)S(1)} %copy-done.41), kind=kCustom, calls=%fused_computation.24 | custom fusion | bytes 1482752 | tf_op jit(solution)/shard_map/gather | solution.py:197
  464.6 7.6 %gather_fusion.11 = f32[2048,90]{1,0:T(8,128)} fusion(f32[2560,90]{1,0:T(8,128)S(1)} %pad_maximum_fusion.1, s32[2048]{0:T(1024)S(1)} %copy-done.42), kind=kCustom, calls=%fused_computation.22 | custom fusion | bytes 1482752 | tf_op jit(solution)/shard_map/gather | solution.py:194
  472.2 7.6 %gather_fusion.12 = f32[2048,90]{1,0:T(8,128)} fusion(f32[2560,90]{1,0:T(8,128)S(1)} %pad_maximum_fusion.1, s32[2048]{0:T(1024)S(1)} %copy-done.43), kind=kCustom, calls=%fused_computation.23 | custom fusion | bytes 1482752 | tf_op jit(solution)/shard_map/gather | solution.py:197
  491.8 9.1 %all-to-all-start.4 = ((bf16[540,128,8]{0,2,1:T(8,128)(2,1)}), bf16[540,128,8]{0,2,1:T(8,128)(2,1)S(1)}, u32[]{:S(2)}, u32[]{:S(2)}) async-start(bf16[540,128,8]{0,2,1:T(8,128)(2,1)} %select_bitcast_fusion), calls=%async_computation.4 | async-start | bytes 2621440 | tf_op jit(solution)/shard_map/all_to_all | solution.py:175
  502.3 7.6 %gather_fusion.22 = f32[2048,90]{1,0:T(8,128)} fusion(f32[2560,90]{1,0:T(8,128)S(1)} %pad_maximum_fusion.2, s32[2048]{0:T(1024)S(1)} %copy-done.38), kind=kCustom, calls=%fused_computation.33 | custom fusion | bytes 1482752 | tf_op jit(solution)/shard_map/gather | solution.py:197
  509.9 7.6 %gather_fusion.21 = f32[2048,90]{1,0:T(8,128)} fusion(f32[2560,90]{1,0:T(8,128)S(1)} %pad_maximum_fusion.2, s32[2048]{0:T(1024)S(1)} %copy-done.39), kind=kCustom, calls=%fused_computation.32 | custom fusion | bytes 1482752 | tf_op jit(solution)/shard_map/gather | solution.py:197
  517.5 7.6 %gather_fusion.20 = f32[2048,90]{1,0:T(8,128)} fusion(f32[2560,90]{1,0:T(8,128)S(1)} %pad_maximum_fusion.2, s32[2048]{0:T(1024)S(1)} %copy-done.40), kind=kCustom, calls=%fused_computation.31 | custom fusion | bytes 1482752 | tf_op jit(solution)/shard_map/gather | solution.py:197
  525.2 7.6 %gather_fusion.19 = f32[2048,90]{1,0:T(8,128)} fusion(f32[2560,90]{1,0:T(8,128)S(1)} %pad_maximum_fusion.2, s32[2048]{0:T(1024)S(1)} %copy-done.41), kind=kCustom, calls=%fused_computation.30 | custom fusion | bytes 1482752 | tf_op jit(solution)/shard_map/gather | solution.py:197
  532.8 7.6 %gather_fusion.17 = f32[2048,90]{1,0:T(8,128)} fusion(f32[2560,90]{1,0:T(8,128)S(1)} %pad_maximum_fusion.2, s32[2048]{0:T(1024)S(1)} %copy-done.42), kind=kCustom, calls=%fused_computation.28 | custom fusion | bytes 1482752 | tf_op jit(solution)/shard_map/gather | solution.py:194
  540.4 7.6 %gather_fusion.18 = f32[2048,90]{1,0:T(8,128)} fusion(f32[2560,90]{1,0:T(8,128)S(1)} %pad_maximum_fusion.2, s32[2048]{0:T(1024)S(1)} %copy-done.43), kind=kCustom, calls=%fused_computation.29 | custom fusion | bytes 1482752 | tf_op jit(solution)/shard_map/gather | solution.py:197
  554.8 9.3 %gather_fusion.39 = bf16[2048,540]{1,0:T(8,128)(2,1)} fusion(bf16[512,540]{1,0:T(8,128)(2,1)S(1)} %broadcast_select_fusion, s32[2048]{0:T(1024)S(1)} %copy-done.44), kind=kCustom, calls=%fused_computation.50 | custom fusion | bytes 4431872 | tf_op jit(solution)/shard_map/jit(_take)/gather | solution.py:56
  (375 shorter events, 317.8 us)
Async XLA Ops:
  0.6 165.4 %copy-start = (bf16[540,512]{1,0:T(8,128)(2,1)S(1)}, bf16[540,512]{1,0:T(8,128)(2,1)}, u32[]{:S(2)}) copy-start(bf16[540,512]{1,0:T(8,128)(2,1)} %param.27) | copy-start | bytes 1658884
  5.1 13.8 %copy-start.55 = (s32[1,512]{1,0:T(1,128)S(1)}, s32[1,512]{1,0:T(1,128)}, u32[]{:S(2)}) copy-start(s32[1,512]{1,0:T(1,128)} %param.33) | copy-start | bytes 6148
  9.2 22.7 %copy-start.49 = (s32[6,2048]{1,0:T(8,128)S(1)}, s32[6,2048]{1,0:T(8,128)}, u32[]{:S(2)}) copy-start(s32[6,2048]{1,0:T(8,128)} %param.36) | copy-start | bytes 147460
  10.0 22.0 %copy-start.31 = (bf16[90,2048]{1,0:T(8,128)(2,1)S(1)}, bf16[90,2048]{1,0:T(8,128)(2,1)}, u32[]{:S(2)}) copy-start(bf16[90,2048]{1,0:T(8,128)(2,1)} %param.26) | copy-start | bytes 1105924
  10.7 306.7 %collective-permute-start.1 = (bf16[90,256]{0,1:T(8,128)(2,1)}, bf16[90,256]{0,1:T(8,128)(2,1)}, u32[]{:S(2)}, u32[]{:S(2)}) collective-permute-start(bf16[90,256]{0,1:T(8,128)(2,1)} %get-tuple-element.62), channel_id=1, source_target_pairs={{1,0},{2,1},{3,2},{4,3},{5,4},{6,5},{7,6},{8,7},{9,8},{10,9},{11,1... | collective-permute-start | bytes 138248 | tf_op jit(solution)/shard_map/ppermute | solution.py:20
  18.9 298.5 %collective-permute-start = (bf16[90,256]{0,1:T(8,128)(2,1)}, bf16[90,256]{0,1:T(8,128)(2,1)}, u32[]{:S(2)}, u32[]{:S(2)}) collective-permute-start(bf16[90,256]{0,1:T(8,128)(2,1)} %get-tuple-element.61), channel_id=1, source_target_pairs={{0,1},{1,2},{2,3},{3,4},{4,5},{5,6},{6,7},{7,8},{8,9},{9,10},{10,1... | collective-permute-start | bytes 138248 | tf_op jit(solution)/shard_map/ppermute | solution.py:19
  22.8 156.3 %all-to-all-start.1 = ((s32[128,8,1]{1,2,0:T(1,128)}), s32[128,8,1]{1,2,0:T(1,128)S(1)}, u32[]{:S(2)}, u32[]{:S(2)}) async-start(s32[128,8,1]{1,2,0:T(1,128)} %bitcast.28), calls=%async_computation.1 | async-start | bytes 131072 | tf_op jit(solution)/shard_map/all_to_all | solution.py:112
  32.3 16.3 %copy-start.10 = (bf16[90,2048]{0,1:T(8,128)(2,1)}, bf16[90,2048]{0,1:T(8,128)(2,1)S(1)}, u32[]{:S(2)}) copy-start(bf16[90,2048]{0,1:T(8,128)(2,1)S(1)} %copy.49) | copy-start | bytes 1105924
  113.6 20.9 %copy-start.75 = (f32[3,256]{1,0:T(4,128)S(1)}, f32[3,256]{1,0:T(4,128)}, u32[]{:S(2)}) copy-start(f32[3,256]{1,0:T(4,128)} %param.31) | copy-start | bytes 9220
  113.6 21.4 %copy-start.50 = (s32[1,2048]{1,0:T(1,128)S(1)}, s32[1,2048]{1,0:T(1,128)}, u32[]{:S(2)}) copy-start(s32[1,2048]{1,0:T(1,128)} %param.32) | copy-start | bytes 24580
  119.7 65.3 %collective-permute-start.7 = (bf16[90,256]{0,1:T(8,128)(2,1)}, bf16[90,256]{0,1:T(8,128)(2,1)}, u32[]{:S(2)}, u32[]{:S(2)}) collective-permute-start(bf16[90,256]{0,1:T(8,128)(2,1)} %get-tuple-element.40), channel_id=1, source_target_pairs={{1,0},{2,1},{3,2},{4,3},{5,4},{6,5},{7,6},{8,7},{9,8},{10,9},{11,1... | collective-permute-start | bytes 138248 | tf_op jit(solution)/shard_map/ppermute | solution.py:20
  126.7 58.3 %collective-permute-start.6 = (bf16[90,256]{0,1:T(8,128)(2,1)}, bf16[90,256]{0,1:T(8,128)(2,1)}, u32[]{:S(2)}, u32[]{:S(2)}) collective-permute-start(bf16[90,256]{0,1:T(8,128)(2,1)} %get-tuple-element.39), channel_id=1, source_target_pairs={{0,1},{1,2},{2,3},{3,4},{4,5},{5,6},{6,7},{7,8},{8,9},{9,10},{10,1... | collective-permute-start | bytes 138248 | tf_op jit(solution)/shard_map/ppermute | solution.py:19
  178.2 65.7 %copy-start.77 = (s32[512,1]{0,1:T(1,128)}, s32[512,1]{0,1:T(1,128)S(1)}, u32[]{:S(2)}) copy-start(s32[512,1]{0,1:T(1,128)S(1)} %compare_select_fusion.19) | copy-start | bytes 6148
  180.7 205.8 %copy-start.46 = (s32[1024]{0:T(1024)}, s32[1024]{0:T(1024)S(1)}, u32[]{:S(2)}) copy-start(s32[1024]{0:T(1024)S(1)} %fusion.105) | copy-start | bytes 12292
  180.7 209.0 %copy-start.63 = (pred[1024]{0:T(1024)(128)(4,1)}, pred[1024]{0:T(1024)(128)(4,1)S(1)}, u32[]{:S(2)}) copy-start(pred[1024]{0:T(1024)(128)(4,1)S(1)} %compare_and_fusion.1) | copy-start | bytes 3076
  227.5 9.1 %collective-permute-start.9 = (bf16[90,256]{0,1:T(8,128)(2,1)S(1)}, bf16[90,256]{0,1:T(8,128)(2,1)S(1)}, u32[]{:S(2)}, u32[]{:S(2)}) collective-permute-start(bf16[90,256]{0,1:T(8,128)(2,1)S(1)} %get-tuple-element.38), channel_id=1, source_target_pairs={{1,0},{2,1},{3,2},{4,3},{5,4},{6,5},{7,6},{8,7},{9,8},{10,9},{11,1... | collective-permute-start | bytes 138248 | tf_op jit(solution)/shard_map/ppermute | solution.py:20
  234.7 9.1 %collective-permute-start.8 = (bf16[90,256]{0,1:T(8,128)(2,1)S(1)}, bf16[90,256]{0,1:T(8,128)(2,1)S(1)}, u32[]{:S(2)}, u32[]{:S(2)}) collective-permute-start(bf16[90,256]{0,1:T(8,128)(2,1)S(1)} %get-tuple-element.37), channel_id=1, source_target_pairs={{0,1},{1,2},{2,3},{3,4},{4,5},{5,6},{6,7},{7,8},{8,9},{9,10},{10,1... | collective-permute-start | bytes 138248 | tf_op jit(solution)/shard_map/ppermute | solution.py:19
  296.7 16.0 %all-to-all-start.3 = ((bf16[90,128,8]{0,2,1:T(8,128)(2,1)}), bf16[90,128,8]{0,2,1:T(8,128)(2,1)S(1)}, u32[]{:S(2)}, u32[]{:S(2)}) async-start(bf16[90,128,8]{0,2,1:T(8,128)(2,1)} %select_bitcast_fusion.2), calls=%async_computation.3 | async-start | bytes 524288 | tf_op jit(solution)/shard_map/all_to_all | solution.py:159
  301.8 15.6 %copy-start.28 = (bf16[90,512]{0,1:T(8,128)(2,1)S(1)}, bf16[90,512]{0,1:T(8,128)(2,1)}, u32[]{:S(2)}) copy-start(bf16[90,512]{0,1:T(8,128)(2,1)} %copy-done.27) | copy-start | bytes 276484
  312.7 69.3 %all-to-all-start = ((bf16[540,128,8]{0,2,1:T(8,128)(2,1)}), bf16[540,128,8]{0,2,1:T(8,128)(2,1)S(1)}, u32[]{:S(2)}, u32[]{:S(2)}) async-start(bf16[540,128,8]{0,2,1:T(8,128)(2,1)} %select_bitcast_fusion.1), calls=%async_computation | async-start | bytes 2621440 | tf_op jit(solution)/shard_map/all_to_all | solution.py:158
  319.2 55.1 %collective-permute-start.11 = (bf16[90,256]{0,1:T(8,128)(2,1)S(1)}, bf16[90,256]{0,1:T(8,128)(2,1)S(1)}, u32[]{:S(2)}, u32[]{:S(2)}) collective-permute-start(bf16[90,256]{0,1:T(8,128)(2,1)S(1)} %get-tuple-element.36), channel_id=1, source_target_pairs={{1,0},{2,1},{3,2},{4,3},{5,4},{6,5},{7,6},{8,7},{9,8},{10,9},{11,1... | collective-permute-start | bytes 138248 | tf_op jit(solution)/shard_map/ppermute | solution.py:20
  326.3 48.0 %collective-permute-start.10 = (bf16[90,256]{0,1:T(8,128)(2,1)S(1)}, bf16[90,256]{0,1:T(8,128)(2,1)}, u32[]{:S(2)}, u32[]{:S(2)}) collective-permute-start(bf16[90,256]{0,1:T(8,128)(2,1)S(1)} %get-tuple-element.35), channel_id=1, source_target_pairs={{0,1},{1,2},{2,3},{3,4},{4,5},{5,6},{6,7},{7,8},{8,9},{9,10},{10,1... | collective-permute-start | bytes 138248 | tf_op jit(solution)/shard_map/ppermute | solution.py:19
  389.7 21.0 %copy-start.56 = (s32[1024]{0:T(1024)S(1)}, s32[1024]{0:T(1024)}, u32[]{:S(2)}) copy-start(s32[1024]{0:T(1024)} %pad_clamp_fusion.6) | copy-start | bytes 12292
  390.6 20.1 %all-to-all-start.2 = ((bf16[90,128,8]{0,2,1:T(8,128)(2,1)}), bf16[90,128,8]{0,2,1:T(8,128)(2,1)S(1)}, u32[]{:S(2)}, u32[]{:S(2)}) async-start(bf16[90,128,8]{0,2,1:T(8,128)(2,1)} %select_bitcast_fusion.3), calls=%async_computation.2 | async-start | bytes 524288 | tf_op jit(solution)/shard_map/all_to_all | solution.py:174
  399.7 12.3 %copy-start.70 = (pred[512]{0:T(512)(128)(4,1)S(1)}, pred[512]{0:T(512)(128)(4,1)}, u32[]{:S(2)}) copy-start(pred[512]{0:T(512)(128)(4,1)} %get-tuple-element.31) | copy-start | bytes 1540
  399.7 12.4 %copy-start.44 = (s32[2048]{0:T(1024)S(1)}, s32[2048]{0:T(1024)}, u32[]{:S(2)}) copy-start(s32[2048]{0:T(1024)} %broadcast_clamp_fusion) | copy-start | bytes 24580
  418.4 61.4 %copy-start.8 = (bf16[2048,90]{1,0:T(8,128)(2,1)}, bf16[2048,90]{1,0:T(8,128)(2,1)S(1)}, u32[]{:S(2)}) copy-start(bf16[2048,90]{1,0:T(8,128)(2,1)S(1)} %gather_fusion.10) | copy-start | bytes 1105924
  422.8 8.1 %collective-permute-start.3 = (bf16[90,256]{0,1:T(8,128)(2,1)S(1)}, bf16[90,256]{0,1:T(8,128)(2,1)}, u32[]{:S(2)}, u32[]{:S(2)}) collective-permute-start(bf16[90,256]{0,1:T(8,128)(2,1)S(1)} %get-tuple-element.60), channel_id=1, source_target_pairs={{1,0},{2,1},{3,2},{4,3},{5,4},{6,5},{7,6},{8,7},{9,8},{10,9},{11,1... | collective-permute-start | bytes 138248 | tf_op jit(solution)/shard_map/ppermute | solution.py:20
  423.8 9.4 %collective-permute-start.2 = (bf16[90,256]{0,1:T(8,128)(2,1)S(1)}, bf16[90,256]{0,1:T(8,128)(2,1)}, u32[]{:S(2)}, u32[]{:S(2)}) collective-permute-start(bf16[90,256]{0,1:T(8,128)(2,1)S(1)} %get-tuple-element.59), channel_id=1, source_target_pairs={{0,1},{1,2},{2,3},{3,4},{4,5},{5,6},{6,7},{7,8},{8,9},{9,10},{10,1... | collective-permute-start | bytes 138248 | tf_op jit(solution)/shard_map/ppermute | solution.py:19
  484.2 16.8 %collective-permute-start.5 = (bf16[90,256]{0,1:T(8,128)(2,1)S(1)}, bf16[90,256]{0,1:T(8,128)(2,1)S(1)}, u32[]{:S(2)}, u32[]{:S(2)}) collective-permute-start(bf16[90,256]{0,1:T(8,128)(2,1)S(1)} %get-tuple-element.58), channel_id=1, source_target_pairs={{1,0},{2,1},{3,2},{4,3},{5,4},{6,5},{7,6},{8,7},{9,8},{10,9},{11,1... | collective-permute-start | bytes 138248 | tf_op jit(solution)/shard_map/ppermute | solution.py:20
  489.2 11.8 %collective-permute-start.4 = (bf16[90,256]{0,1:T(8,128)(2,1)S(1)}, bf16[90,256]{0,1:T(8,128)(2,1)S(1)}, u32[]{:S(2)}, u32[]{:S(2)}) collective-permute-start(bf16[90,256]{0,1:T(8,128)(2,1)S(1)} %get-tuple-element.57), channel_id=1, source_target_pairs={{0,1},{1,2},{2,3},{3,4},{4,5},{5,6},{6,7},{7,8},{8,9},{9,10},{10,1... | collective-permute-start | bytes 138248 | tf_op jit(solution)/shard_map/ppermute | solution.py:19
  491.8 60.8 %all-to-all-start.4 = ((bf16[540,128,8]{0,2,1:T(8,128)(2,1)}), bf16[540,128,8]{0,2,1:T(8,128)(2,1)S(1)}, u32[]{:S(2)}, u32[]{:S(2)}) async-start(bf16[540,128,8]{0,2,1:T(8,128)(2,1)} %select_bitcast_fusion), calls=%async_computation.4 | async-start | bytes 2621440 | tf_op jit(solution)/shard_map/all_to_all | solution.py:175
  (65 other events, 222.8 us)
where the time goes:
time: 590 us; the launch traced here: 580 us
  local copies, waits for them, and re-layouts  395 us (67%)
  starting transfers between devices  72.7 us (12%)
  other arithmetic  71.6 us (12%)
  waiting for transfers between devices  32.6 us (6%)
    gather x15, local copies, waits for them, and re-layouts, local(): extended_rows[adjacent_source_slots[spreading_link_index]]  114 us
    gather x15, local copies, waits for them, and re-layouts, local(): spread_rows = spread_rows + scaled_rows[reverse_links[spread_link_index]]  83 us
    scatter x6, local copies, waits for them, and re-layouts, local(): reverse_links = [jnp.full((extended_count,), fine_cells, jnp.int32).at[ad...  48.5 us
    gather x14, local copies, waits for them, and re-layouts, pick_columns(): return jnp.take(values.T, index, axis=0, mode='fill', fill_value=0).T  43.5 us
    ppermute x6, starting transfers between devices, extended(): after = lax.ppermute(initial, axis, down)  35.6 us
    gather x3, local copies, waits for them, and re-layouts, local(): overall_reduction_sum = extended_rows[adjacent_source_slots[0]]  22.8 us
    unnamed x169, local copies, waits for them, and re-layouts  17.1 us
    gather x3, local copies, waits for them, and re-layouts, local(): spread_rows = scaled_rows[reverse_links[0]]  16.9 us
  transfers between devices with their start and end apart: 17, of which 5 were waited for; matrix products, arithmetic and copies ran while one was open for 62% of the time, Pallas kernels for 0%

commit v1 on v0

v1 whole, which is shorter than its diff:
```python
import jax
import jax.numpy as jnp
from jax import lax
from jax.experimental import pallas as pl
from jax.experimental.pallas import tpu as pltpu
from jax.sharding import PartitionSpec as P

LEV, FEAT, HID = 90, 540, 256
COLS, CELLS, HALO = 512, 2048, 256
EXT = CELLS + 2 * HALO
DEVS, CAP = 128, 8
SLOTS = DEVS * CAP
KEEP, SPREAD = 0.25, 0.125

f32, bf16, i32 = jnp.float32, jnp.bfloat16, jnp.int32
NN = (((1,), (0,)), ((), ()))
NT = (((1,), (1,)), ((), ()))
TN = (((0,), (0,)), ((), ()))
VMEM = pl.BlockSpec(memory_space=pltpu.VMEM)
SMEM = pl.BlockSpec(memory_space=pltpu.SMEM)


def dot(a, b, dims):
    return lax.dot_general(a, b, dims, preferred_element_type=f32)


def shape(dims, dtype):
    return jax.ShapeDtypeStruct(dims, dtype)


def kernel(body, outs, args, specs=None, scratch=(), limit=24, flops=0, name=None):
    bytes_accessed = sum(a.size * a.dtype.itemsize for a in args)
    bytes_accessed += sum(o.size * o.dtype.itemsize for o in outs)
    return pl.pallas_call(
        body,
        out_shape=outs,
        in_specs=specs or [VMEM] * len(args),
        out_specs=tuple(VMEM for _ in outs),
        scratch_shapes=list(scratch),
        compiler_params=pltpu.CompilerParams(vmem_limit_bytes=limit * 1024 * 1024),
        cost_estimate=pl.CostEstimate(
            flops=flops, bytes_accessed=bytes_accessed, transcendentals=0
        ),
        name=name,
    )(*args)


def row_iota(rows, columns):
    return lax.broadcasted_iota(i32, (rows, columns), 0)


def lane_iota(rows, columns):
    return lax.broadcasted_iota(i32, (rows, columns), 1)


def onehot(mask):
    return jnp.where(mask, 1.0, 0.0).astype(bf16)


def to_column(row):
    return jnp.broadcast_to(row, (128, row.shape[1])).T[:, :1]


def chunk(i, size):
    return pl.ds(pl.multiple_of(i * size, size), size)


def route_kernel(parent_ref, request_ref, slot_ref):
    parents = parent_ref[...]
    target = parents >> 9
    column = (parents & (COLS - 1)) + 1
    target_column = to_column(target.astype(f32))
    same = (target_column == target.astype(f32)) & (row_iota(COLS, COLS) < lane_iota(COLS, COLS))
    rank = jnp.sum(jnp.where(same, 1.0, 0.0), axis=0, keepdims=True).astype(i32)
    slot_ref[...] = target * CAP + rank
    owners = onehot(row_iota(DEVS, COLS) == target)
    ranked = row_iota(DEVS, COLS) == rank
    high = jnp.where(ranked, (column >> 4).astype(f32), 0.0).astype(bf16)
    low = jnp.where(ranked, (column & 15).astype(f32), 0.0).astype(bf16)
    request = dot(owners, high, NT) * 16.0 + dot(owners, low, NT)
    request_ref[...] = request.reshape(DEVS, 1, 128)


def build_kernel(
    slots_ref, forcing_ref, state_ref, lists_ref, traj_ref, w_in_ref, bias_ref,
    links_ref, border_ref, u_ref, part_ref, up_ref, down_ref,
):
    slots = slots_ref[...]
    high = slots >> 8
    low = slots & 255
    times = jnp.zeros((6, CELLS), f32)
    for k in range(6):
        times = times + jnp.where(slots == slots[k : k + 1, :], 1.0, 0.0)
    times = times.astype(bf16)
    forcing = forcing_ref[...]

    def block(jb):
        here = jnp.where(high == jb, low, -1).astype(f32).astype(bf16)
        rows = chunk(jb, 256)
        for c in range(8):
            sl = slice(c * 256, (c + 1) * 256)
            place = row_iota(256, 256).astype(f32).astype(bf16)
            count = jnp.zeros((256, 256), bf16)
            for k in range(6):
                count = jnp.where(here[k : k + 1, sl] == place, times[k : k + 1, sl], count)
            links_ref[rows, sl] = count
        return SPREAD * dot(forcing, links_ref[rows, :], NT)

    def own(jb, _):
        cells = chunk(jb, 256)
        part_ref[:, cells] = KEEP * forcing_ref[:, cells].astype(f32) + block(jb)
        return 0

    lax.fori_loop(0, 8, own, 0)
    down_ref[0] = block(8).astype(bf16)
    up_ref[0] = block(9).astype(bf16)

    for b in range(8):
        sl = slice(b * 256, (b + 1) * 256)
        for side in range(2):
            border_ref[sl, side * 256 : (side + 1) * 256] = onehot(
                row_iota(256, 256) + b * 256 == lists_ref[side : side + 1, :]
            )
    border = dot(state_ref[:LEV, :], border_ref[...], NN)
    down_ref[1] = border[:, :HALO].astype(bf16)
    up_ref[1] = border[:, HALO:].astype(bf16)

    z = dot(traj_ref[...], w_in_ref[...], TN) + bias_ref[0:1, :]
    decay = jnp.exp(-2.0 * jnp.minimum(jnp.abs(z), 30.0))
    u_ref[...] = jnp.where(z < 0.0, -decay, decay).astype(bf16)


def answer_kernel(request_ref, u_ref, rank_ref, count_ref, answer_ref, left_ref, right_ref):
    daylit = rank_ref[...] < count_ref[0]
    number = jnp.where(daylit, lane_iota(1, COLS) + 1, -1).astype(f32)
    request = request_ref[...].reshape(DEVS, 128)
    for k in range(CAP):
        chosen = onehot(request[:, k : k + 1] == number)
        rows = dot(chosen, u_ref[...], NN)
        left_ref[pl.ds(k, DEVS, stride=CAP), :] = rows[:, :128]
        right_ref[pl.ds(k, DEVS, stride=CAP), :] = rows[:, 128:]
    answer_ref[:, :128] = left_ref[...].astype(bf16)
    answer_ref[:, 128:] = right_ref[...].astype(bf16)


def adjoint_step(adjoint, links_ref, part_ref, up_ref, down_ref, scratch_ref):
    scratch_ref[...] = adjoint
    rounded = adjoint.astype(bf16)

    def own(jb, _):
        cells = chunk(jb, 256)
        part_ref[:, cells] = KEEP * scratch_ref[:, cells] + SPREAD * dot(
            rounded, links_ref[cells, :], NT
        )
        return 0

    lax.fori_loop(0, 8, own, 0)
    down_ref[0] = (SPREAD * dot(rounded, links_ref[CELLS : CELLS + HALO, :], NT)).astype(bf16)
    up_ref[0] = (SPREAD * dot(rounded, links_ref[CELLS + HALO :, :], NT)).astype(bf16)


def second_kernel(
    part_ref, below_ref, above_ref, links_ref, border_ref, state_ref, forcing_ref,
    next_ref, up_ref, down_ref, heat_back_ref, first_ref, scratch_ref,
):
    adjoint = (
        part_ref[...]
        + dot(below_ref[0], border_ref[:, :HALO], NT)
        + dot(above_ref[0], border_ref[:, HALO:], NT)
    )
    heat_back_ref[...] = forcing_ref[...].astype(f32) + adjoint
    adjoint_step(adjoint, links_ref, next_ref, up_ref, down_ref, scratch_ref)

    def ahead(c, _):
        cells = chunk(c, 256)
        total = dot(state_ref[:LEV, :], links_ref[:CELLS, cells], NN)
        total = total + dot(below_ref[1], links_ref[CELLS : CELLS + HALO, cells], NN)
        total = total + dot(above_ref[1], links_ref[CELLS + HALO :, cells], NN)
        first_ref[:, cells] = KEEP * state_ref[:LEV, cells].astype(f32) + SPREAD * total
        return 0

    lax.fori_loop(0, 8, ahead, 0)


def group_kernel(order_ref, state_ref, w_in_ref, groups_ref, drive_ref):
    group = order_ref[...] >> 2
    for c in range(8):
        sl = slice(c * 256, (c + 1) * 256)
        groups_ref[:, sl] = onehot(row_iota(COLS, 256) == group[:, sl])
    mean = (0.25 * dot(state_ref[...], groups_ref[...], NT)).astype(bf16)
    drive_ref[...] = dot(w_in_ref[...], mean, TN)


def third_kernel(
    part_ref, below_ref, above_ref, links_ref, border_ref, heat_back_ref, groups_ref,
    next_ref, up_ref, down_ref, back_ref, scratch_ref,
):
    adjoint = (
        part_ref[...]
        + dot(below_ref[0], border_ref[:, :HALO], NT)
        + dot(above_ref[0], border_ref[:, HALO:], NT)
    )
    total = heat_back_ref[...] + adjoint
    back_ref[...] = dot(total.astype(bf16), groups_ref[...], NT).astype(bf16)
    adjoint_step(adjoint, links_ref, next_ref, up_ref, down_ref, scratch_ref)


def network_kernel(
    answer_ref, slot_ref, drive_ref, first_ref, groups_ref, border_ref, w_hidden_ref, w_out_ref,
    bias_ref, heat_ref, temp_ref, up_ref, down_ref, slope_ref,
):
    chosen = onehot(row_iota(SLOTS, COLS) == slot_ref[...])
    u = dot(answer_ref[...], chosen, TN)
    size = jnp.abs(u)
    inverse = 1.0 / (1.0 + size)
    act = jnp.where(u < 0.0, size - 1.0, 1.0 - size) * inverse
    slope = 4.0 * size * inverse * inverse
    slope_ref[0] = slope
    tangent = (slope * drive_ref[...]).astype(bf16)
    for layer in range(2):
        weight = w_hidden_ref[layer]
        bias = to_column(bias_ref[layer + 1 : layer + 2, :])
        act = jnp.tanh(dot(weight, act.astype(bf16), TN) + bias)
        slope = 1.0 - act * act
        slope_ref[layer + 1] = slope
        tangent = (slope * dot(weight, tangent, TN)).astype(bf16)
    heating = dot(w_out_ref[...], tangent, TN).astype(bf16)
    heat = dot(heating, groups_ref[...], NN)
    heat_ref[...] = heat
    temp = first_ref[...] + heat
    temp_ref[...] = temp
    border = dot(temp.astype(bf16), border_ref[...], NN)
    down_ref[...] = border[:, :HALO].astype(bf16)
    up_ref[...] = border[:, HALO:].astype(bf16)


def inner_kernel(temp_ref, heat_ref, links_ref, part_ref):
    rounded = temp_ref[...].astype(bf16)

    def own(c, _):
        cells = chunk(c, 256)
        total = dot(rounded, links_ref[:CELLS, cells], NN)
        part_ref[:, cells] = KEEP * temp_ref[:, cells] + heat_ref[:, cells] + SPREAD * total
        return 0

    lax.fori_loop(0, 8, own, 0)


def outer(part_ref, below_ref, above_ref, links_ref, temp_ref):
    def halo(c, _):
        cells = chunk(c, 256)
        total = dot(below_ref[...], links_ref[CELLS : CELLS + HALO, cells], NN)
        total = total + dot(above_ref[...], links_ref[CELLS + HALO :, cells], NN)
        temp_ref[:, cells] = part_ref[:, cells] + SPREAD * total
        return 0

    lax.fori_loop(0, 8, halo, 0)


def outer_kernel(
    part_ref, below_ref, above_ref, links_ref, border_ref, temp_ref, up_ref, down_ref
):
    outer(part_ref, below_ref, above_ref, links_ref, temp_ref)
    border = dot(temp_ref[...].astype(bf16), border_ref[...], NN)
    down_ref[...] = border[:, :HALO].astype(bf16)
    up_ref[...] = border[:, HALO:].astype(bf16)


def last_kernel(part_ref, below_ref, above_ref, links_ref, temp_ref):
    outer(part_ref, below_ref, above_ref, links_ref, temp_ref)


def sensitivity_kernel(
    back_ref, slope_ref, w_in_ref, w_hidden_ref, w_out_ref, groups_ref,
    part_ref, below_ref, above_ref, border_ref, out_ref,
):
    back = (slope_ref[2] * dot(w_out_ref[...], back_ref[...], NN)).astype(bf16)
    back = (slope_ref[1] * dot(w_hidden_ref[1], back, NN)).astype(bf16)
    back = (slope_ref[0] * dot(w_hidden_ref[0], back, NN)).astype(bf16)
    sens = (0.25 * dot(w_in_ref[...], back, NN)).astype(bf16)

    def spread(c, _):
        cells = chunk(c, 256)
        fine = dot(sens, groups_ref[:, cells], NN)
        adjoint = (
            part_ref[:, cells]
            + dot(below_ref[0], border_ref[cells, :HALO], NT)
            + dot(above_ref[0], border_ref[cells, HALO:], NT)
        )
        out_ref[:, cells] = fine.astype(bf16)
        out_ref[:LEV, cells] = (fine[:LEV] + adjoint).astype(bf16)
        return 0

    lax.fori_loop(0, 8, spread, 0)


def local(
    state_deviation, forcing, trajectory, w_in, w_hidden, w_out, biases, fine_order, group_parent,
    daylit_counts, sun_rank, adjacent_source_slots, outgoing_local_lists,
):
    up_pairs = [(i, (i + 1) % DEVS) for i in range(DEVS)]
    down_pairs = [(j, i) for i, j in up_pairs]

    def swap(up, down):
        below = lax.ppermute(up, "cells", up_pairs)
        above = lax.ppermute(down, "cells", down_pairs)
        return below, above

    count = lax.dynamic_slice(daylit_counts, (lax.axis_index("cells"),), (1,))
    lists = outgoing_local_lists[0]

    request, slot = kernel(
        route_kernel,
        (shape((DEVS, 1, 128), f32), shape((1, COLS), i32)),
        (group_parent,),
        flops=10**7,
        name="route",
    )
    asked = lax.all_to_all(request, "cells", 0, 0, tiled=True)

    message = shape((2, LEV, HALO), bf16)
    single = shape((1, LEV, HALO), bf16)
    plain = shape((LEV, HALO), bf16)
    field = shape((LEV, CELLS), f32)
    links, border, u, part, up, down = kernel(
        build_kernel,
        (
            shape((EXT, CELLS), bf16),
            shape((CELLS, 2 * HALO), bf16),
            shape((COLS, HID), bf16),
            field,
            message,
            message,
        ),
        (adjacent_source_slots, forcing, state_deviation, lists, trajectory, w_in, biases),
        flops=3 * 10**9,
        name="build",
    )
    below, above = swap(up, down)
    (answer,) = kernel(
        answer_kernel,
        (shape((SLOTS, HID), bf16),),
        (asked, u, sun_rank, count),
        specs=[VMEM, VMEM, VMEM, SMEM],
        scratch=[pltpu.VMEM((SLOTS, 128), f32)] * 2,
        flops=10**9,
        name="answer",
    )
    got = lax.all_to_all(answer.reshape(DEVS, CAP, HID), "cells", 0, 0, tiled=True)
    got = got.reshape(SLOTS, HID)

    groups, drive = kernel(
        group_kernel,
        (shape((COLS, CELLS), bf16), shape((HID, COLS), f32)),
        (fine_order, state_deviation, w_in),
        flops=2 * 10**9,
        name="group",
    )
    part, up, down, heat_back, first = kernel(
        second_kernel,
        (field, single, single, field, field),
        (part, below, above, links, border, state_deviation, forcing),
        scratch=[pltpu.VMEM((LEV, CELLS), f32)],
        flops=3 * 10**9,
        name="second",
    )
    below, above = swap(up, down)
    part, up, down, back = kernel(
        third_kernel,
        (field, single, single, shape((LEV, COLS), bf16)),
        (part, below, above, links, border, heat_back, groups),
        scratch=[pltpu.VMEM((LEV, CELLS), f32)],
        flops=3 * 10**9,
        name="third",
    )
    below, above = swap(up, down)

    heat, temp, up, down, slope = kernel(
        network_kernel,
        (field, field, plain, plain, shape((3, HID, COLS), f32)),
        (got, slot, drive, first, groups, border, w_hidden, w_out, biases),
        flops=3 * 10**9,
        name="network",
    )
    t_below, t_above = swap(up, down)
    (inner,) = kernel(inner_kernel, (field,), (temp, heat, links), flops=10**9, name="inner")
    (sens,) = kernel(
        sensitivity_kernel,
        (shape((FEAT, CELLS), bf16),),
        (back, slope, w_in, w_hidden, w_out, groups, part, below, above, border),
        flops=2 * 10**9,
        name="sensitivity",
    )
    temp, up, down = kernel(
        outer_kernel,
        (field, plain, plain),
        (inner, t_below, t_above, links, border),
        flops=10**9,
        name="outer",
    )
    t_below, t_above = swap(up, down)
    (inner,) = kernel(inner_kernel, (field,), (temp, heat, links), flops=10**9, name="inner")
    (temp,) = kernel(last_kernel, (field,), (inner, t_below, t_above, links), flops=10**9, name="last")
    return temp, sens


def solution(mesh):
    return jax.shard_map(
        local,
        mesh=mesh,
        in_specs=(
            P(None, "cells"),
            P(None, "cells"),
            P(None, "cells"),
            P(),
            P(),
            P(),
            P(),
            P("cells", None),
            P("cells", None),
            P(),
            P("cells", None),
            P(None, "cells"),
            P("cells", None, None),
        ),
        out_specs=(P(None, "cells"), P(None, "cells")),
        check_vma=False,
    )
```

time: 590 us -> 140 us (0.24); the launches traced: 580 us -> 139 us
  local copies, waits for them, and re-layouts: 395 us -> 39.5 us
  other arithmetic: 71.6 us -> 0.01 us
  Pallas kernels: 0 us -> 46.9 us
  waiting for transfers between devices: 32.6 us -> 0.03 us
  starting transfers between devices: 72.7 us -> 51.8 us
    gather x58 -> x0, local copies, waits for them, and re-layouts: 296 us -> none  [the longest x15 114 us: local(): extended_rows[adjacent_source_slots[spreading_link_index]]]
    scatter x10 -> x0, local copies, waits for them, and re-layouts: 65.7 us -> none  [the longest x6 48.5 us: local(): reverse_links = [jnp.full((extended_count,), fine_cells, jnp.int32).at[ad...]
    pallas_call x0 -> x12, Pallas kernels: none -> 46.9 us  [kernel(): pl.pallas_call(body, out_shape=outs, in_specs=specs or [VMEM] * len(args)...]
    unnamed x169 -> x83, local copies, waits for them, and re-layouts: 17.1 us -> 38.9 us
    all_to_all x5 -> x2, waiting for transfers between devices: 21.4 us -> 0.01 us  [the longest x1 0.01 us: local(): asked = lax.all_to_all(request, 'cells', 0, 0, tiled=True)]
    all_to_all x5 -> x2, starting transfers between devices: 37 us -> 15.8 us  [the longest x1 11.1 us: local(): asked = lax.all_to_all(request, 'cells', 0, 0, tiled=True)]
    scatter-add x3 -> x0, other arithmetic: 13 us -> none  [local(): adjoint = result.T.at[borrowed_slot_number].add(incoming_sums.T).T]
    another operation x6 -> x0, other arithmetic: 13 us -> none
  transfers between devices with their start and end apart: 17 -> 12, of which waited for: 5 -> 0; matrix products, arithmetic and copies ran while one was open for 62% -> 1% of each run, Pallas kernels for 0% -> 30%
where the time goes in v1:
time: 140 us; the launch traced here: 139 us
  starting transfers between devices  51.8 us (37%)
  Pallas kernels  46.9 us (34%)
  local copies, waits for them, and re-layouts  39.5 us (28%)
    pallas_call x12, Pallas kernels, kernel(): pl.pallas_call(body, out_shape=outs, in_specs=specs or [VMEM] * len(args)...  46.9 us
    unnamed x83, local copies, waits for them, and re-layouts  38.9 us
    ppermute x5, starting transfers between devices, swap(): above = lax.ppermute(down, 'cells', down_pairs)  35.8 us
    all_to_all x1, starting transfers between devices, local(): asked = lax.all_to_all(request, 'cells', 0, 0, tiled=True)  11.1 us
    all_to_all x1, starting transfers between devices, local(): lax.all_to_all(answer.reshape(DEVS, CAP, HID), 'cells', 0, 0, tiled=True)  4.61 us
  transfers between devices with their start and end apart: 12, of which 0 were waited for; matrix products, arithmetic and copies ran while one was open for 1% of the time, Pallas kernels for 30%

profile of v1, /device:TPU:0, one launch (start us, length us, event | category | flops | bytes accessed | tf_op | source)
XLA Modules:
  0.0 139.1 jit_solution(17791560181775080934)
XLA Ops:
  1.3 1.2 route.1
  2.5 11.1 %all-to-all-start = ((f32[128,1,128]{2,1,0:T(1,128)}), f32[128,1,128]{2,1,0:T(1,128)S(1)}, u32[]{:S(2)}, u32[]{:S(2)}) async-start(f32[128,1,128]{2,1,0:T(1,128)} %get-tuple-element.29), calls=%async_computation | async-start | bytes 131072 | tf_op jit(solution)/shard_map/all_to_all | solution.py:319
  13.7 1.6 %copy-done.7 = bf16[540,2048]{1,0:T(8,128)(2,1)S(1)} copy-done((bf16[540,2048]{1,0:T(8,128)(2,1)S(1)}, bf16[540,2048]{1,0:T(8,128)(2,1)}, u32[]{:S(2)}) %copy-start.7) | copy-done | bytes 2211864
  17.2 1.1 copy-done.27
  20.5 8.0 %build.1 = (bf16[2560,2048]{1,0:T(8,128)(2,1)S(1)}, bf16[2048,512]{1,0:T(8,128)(2,1)S(1)}, bf16[512,256]{1,0:T(8,128)(2,1)S(1)}, f32[90,2048]{1,0:T(8,128)S(1)},...) custom-call(s32[6,2048]{1,0:T(8,128)S(1)} %copy-done.28, bf16[90,2048]{1,0:T(8,128)(2,1)S(1)} %copy-done.17, ...), custom_call_target="tpu_custom_call" | custom-call | flops 3000000000 | bytes 17230848 | tf_op jit(solution)/shard_map/build/pallas_call | solution.py:34
  28.5 4.0 %copy-done = bf16[2560,2048]{1,0:T(8,128)(2,1)} copy-done((bf16[2560,2048]{1,0:T(8,128)(2,1)}, bf16[2560,2048]{1,0:T(8,128)(2,1)S(1)}, u32[]{:S(2)}) %copy-start) | copy-done | bytes 10485784
  32.5 7.2 %collective-permute-start.1 = (bf16[2,90,256]{2,1,0:T(8,128)(2,1)}, bf16[2,90,256]{2,1,0:T(8,128)(2,1)}, u32[]{:S(2)}, u32[]{:S(2)}) collective-permute-start(bf16[2,90,256]{2,1,0:T(8,128)(2,1)} %get-tuple-element.35), channel_id=1, source_target_pairs={{1,0},{2,1},{3,2},{4,3},{5,4},{6,5},{7,6},{8,7},{9,8},{10,9},{11,1... | collective-permute-start | bytes 276488 | tf_op jit(solution)/shard_map/ppermute | solution.py:306
  40.4 2.0 %answer.1 = bf16[1024,256]{1,0:T(8,128)(2,1)S(1)} custom-call(f32[128,1,128]{2,1,0:T(1,128)S(1)} %all-to-all-done.request_ref, bf16[512,256]{1,0:T(8,128)(2,1)S(1)} %get-tuple-element.30.u_ref, s32[1,512]{1,0:T(1,128)S(1)} %copy-done.34, s32[1]{0:T(128)} %dynamic_slice.3.count_ref), custom_call_target="tpu_custom_call" | custom-call | flops 1000000000 | bytes 854020 | tf_op jit(solution)/shard_map/answer/pallas_call | solution.py:34
  43.2 4.6 %all-to-all-start.1 = ((bf16[128,8,256]{2,1,0:T(8,128)(2,1)}), bf16[128,8,256]{2,1,0:T(8,128)(2,1)S(1)}, u32[]{:S(2)}, u32[]{:S(2)}) async-start(bf16[128,8,256]{2,1,0:T(8,128)(2,1)} %bitcast.6), calls=%async_computation.1 | async-start | bytes 1048576 | tf_op jit(solution)/shard_map/all_to_all | solution.py:349
  47.9 4.0 %copy-done.1 = bf16[2560,2048]{1,0:T(8,128)(2,1)S(1)} copy-done((bf16[2560,2048]{1,0:T(8,128)(2,1)S(1)}, bf16[2560,2048]{1,0:T(8,128)(2,1)}, u32[]{:S(2)}) %copy-start.1) | copy-done | bytes 10485784
  51.9 1.6 %copy-done.8 = bf16[540,2048]{1,0:T(8,128)(2,1)S(1)} copy-done((bf16[540,2048]{1,0:T(8,128)(2,1)S(1)}, bf16[540,2048]{1,0:T(8,128)(2,1)}, u32[]{:S(2)}) %copy-start.8) | copy-done | bytes 2211864
  54.5 9.8 %second.1 = (f32[90,2048]{1,0:T(8,128)S(1)}, bf16[1,90,256]{2,1,0:T(8,128)(2,1)}, bf16[1,90,256]{2,1,0:T(8,128)(2,1)}, f32[90,2048]{1,0:T(8,128)S(1)}, f32[90,2048]{1,0:T(8,128)S(1)}) custom-call(f32[90,2048]{1,0:T(8,128)S(1)} %get-tuple-element.33.part_ref, bf16[2,90,256]{2,1,0:T(8,128)(2,1)S(1)} %collective-permute-done.below_ref, ...), custom_call_target="tpu_custom_call" | custom-call | flops 3000000000 | bytes 18388992 | tf_op jit(solution)/shard_map/second/pallas_call | solution.py:34
  67.0 7.2 %collective-permute-start.7 = (bf16[1,90,256]{2,1,0:T(8,128)(2,1)}, bf16[1,90,256]{2,1,0:T(8,128)(2,1)}, u32[]{:S(2)}, u32[]{:S(2)}) collective-permute-start(bf16[1,90,256]{2,1,0:T(8,128)(2,1)} %get-tuple-element.49), channel_id=1, source_target_pairs={{1,0},{2,1},{3,2},{4,3},{5,4},{6,5},{7,6},{8,7},{9,8},{10,9},{11,1... | collective-permute-start | bytes 138248 | tf_op jit(solution)/shard_map/ppermute | solution.py:306
  74.2 1.6 %group.1 = (bf16[512,2048]{1,0:T(8,128)(2,1)S(1)}, f32[256,512]{1,0:T(8,128)S(1)}) custom-call(s32[1,2048]{1,0:T(1,128)S(1)} %copy-done.29, bf16[540,2048]{1,0:T(8,128)(2,1)S(1)} %copy-done.9, bf16[540,256]{1,0:T(8,128)(2,1)S(1)} %copy-done.20), custom_call_target="tpu_custom_call" | custom-call | flops 2000000000 | bytes 5117952 | tf_op jit(solution)/shard_map/group/pallas_call | solution.py:34
  75.8 1.3 copy-done.3
  78.9 4.0 %copy-done.2 = bf16[2560,2048]{1,0:T(8,128)(2,1)S(1)} copy-done((bf16[2560,2048]{1,0:T(8,128)(2,1)S(1)}, bf16[2560,2048]{1,0:T(8,128)(2,1)}, u32[]{:S(2)}) %copy-start.2) | copy-done | bytes 10485784
  82.9 1.6 %copy-done.4 = bf16[512,2048]{1,0:T(8,128)(2,1)S(1)} copy-done((bf16[512,2048]{1,0:T(8,128)(2,1)S(1)}, bf16[512,2048]{1,0:T(8,128)(2,1)}, u32[]{:S(2)}) %copy-start.4) | copy-done | bytes 2097176
  84.5 1.1 copy-done.13
  85.6 7.3 %third.1 = (f32[90,2048]{1,0:T(8,128)S(1)}, bf16[1,90,256]{2,1,0:T(8,128)(2,1)}, bf16[1,90,256]{2,1,0:T(8,128)(2,1)}, bf16[90,512]{1,0:T(8,128)(2,1)S(1)}) custom-call(f32[90,2048]{1,0:T(8,128)S(1)} %copy-done.11, bf16[1,90,256]{2,1,0:T(8,128)(2,1)S(1)} %collective-permute-done.6.below_ref, bf16[1,90,256]{2,1,0:T(8,128)(2,1)} %collective-permute-done.7.above_ref, ...), custom_call_target="tpu_custom_call" | custom-call | flops 3000000000 | bytes 17168384 | tf_op jit(solution)/shard_map/third/pallas_call | solution.py:34
  94.5 7.2 %collective-permute-start.9 = (bf16[1,90,256]{2,1,0:T(8,128)(2,1)}, bf16[1,90,256]{2,1,0:T(8,128)(2,1)S(1)}, u32[]{:S(2)}, u32[]{:S(2)}) collective-permute-start(bf16[1,90,256]{2,1,0:T(8,128)(2,1)} %get-tuple-element.55), channel_id=1, source_target_pairs={{1,0},{2,1},{3,2},{4,3},{5,4},{6,5},{7,6},{8,7},{9,8},{10,9},{11,1... | collective-permute-start | bytes 138248 | tf_op jit(solution)/shard_map/ppermute | solution.py:306
  101.7 1.6 %copy-done.5 = bf16[512,2048]{1,0:T(8,128)(2,1)S(1)} copy-done((bf16[512,2048]{1,0:T(8,128)(2,1)S(1)}, bf16[512,2048]{1,0:T(8,128)(2,1)}, u32[]{:S(2)}) %copy-start.5) | copy-done | bytes 2097176
  104.2 1.1 copy-done.26
  105.3 1.0 copy-done.36
  106.4 2.0 %network.1 = (f32[90,2048]{1,0:T(8,128)S(1)}, f32[90,2048]{1,0:T(8,128)S(1)}, bf16[90,256]{1,0:T(8,128)(2,1)S(1)}, bf16[90,256]{1,0:T(8,128)(2,1)S(1)}, f32[3,256,512]{2,1,0:T(8,128)S(1)}) custom-call(bf16[1024,256]{1,0:T(8,128)(2,1)S(1)} %bitcast.5, s32[1,512]{1,0:T(1,128)S(1)} %get-tuple-element.31.slot_ref, f32[256,512]{1,0:T(8,128)S(1)} %copy-done.36, ...), custom_call_target="tpu_custom_call" | custom-call | flops 3000000000 | bytes 9433088 | tf_op jit(solution)/shard_map/network/pallas_call | solution.py:34
  108.5 7.2 %collective-permute-start.3 = (bf16[90,256]{1,0:T(8,128)(2,1)S(1)}, bf16[90,256]{1,0:T(8,128)(2,1)S(1)}, u32[]{:S(2)}, u32[]{:S(2)}) collective-permute-start(bf16[90,256]{1,0:T(8,128)(2,1)S(1)} %get-tuple-element.43), channel_id=1, source_target_pairs={{1,0},{2,1},{3,2},{4,3},{5,4},{6,5},{7,6},{8,7},{9,8},{10,9},{11,1... | collective-permute-start | bytes 138248 | tf_op jit(solution)/shard_map/ppermute | solution.py:306
  115.7 1.1 copy-done.15
  116.8 5.2 %sensitivity.1 = bf16[540,2048]{1,0:T(8,128)(2,1)} custom-call(bf16[90,512]{1,0:T(8,128)(2,1)S(1)} %copy-done.24, f32[3,256,512]{2,1,0:T(8,128)S(1)} %get-tuple-element.52.slope_ref, bf16[540,256]{1,0:T(8,128)(2,1)S(1)} %copy-done.21, bf16[2,256,256]{2,1,0:T(8,128)(2,1)S(1)} %copy-done.22, bf16[256,90]{1,0:T(8,128)(2,1)S(1)} %copy.15.w_out_ref, ...), custom_call_target="tpu_custom_call" | custom-call | flops 2000000000 | bytes 9485312 | tf_op jit(solution)/shard_map/sensitivity/pallas_call | solution.py:34
  122.1 2.7 %inner.2.part_ref = f32[90,2048]{1,0:T(8,128)S(1)} custom-call(f32[90,2048]{1,0:T(8,128)S(1)} %get-tuple-element.40.temp_ref, f32[90,2048]{1,0:T(8,128)S(1)} %get-tuple-element.41.heat_ref, bf16[2560,2048]{1,0:T(8,128)(2,1)S(1)} %bitcast.4), custom_call_target="tpu_custom_call" | custom-call | flops 1000000000 | bytes 12697600 | tf_op jit(solution)/shard_map/inner/pallas_call | solution.py:34
  124.7 2.0 %outer.1 = (f32[90,2048]{1,0:T(8,128)S(1)}, bf16[90,256]{1,0:T(8,128)(2,1)S(1)}, bf16[90,256]{1,0:T(8,128)(2,1)S(1)}) custom-call(f32[90,2048]{1,0:T(8,128)S(1)} %inner.2.part_ref, bf16[90,256]{1,0:T(8,128)(2,1)S(1)} %collective-permute-done.2.below_ref, bf16[90,256]{1,0:T(8,128)(2,1)S(1)} %collective-permute-done.3.above_ref, ...), custom_call_target="tpu_custom_call" | custom-call | flops 1000000000 | bytes 14241792 | tf_op jit(solution)/shard_map/outer/pallas_call | solution.py:34
  126.8 7.2 %collective-permute-start.5 = (bf16[90,256]{1,0:T(8,128)(2,1)S(1)}, bf16[90,256]{1,0:T(8,128)(2,1)S(1)}, u32[]{:S(2)}, u32[]{:S(2)}) collective-permute-start(bf16[90,256]{1,0:T(8,128)(2,1)S(1)} %get-tuple-element.46), channel_id=1, source_target_pairs={{1,0},{2,1},{3,2},{4,3},{5,4},{6,5},{7,6},{8,7},{9,8},{10,9},{11,1... | collective-permute-start | bytes 138248 | tf_op jit(solution)/shard_map/ppermute | solution.py:306
  134.0 2.7 %inner.3.part_ref = f32[90,2048]{1,0:T(8,128)S(1)} custom-call(f32[90,2048]{1,0:T(8,128)S(1)} %get-tuple-element.44.temp_ref, f32[90,2048]{1,0:T(8,128)S(1)} %get-tuple-element.41.heat_ref, bf16[2560,2048]{1,0:T(8,128)(2,1)S(1)} %bitcast.4), custom_call_target="tpu_custom_call" | custom-call | flops 1000000000 | bytes 12697600 | tf_op jit(solution)/shard_map/inner/pallas_call | solution.py:34
  136.7 2.4 %last.1 = f32[90,2048]{1,0:T(8,128)} custom-call(f32[90,2048]{1,0:T(8,128)S(1)} %inner.3.part_ref, bf16[90,256]{1,0:T(8,128)(2,1)S(1)} %collective-permute-done.4.below_ref, bf16[90,256]{1,0:T(8,128)(2,1)S(1)} %collective-permute-done.5.above_ref, bf16[2560,2048]{1,0:T(8,128)(2,1)S(1)} %bitcast.4), custom_call_target="tpu_custom_call" | custom-call | flops 1000000000 | bytes 12052480 | tf_op jit(solution)/shard_map/last/pallas_call | solution.py:34
  (89 shorter events, 14.4 us)
Async XLA Ops:
  2.5 37.9 %all-to-all-start = ((f32[128,1,128]{2,1,0:T(1,128)}), f32[128,1,128]{2,1,0:T(1,128)S(1)}, u32[]{:S(2)}, u32[]{:S(2)}) async-start(f32[128,1,128]{2,1,0:T(1,128)} %get-tuple-element.29), calls=%async_computation | async-start | bytes 131072 | tf_op jit(solution)/shard_map/all_to_all | solution.py:319
  13.6 1.6 %copy-start.7 = (bf16[540,2048]{1,0:T(8,128)(2,1)S(1)}, bf16[540,2048]{1,0:T(8,128)(2,1)}, u32[]{:S(2)}) copy-start(bf16[540,2048]{1,0:T(8,128)(2,1)} %state_ref.5) | copy-start | bytes 6635524
  20.5 19.2 %copy-start.37 = (s32[128]{0:T(128)S(1)}, s32[128]{0:T(128)}, u32[]{:S(2)}) copy-start(s32[128]{0:T(128)} %param.22) | copy-start | bytes 1540
  20.5 19.9 %copy-start.34 = (s32[1,512]{1,0:T(1,128)S(1)}, s32[1,512]{1,0:T(1,128)}, u32[]{:S(2)}) copy-start(s32[1,512]{1,0:T(1,128)} %rank_ref.1) | copy-start | bytes 6148
  28.5 4.1 %copy-start = (bf16[2560,2048]{1,0:T(8,128)(2,1)}, bf16[2560,2048]{1,0:T(8,128)(2,1)S(1)}, u32[]{:S(2)}) copy-start(bf16[2560,2048]{1,0:T(8,128)(2,1)S(1)} %get-tuple-element.36.links_ref) | copy-start | bytes 31457284
  32.5 15.3 %collective-permute-start = (bf16[2,90,256]{2,1,0:T(8,128)(2,1)}, bf16[2,90,256]{2,1,0:T(8,128)(2,1)S(1)}, u32[]{:S(2)}, u32[]{:S(2)}) collective-permute-start(bf16[2,90,256]{2,1,0:T(8,128)(2,1)} %get-tuple-element.34), channel_id=1, source_target_pairs={{0,1},{1,2},{2,3},{3,4},{4,5},{5,6},{6,7},{7,8},{8,9},{9,10},{10,1... | collective-permute-start | bytes 276488 | tf_op jit(solution)/shard_map/ppermute | solution.py:305
  32.5 15.3 %collective-permute-start.1 = (bf16[2,90,256]{2,1,0:T(8,128)(2,1)}, bf16[2,90,256]{2,1,0:T(8,128)(2,1)}, u32[]{:S(2)}, u32[]{:S(2)}) collective-permute-start(bf16[2,90,256]{2,1,0:T(8,128)(2,1)} %get-tuple-element.35), channel_id=1, source_target_pairs={{1,0},{2,1},{3,2},{4,3},{5,4},{6,5},{7,6},{8,7},{9,8},{10,9},{11,1... | collective-permute-start | bytes 276488 | tf_op jit(solution)/shard_map/ppermute | solution.py:306
  43.2 58.4 %all-to-all-start.1 = ((bf16[128,8,256]{2,1,0:T(8,128)(2,1)}), bf16[128,8,256]{2,1,0:T(8,128)(2,1)S(1)}, u32[]{:S(2)}, u32[]{:S(2)}) async-start(bf16[128,8,256]{2,1,0:T(8,128)(2,1)} %bitcast.6), calls=%async_computation.1 | async-start | bytes 1048576 | tf_op jit(solution)/shard_map/all_to_all | solution.py:349
  47.9 4.0 %copy-start.1 = (bf16[2560,2048]{1,0:T(8,128)(2,1)S(1)}, bf16[2560,2048]{1,0:T(8,128)(2,1)}, u32[]{:S(2)}) copy-start(bf16[2560,2048]{1,0:T(8,128)(2,1)} %copy-done) | copy-start | bytes 31457284
  51.9 1.6 %copy-start.8 = (bf16[540,2048]{1,0:T(8,128)(2,1)S(1)}, bf16[540,2048]{1,0:T(8,128)(2,1)}, u32[]{:S(2)}) copy-start(bf16[540,2048]{1,0:T(8,128)(2,1)} %state_ref.5) | copy-start | bytes 6635524
  54.5 19.7 %copy-start.9 = (bf16[540,2048]{1,0:T(8,128)(2,1)S(1)}, bf16[540,2048]{1,0:T(8,128)(2,1)}, u32[]{:S(2)}) copy-start(bf16[540,2048]{1,0:T(8,128)(2,1)} %state_ref.5) | copy-start | bytes 6635524
  54.5 19.7 %copy-start.20 = (bf16[540,256]{1,0:T(8,128)(2,1)S(1)}, bf16[540,256]{1,0:T(8,128)(2,1)}, u32[]{:S(2)}) copy-start(bf16[540,256]{1,0:T(8,128)(2,1)} %w_in_ref.5) | copy-start | bytes 829444
  54.5 19.7 %copy-start.29 = (s32[1,2048]{1,0:T(1,128)S(1)}, s32[1,2048]{1,0:T(1,128)}, u32[]{:S(2)}) copy-start(s32[1,2048]{1,0:T(1,128)} %order_ref.1) | copy-start | bytes 24580
  67.0 11.8 %collective-permute-start.6 = (bf16[1,90,256]{2,1,0:T(8,128)(2,1)}, bf16[1,90,256]{2,1,0:T(8,128)(2,1)S(1)}, u32[]{:S(2)}, u32[]{:S(2)}) collective-permute-start(bf16[1,90,256]{2,1,0:T(8,128)(2,1)} %get-tuple-element.48), channel_id=1, source_target_pairs={{0,1},{1,2},{2,3},{3,4},{4,5},{5,6},{6,7},{7,8},{8,9},{9,10},{10,1... | collective-permute-start | bytes 138248 | tf_op jit(solution)/shard_map/ppermute | solution.py:305
  67.0 11.9 %copy-start.11 = (f32[90,2048]{1,0:T(8,128)S(1)}, f32[90,2048]{1,0:T(8,128)}, u32[]{:S(2)}) copy-start(f32[90,2048]{1,0:T(8,128)} %copy-done.10) | copy-start | bytes 2211844
  67.0 11.8 %collective-permute-start.7 = (bf16[1,90,256]{2,1,0:T(8,128)(2,1)}, bf16[1,90,256]{2,1,0:T(8,128)(2,1)}, u32[]{:S(2)}, u32[]{:S(2)}) collective-permute-start(bf16[1,90,256]{2,1,0:T(8,128)(2,1)} %get-tuple-element.49), channel_id=1, source_target_pairs={{1,0},{2,1},{3,2},{4,3},{5,4},{6,5},{7,6},{8,7},{9,8},{10,9},{11,1... | collective-permute-start | bytes 138248 | tf_op jit(solution)/shard_map/ppermute | solution.py:306
  78.9 4.0 %copy-start.2 = (bf16[2560,2048]{1,0:T(8,128)(2,1)S(1)}, bf16[2560,2048]{1,0:T(8,128)(2,1)}, u32[]{:S(2)}) copy-start(bf16[2560,2048]{1,0:T(8,128)(2,1)} %copy-done) | copy-start | bytes 31457284
  82.9 1.6 %copy-start.4 = (bf16[512,2048]{1,0:T(8,128)(2,1)S(1)}, bf16[512,2048]{1,0:T(8,128)(2,1)}, u32[]{:S(2)}) copy-start(bf16[512,2048]{1,0:T(8,128)(2,1)} %copy-done.3) | copy-start | bytes 6291460
  85.6 16.0 %copy-start.31 = (f32[3,256]{1,0:T(4,128)S(1)}, f32[3,256]{1,0:T(4,128)}, u32[]{:S(2)}) copy-start(f32[3,256]{1,0:T(4,128)} %bias_ref.3) | copy-start | bytes 9220
  94.5 21.2 %collective-permute-start.8 = (bf16[1,90,256]{2,1,0:T(8,128)(2,1)}, bf16[1,90,256]{2,1,0:T(8,128)(2,1)S(1)}, u32[]{:S(2)}, u32[]{:S(2)}) collective-permute-start(bf16[1,90,256]{2,1,0:T(8,128)(2,1)} %get-tuple-element.54), channel_id=1, source_target_pairs={{0,1},{1,2},{2,3},{3,4},{4,5},{5,6},{6,7},{7,8},{8,9},{9,10},{10,1... | collective-permute-start | bytes 138248 | tf_op jit(solution)/shard_map/ppermute | solution.py:305
  94.5 21.2 %collective-permute-start.9 = (bf16[1,90,256]{2,1,0:T(8,128)(2,1)}, bf16[1,90,256]{2,1,0:T(8,128)(2,1)S(1)}, u32[]{:S(2)}, u32[]{:S(2)}) collective-permute-start(bf16[1,90,256]{2,1,0:T(8,128)(2,1)} %get-tuple-element.55), channel_id=1, source_target_pairs={{1,0},{2,1},{3,2},{4,3},{5,4},{6,5},{7,6},{8,7},{9,8},{10,9},{11,1... | collective-permute-start | bytes 138248 | tf_op jit(solution)/shard_map/ppermute | solution.py:306
  101.7 1.6 %copy-start.5 = (bf16[512,2048]{1,0:T(8,128)(2,1)S(1)}, bf16[512,2048]{1,0:T(8,128)(2,1)}, u32[]{:S(2)}) copy-start(bf16[512,2048]{1,0:T(8,128)(2,1)} %copy-done.3) | copy-start | bytes 6291460
  106.4 9.3 %copy-start.6 = (bf16[512,2048]{1,0:T(8,128)(2,1)S(1)}, bf16[512,2048]{1,0:T(8,128)(2,1)}, u32[]{:S(2)}) copy-start(bf16[512,2048]{1,0:T(8,128)(2,1)} %copy-done.3) | copy-start | bytes 6291460
  106.4 9.3 %copy-start.21 = (bf16[540,256]{1,0:T(8,128)(2,1)S(1)}, bf16[540,256]{1,0:T(8,128)(2,1)}, u32[]{:S(2)}) copy-start(bf16[540,256]{1,0:T(8,128)(2,1)} %w_in_ref.5) | copy-start | bytes 829444
  106.4 9.3 %copy-start.24 = (bf16[90,512]{1,0:T(8,128)(2,1)S(1)}, bf16[90,512]{1,0:T(8,128)(2,1)}, u32[]{:S(2)}) copy-start(bf16[90,512]{1,0:T(8,128)(2,1)} %copy-done.23) | copy-start | bytes 276484
  106.4 15.7 %slice-start = ((s8[10485760]{0:T(1024)(128)(4,1)}), s8[4194304]{0:T(1024)(128)(4,1)S(1)}, s32[]{:S(2)}) async-start(s8[10485760]{0:T(1024)(128)(4,1)} %bitcast.3), calls=%async_computation.2 | async-start | bytes 8388608
  106.4 15.7 %slice-start.1 = ((s8[10485760]{0:T(1024)(128)(4,1)}), s8[4194304]{0:T(1024)(128)(4,1)S(1)}, s32[]{:S(2)}) async-start(s8[10485760]{0:T(1024)(128)(4,1)} %bitcast.3), calls=%async_computation.3 | async-start | bytes 8388608
  108.4 16.3 %collective-permute-start.2 = (bf16[90,256]{1,0:T(8,128)(2,1)S(1)}, bf16[90,256]{1,0:T(8,128)(2,1)S(1)}, u32[]{:S(2)}, u32[]{:S(2)}) collective-permute-start(bf16[90,256]{1,0:T(8,128)(2,1)S(1)} %get-tuple-element.42), channel_id=1, source_target_pairs={{0,1},{1,2},{2,3},{3,4},{4,5},{5,6},{6,7},{7,8},{8,9},{9,10},{10,1... | collective-permute-start | bytes 138248 | tf_op jit(solution)/shard_map/ppermute | solution.py:305
  108.5 16.2 %collective-permute-start.3 = (bf16[90,256]{1,0:T(8,128)(2,1)S(1)}, bf16[90,256]{1,0:T(8,128)(2,1)S(1)}, u32[]{:S(2)}, u32[]{:S(2)}) collective-permute-start(bf16[90,256]{1,0:T(8,128)(2,1)S(1)} %get-tuple-element.43), channel_id=1, source_target_pairs={{1,0},{2,1},{3,2},{4,3},{5,4},{6,5},{7,6},{8,7},{9,8},{10,9},{11,1... | collective-permute-start | bytes 138248 | tf_op jit(solution)/shard_map/ppermute | solution.py:306
  116.8 5.2 %slice-start.2 = ((s8[10485760]{0:T(1024)(128)(4,1)}), s8[2097152]{0:T(1024)(128)(4,1)S(1)}, s32[]{:S(2)}) async-start(s8[10485760]{0:T(1024)(128)(4,1)} %bitcast.3), calls=%async_computation.4 | async-start | bytes 4194304
  126.7 9.9 %collective-permute-start.4 = (bf16[90,256]{1,0:T(8,128)(2,1)S(1)}, bf16[90,256]{1,0:T(8,128)(2,1)S(1)}, u32[]{:S(2)}, u32[]{:S(2)}) collective-permute-start(bf16[90,256]{1,0:T(8,128)(2,1)S(1)} %get-tuple-element.45), channel_id=1, source_target_pairs={{0,1},{1,2},{2,3},{3,4},{4,5},{5,6},{6,7},{7,8},{8,9},{9,10},{10,1... | collective-permute-start | bytes 138248 | tf_op jit(solution)/shard_map/ppermute | solution.py:305
  126.8 9.8 %collective-permute-start.5 = (bf16[90,256]{1,0:T(8,128)(2,1)S(1)}, bf16[90,256]{1,0:T(8,128)(2,1)S(1)}, u32[]{:S(2)}, u32[]{:S(2)}) collective-permute-start(bf16[90,256]{1,0:T(8,128)(2,1)S(1)} %get-tuple-element.46), channel_id=1, source_target_pairs={{1,0},{2,1},{3,2},{4,3},{5,4},{6,5},{7,6},{8,7},{9,8},{10,9},{11,1... | collective-permute-start | bytes 138248 | tf_op jit(solution)/shard_map/ppermute | solution.py:306
  (21 other events, 19.4 us)

commit v2 on v1

v2 whole, which is shorter than its diff:
```python
import jax
import jax.numpy as jnp
from jax import lax
from jax.experimental import pallas as pl
from jax.experimental.pallas import tpu as pltpu
from jax.sharding import PartitionSpec as P

LEV, FEAT, HID = 90, 540, 256
COLS, CELLS, HALO = 512, 2048, 256
EXT = CELLS + 2 * HALO
DEVS, CAP = 128, 8
SLOTS = DEVS * CAP
KEEP, SPREAD = 0.25, 0.125
TOP = 96
PIECE = 512
OWN = CELLS // PIECE

f32, bf16, i32 = jnp.float32, jnp.bfloat16, jnp.int32
NN = (((1,), (0,)), ((), ()))
NT = (((1,), (1,)), ((), ()))
TN = (((0,), (0,)), ((), ()))


def dot(a, b, dims):
    return lax.dot_general(a, b, dims, preferred_element_type=f32)


def shape(dims, dtype):
    return jax.ShapeDtypeStruct(dims, dtype)


class Fetch:
    def __init__(self, source, ref, sems, rows, start):
        self.ref, self.rows, self.copies, self.done = ref, rows, [], set()
        for i in range(ref.shape[0] // rows):
            part = pl.ds(i * rows, rows)
            origin = source.at[pl.ds(start + i * rows, rows)]
            self.copies.append(pltpu.make_async_copy(origin, ref.at[part], sems.at[i]))

    def order(self):
        return [len(self.copies) - 1, *range(len(self.copies) - 1)]

    def __call__(self):
        for i in range(len(self.copies)):
            self.piece(i)
        return self.ref

    def piece(self, i):
        if i not in self.done:
            self.copies[i].wait()
            self.done.add(i)
        return self.ref.at[pl.ds(i * self.rows, self.rows)]


class Store:
    def __init__(self, target, ref, sem):
        self.ref = ref
        self.copy = pltpu.make_async_copy(ref, target, sem)

    def put(self):
        self.copy.start()


def kernel(body, name, args, outs, limit=48, flops=10**9, scratch=(), aliases=None):
    arrays, in_specs, plan, scratches = [], [], [], []
    for arg in args:
        if isinstance(arg, tuple) and arg[0] == "raw":
            arrays.append(pltpu.with_memory_space_constraint(arg[1], pltpu.HBM))
            in_specs.append(pl.BlockSpec(memory_space=pl.ANY))
            plan.append(None)
        elif isinstance(arg, tuple):
            array, rows, piece, *start = arg
            arrays.append(pltpu.with_memory_space_constraint(array, pltpu.HBM))
            in_specs.append(pl.BlockSpec(memory_space=pl.ANY))
            plan.append((piece, start[0] if start else 0))
            scratches.append(pltpu.VMEM((rows,) + array.shape[1:], array.dtype))
            scratches.append(pltpu.SemaphoreType.DMA((rows // piece,)))
        else:
            arrays.append(arg)
            in_specs.append(pl.BlockSpec(memory_space=pltpu.VMEM))
            plan.append(None)
    out_shapes, out_specs = [], []
    for out, far in outs:
        if far == "raw":
            out_shapes.append(pltpu.HBM(out.shape, out.dtype))
            out_specs.append(pl.BlockSpec(memory_space=pl.ANY))
        elif far:
            out_shapes.append(pltpu.HBM(out.shape, out.dtype))
            out_specs.append(pl.BlockSpec(memory_space=pl.ANY))
            scratches.append(pltpu.VMEM(out.shape, out.dtype))
            scratches.append(pltpu.SemaphoreType.DMA)
        else:
            out_shapes.append(out)
            out_specs.append(pl.BlockSpec(memory_space=pltpu.VMEM))

    def wrapped(*refs):
        ins, results = refs[: len(args)], refs[len(args) : len(args) + len(outs)]
        rest = list(refs[len(args) + len(outs) :])
        operands, targets = [], []
        for ref, how in zip(ins, plan):
            if how is None:
                operands.append(ref)
            else:
                place, sems = rest.pop(0), rest.pop(0)
                operands.append(Fetch(ref, place, sems, *how))
        for last in (False, True):
            for o in operands:
                if isinstance(o, Fetch) and (len(o.copies) > 1) == last:
                    for i in o.order():
                        o.copies[i].start()
        for ref, (out, far) in zip(results, outs):
            if far is True:
                targets.append(Store(ref, rest.pop(0), rest.pop(0)))
            else:
                targets.append(ref)
        body(*operands, *targets, *rest)
        for target in targets:
            if isinstance(target, Store):
                target.copy.wait()

    size = sum(a.size * a.dtype.itemsize for a in arrays)
    size += sum(o.size * o.dtype.itemsize for o, _ in outs)
    return pl.pallas_call(
        wrapped,
        out_shape=tuple(out_shapes),
        in_specs=in_specs,
        out_specs=tuple(out_specs),
        scratch_shapes=scratches + list(scratch),
        input_output_aliases=aliases or {},
        compiler_params=pltpu.CompilerParams(vmem_limit_bytes=limit * 1024 * 1024),
        cost_estimate=pl.CostEstimate(flops=flops, bytes_accessed=size, transcendentals=0),
        name=name,
    )(*arrays)


def whole(array):
    return (array, array.shape[0], array.shape[0])


def row_iota(rows, columns):
    return lax.broadcasted_iota(i32, (rows, columns), 0)


def lane_iota(rows, columns):
    return lax.broadcasted_iota(i32, (rows, columns), 1)


def onehot(mask):
    return jnp.where(mask, 1.0, 0.0).astype(bf16)


def to_column(row):
    return jnp.broadcast_to(row, (128, row.shape[1])).T[:, :1]


def chunk(i, size):
    return pl.ds(pl.multiple_of(i * size, size), size)


def route_kernel(parent_ref, request_ref, slot_ref):
    parents = parent_ref[...]
    target = parents >> 9
    column = (parents & (COLS - 1)) + 1
    target_column = to_column(target.astype(f32))
    same = (target_column == target.astype(f32)) & (row_iota(COLS, COLS) < lane_iota(COLS, COLS))
    rank = jnp.sum(jnp.where(same, 1.0, 0.0), axis=0, keepdims=True).astype(i32)
    slot_ref.ref[...] = target * CAP + rank
    slot_ref.put()
    owners = onehot(row_iota(DEVS, COLS) == target)
    ranked = row_iota(DEVS, COLS) == rank
    high = jnp.where(ranked, (column >> 4).astype(f32), 0.0).astype(bf16)
    low = jnp.where(ranked, (column & 15).astype(f32), 0.0).astype(bf16)
    request = dot(owners, high, NT) * 16.0 + dot(owners, low, NT)
    request_ref.ref[...] = request.reshape(DEVS, 1, 128)
    request_ref.put()


def prepare_kernel(
    order_ref, state_ref, w_in_ref, traj_ref, bias_ref, rank_ref, count_ref,
    groups_ref, drive_ref, u_ref, number_ref,
):
    me = lax.axis_index("cells")
    group = order_ref()[...] >> 2
    for c in range(8):
        sl = slice(c * 256, (c + 1) * 256)
        groups_ref.ref[:, sl] = onehot(row_iota(COLS, 256) == group[:, sl])
    groups_ref.put()
    z = dot(traj_ref()[...], w_in_ref()[...], TN) + bias_ref()[0:1, :]
    decay = jnp.exp(-2.0 * jnp.minimum(jnp.abs(z), 30.0))
    u_ref.ref[...] = jnp.where(z < 0.0, -decay, decay).astype(bf16)
    u_ref.put()
    mine = jnp.where(lane_iota(1, DEVS) == me, count_ref()[...], 0).astype(f32)
    daylit = rank_ref()[...].astype(f32) < jnp.sum(mine, axis=1, keepdims=True)
    number_ref.ref[...] = jnp.where(daylit, lane_iota(1, COLS) + 1, -1).astype(f32)
    number_ref.put()
    mean = (0.25 * dot(state_ref()[...], groups_ref.ref[...], NT)).astype(bf16)
    drive_ref.ref[...] = dot(w_in_ref.ref[...], mean, TN)
    drive_ref.put()


def answer_kernel(request_ref, u_ref, number_ref, answer_ref, token_ref, left_ref, right_ref):
    request = request_ref()[...].reshape(DEVS, 128)
    number, u = number_ref()[...], u_ref()
    token_ref[...] = number[:, :128]
    for k in range(CAP):
        chosen = onehot(request[:, k : k + 1] == number)
        rows = dot(chosen, u[...], NN)
        left_ref[pl.ds(k, DEVS, stride=CAP), :] = rows[:, :128]
        right_ref[pl.ds(k, DEVS, stride=CAP), :] = rows[:, 128:]
    answer_ref.ref[:, :128] = left_ref[...].astype(bf16)
    answer_ref.ref[:, 128:] = right_ref[...].astype(bf16)
    answer_ref.put()


def build_kernel(
    slots_ref, lists_ref, forcing_ref, state_ref, token_ref,
    links_ref, border_ref, part_ref, first_ref, second_ref, links, sems,
):
    even = (lax.axis_index("cells") & 1) == 0
    slots = slots_ref()[...]
    high = slots >> 8
    high = jnp.where(even & (high >= 8), 17 - high, high)
    low = slots & 255
    times = jnp.zeros((6, CELLS), f32)
    for k in range(6):
        times = times + jnp.where(slots == slots[k : k + 1, :], 1.0, 0.0)
    times = times.astype(bf16)
    lists = lists_ref()
    near = jnp.where(even, lists[1:2, :], lists[0:1, :])
    far = jnp.where(even, lists[0:1, :], lists[1:2, :])
    forcing = forcing_ref()

    def fill(jb):
        here = jnp.where(high == jb, low, -1).astype(f32).astype(bf16)
        rows = slice(jb * 256, (jb + 1) * 256)
        for c in range(8):
            sl = slice(c * 256, (c + 1) * 256)
            place = row_iota(256, 256).astype(f32).astype(bf16)
            count = jnp.zeros((256, 256), bf16)
            for k in range(6):
                count = jnp.where(here[k : k + 1, sl] == place, times[k : k + 1, sl], count)
            links[rows, sl] = count
        out(jb).start()
        return SPREAD * dot(forcing[...], links[rows, :], NT)

    def out(jb):
        rows = pl.ds(jb * 256, 256)
        return pltpu.make_async_copy(links.at[rows], links_ref.at[rows], sems.at[jb])

    first_ref.ref[0] = fill(8).astype(bf16)
    second_ref.ref[0] = fill(9).astype(bf16)
    state = state_ref()
    for b in range(8):
        sl = slice(b * 256, (b + 1) * 256)
        cell = row_iota(256, 256) + b * 256
        border_ref.ref[sl, :HALO] = onehot(cell == near)
        border_ref.ref[sl, HALO:] = onehot(cell == far)
    border_ref.put()
    border = dot(state[:LEV, :], border_ref.ref[...], NN)
    first_ref.ref[1] = border[:, :HALO].astype(bf16)
    second_ref.ref[1] = border[:, HALO:].astype(bf16)
    first_ref.put()
    second_ref.put()
    for jb in range(8):
        sl = slice(jb * 256, (jb + 1) * 256)
        part_ref.ref[:, sl] = KEEP * forcing[:, sl].astype(f32) + fill(jb)
    part_ref.put()
    for jb in range(10):
        out(jb).wait()


def received(first, second, border):
    return dot(first, border[:, :HALO], NT) + dot(second, border[:, HALO:], NT)


def pull(adjoint, links, wait, part_ref, first_ref, second_ref):
    rounded = adjoint.astype(bf16)
    wait(OWN)
    share = SPREAD * dot(rounded, links[CELLS:, :], NT)
    first_ref[0] = share[:, :HALO].astype(bf16)
    second_ref[0] = share[:, HALO:].astype(bf16)
    for i in range(OWN):
        sl = slice(i * PIECE, (i + 1) * PIECE)
        wait(i)
        part_ref[:, sl] = KEEP * adjoint[:, sl] + SPREAD * dot(rounded, links[sl, :], NT)


def send_border(temp, border, first_ref, second_ref):
    values = dot(temp.astype(bf16), border[...], NN)
    first_ref[1] = values[:, :HALO].astype(bf16)
    second_ref[1] = values[:, HALO:].astype(bf16)


def middle_kernel(
    answer_ref, slot_ref, drive_ref, w_hidden_ref, w_out_ref, bias_ref, first_in, second_in, part_in,
    forcing_ref, state_ref, groups_far, border_far, links_far,
    groups, border, links, heat_ref, temp_ref, slope_ref, part_ref, heat_back_ref, first_ref, second_ref,
    sems,
):
    groups_copy = pltpu.make_async_copy(groups_far, groups, sems.at[5])
    border_copy = pltpu.make_async_copy(border_far, border, sems.at[6])

    def piece(i):
        rows = pl.ds(i * PIECE, PIECE)
        return pltpu.make_async_copy(links_far.at[rows], links.at[rows], sems.at[i])

    groups_copy.start()
    border_copy.start()
    for i in (OWN, *range(OWN)):
        piece(i).start()

    chosen = onehot(row_iota(SLOTS, COLS) == slot_ref()[...])
    u = dot(answer_ref()[...], chosen, TN)
    size = jnp.abs(u)
    inverse = 1.0 / (1.0 + size)
    act = jnp.where(u < 0.0, size - 1.0, 1.0 - size) * inverse
    slope = 4.0 * size * inverse * inverse
    slope_ref[0] = slope
    tangent = (slope * drive_ref()[...]).astype(bf16)
    weights, biases = w_hidden_ref(), bias_ref()
    for layer in range(2):
        weight = weights[layer]
        bias = to_column(biases[layer + 1 : layer + 2, :])
        act = jnp.tanh(dot(weight, act.astype(bf16), TN) + bias)
        slope = 1.0 - act * act
        slope_ref[layer + 1] = slope
        tangent = (slope * dot(weight, tangent, TN)).astype(bf16)
    heating = dot(w_out_ref()[...], tangent, NN).astype(bf16)
    groups_copy.wait()
    heat_ref[...] = dot(heating, groups[...], NN)

    border_copy.wait()
    adjoint = part_in()[...] + received(first_in()[0], second_in()[0], border)
    heat_back_ref[...] = forcing_ref()[...].astype(f32) + adjoint
    pull(adjoint, links, lambda i: piece(i).wait(), part_ref, first_ref, second_ref)
    state = state_ref()
    sides = jnp.concatenate([state[:LEV, :], first_in.ref[1], second_in.ref[1]], axis=1)
    for i in range(OWN):
        sl = slice(i * PIECE, (i + 1) * PIECE)
        temp_ref[:, sl] = (
            KEEP * state[:LEV, sl].astype(f32)
            + heat_ref[:, sl]
            + SPREAD * dot(sides, links[:, sl], NN)
        )
    send_border(temp_ref[...], border, first_ref, second_ref)


def inner(temp_ref, heat_ref, links, part_ref):
    rounded = temp_ref[...].astype(bf16)
    for i in range(OWN):
        sl = slice(i * PIECE, (i + 1) * PIECE)
        part_ref[:, sl] = (
            KEEP * temp_ref[:, sl]
            + heat_ref[:, sl]
            + SPREAD * dot(rounded, links[:CELLS, sl], NN)
        )


def outer(part_ref, first, second, links):
    sides = jnp.concatenate([first, second], axis=1)
    return part_ref[...] + SPREAD * dot(sides, links[CELLS:, :], NN)


def third_kernel(
    first_in, second_in, border, part_in, heat_back_ref, links, ahead_ref,
    part_ref, back_ref, temp_ref, first_ref, second_ref,
):
    adjoint = part_in[...] + received(first_in[0], second_in[0], border)
    back_ref[...] = (heat_back_ref[...] + adjoint).astype(bf16)
    pull(adjoint, links, lambda i: None, part_ref, first_ref, second_ref)
    temp = outer(ahead_ref, first_in[1], second_in[1], links)
    temp_ref[...] = temp
    send_border(temp, border, first_ref, second_ref)


def window_kernel(
    temp_ref, heat_ref, links, slope_ref, back_ref, groups, w_out_ref, w_hidden_ref, w_in_ref,
    sens_far, top_ref, part_ref, low_ref, sem,
):
    inputs = dot(back_ref[...], groups[...], NT).astype(bf16)
    weights = w_hidden_ref()
    back = (slope_ref[2] * dot(w_out_ref()[...], inputs, TN)).astype(bf16)
    back = (slope_ref[1] * dot(weights[1], back, NN)).astype(bf16)
    back = (slope_ref[0] * dot(weights[0], back, NN)).astype(bf16)
    sens = (0.25 * dot(w_in_ref()[...], back, NN)).astype(bf16)
    low_ref[...] = dot(sens[TOP:], groups[...], NN).astype(bf16)
    copy = pltpu.make_async_copy(low_ref, sens_far.at[pl.ds(TOP, FEAT - TOP)], sem)
    copy.start()
    top_ref[...] = dot(sens[:TOP], groups[...], NN)
    inner(temp_ref, heat_ref, links, part_ref)
    copy.wait()


def finish_kernel(
    first_in, second_in, border, part_in, links, ahead_ref, top_in, sens_in,
    sens_far, temp_far, top_ref, sem,
):
    temp_far.ref[...] = outer(ahead_ref, first_in[1], second_in[1], links)
    temp_far.put()
    adjoint = part_in[...] + received(first_in[0], second_in[0], border)
    top_ref[:LEV] = (top_in[:LEV] + adjoint).astype(bf16)
    top_ref[LEV:] = top_in[LEV:].astype(bf16)
    copy = pltpu.make_async_copy(top_ref, sens_far.at[pl.ds(0, TOP)], sem)
    copy.start()
    copy.wait()


def local(
    state_deviation, forcing, trajectory, w_in, w_hidden, w_out, biases, fine_order, group_parent,
    daylit_counts, sun_rank, adjacent_source_slots, outgoing_local_lists,
):
    near_pairs = [(i, i ^ 1) for i in range(DEVS)]
    far_pairs = [(i, (i + 1) % DEVS if i % 2 else (i - 1) % DEVS) for i in range(DEVS)]

    def swap(first, second):
        second = lax.ppermute(second, "cells", far_pairs)
        return lax.ppermute(first, "cells", near_pairs), second

    request, slot = kernel(
        route_kernel,
        "route",
        [group_parent],
        [(shape((DEVS, 1, 128), f32), True), (shape((1, COLS), i32), True)],
        flops=10**7,
    )
    asked = lax.all_to_all(request, "cells", 0, 0, tiled=True)

    side = shape((2, LEV, HALO), bf16)
    field = shape((LEV, CELLS), f32)
    all_links, all_border = shape((EXT, CELLS), bf16), shape((CELLS, 2 * HALO), bf16)
    all_groups = shape((COLS, CELLS), bf16)
    state_rows = (state_deviation, TOP, TOP)

    groups, drive, u, number = kernel(
        prepare_kernel,
        "prepare",
        [
            whole(fine_order), whole(state_deviation), whole(w_in), whole(trajectory), whole(biases),
            whole(sun_rank), whole(daylit_counts.reshape(1, DEVS)),
        ],
        [
            (all_groups, True),
            (shape((HID, COLS), f32), True),
            (shape((COLS, HID), bf16), True),
            (shape((1, COLS), f32), True),
        ],
        flops=2 * 10**9,
    )
    answer, token = kernel(
        answer_kernel,
        "answer",
        [whole(asked), whole(u), whole(number)],
        [(shape((SLOTS, HID), bf16), True), (shape((1, 128), f32), False)],
        scratch=[pltpu.VMEM((SLOTS, 128), f32)] * 2,
    )
    got = lax.all_to_all(answer.reshape(DEVS, CAP, HID), "cells", 0, 0, tiled=True)
    got = got.reshape(SLOTS, HID)
    links, border, part, first, second = kernel(
        build_kernel,
        "build",
        [
            whole(adjacent_source_slots), whole(outgoing_local_lists[0]), whole(forcing), state_rows,
            ("raw", token),
        ],
        [(all_links, "raw"), (all_border, True), (field, True), (side, True), (side, True)],
        scratch=[pltpu.VMEM((EXT, CELLS), bf16), pltpu.SemaphoreType.DMA((10,))],
        flops=3 * 10**9,
    )
    first, second = swap(first, second)

    groups, border, links, heat, temp, slope, part, heat_back, first, second = kernel(
        middle_kernel,
        "middle",
        [
            whole(got), whole(slot), whole(drive), whole(w_hidden), whole(w_out.T), whole(biases),
            whole(first), whole(second), whole(part), whole(forcing), state_rows,
            ("raw", groups), ("raw", border), ("raw", links),
        ],
        [
            (all_groups, False), (all_border, False), (all_links, False), (field, False),
            (field, False), (shape((3, HID, COLS), f32), False), (field, False), (field, False),
            (side, False), (side, False),
        ],
        scratch=[pltpu.SemaphoreType.DMA((7,))],
        limit=32,
        flops=5 * 10**9,
    )
    first, second = swap(first, second)
    (ahead,) = kernel(inner, "inner", [temp, heat, links], [(field, False)], limit=32)
    part, back, temp, first, second = kernel(
        third_kernel,
        "third",
        [first, second, border, part, heat_back, links, ahead],
        [
            (field, False), (shape((LEV, CELLS), bf16), False), (field, False), (side, False),
            (side, False),
        ],
        limit=32,
        flops=3 * 10**9,
    )
    first, second = swap(first, second)
    sens, top, ahead = kernel(
        window_kernel,
        "window",
        [temp, heat, links, slope, back, groups, whole(w_out.T), whole(w_hidden), whole(w_in)],
        [
            (shape((FEAT, CELLS), bf16), "raw"), (shape((TOP, CELLS), f32), False), (field, False),
        ],
        scratch=[pltpu.VMEM((FEAT - TOP, CELLS), bf16), pltpu.SemaphoreType.DMA],
        limit=32,
        flops=3 * 10**9,
    )
    sens, temp = kernel(
        finish_kernel,
        "finish",
        [first, second, border, part, links, ahead, top, ("raw", sens)],
        [(shape((FEAT, CELLS), bf16), "raw"), (field, True)],
        scratch=[pltpu.VMEM((TOP, CELLS), bf16), pltpu.SemaphoreType.DMA],
        limit=32,
        aliases={7: 0},
    )
    return temp, sens


def solution(mesh):
    return jax.shard_map(
        local,
        mesh=mesh,
        in_specs=(
            P(None, "cells"),
            P(None, "cells"),
            P(None, "cells"),
            P(),
            P(),
            P(),
            P(),
            P("cells", None),
            P("cells", None),
            P(),
            P("cells", None),
            P(None, "cells"),
            P("cells", None, None),
        ),
        out_specs=(P(None, "cells"), P(None, "cells")),
        check_vma=False,
    )
```

time: 140 us -> 96.6 us (0.69)
  local copies, waits for them, and re-layouts: 39.5 us -> 2.62 us
  starting transfers between devices: 51.8 us -> 39.1 us
  waiting for transfers between devices: 0.03 us -> 7.53 us
    unnamed x83 -> x12, local copies, waits for them, and re-layouts: 38.9 us -> 2.62 us
    ppermute x10 -> x6, starting transfers between devices: 36 us -> 22.4 us  [the longest x3 22.1 us: swap(): second = lax.ppermute(second, 'cells', far_pairs)]
    all_to_all x1, waiting for transfers between devices: 0.01 us -> 4.15 us  [local(): asked = lax.all_to_all(request, 'cells', 0, 0, tiled=True)]
    ppermute x10 -> x6, waiting for transfers between devices: 0.03 us -> 3.38 us  [the longest x3 3.37 us: swap(): second = lax.ppermute(second, 'cells', far_pairs)]
    pallas_call x12 -> x9, Pallas kernels: 46.9 us -> 46.1 us  [kernel(): pl.pallas_call(wrapped, out_shape=tuple(out_shapes), in_specs=in_specs, o...]
  transfers between devices with their start and end apart: 12 -> 8, of which waited for: 0 -> 3; matrix products, arithmetic and copies ran while one was open for 1% -> 0% of each run, Pallas kernels for 30% -> 22%
where the time goes in v2:
time: 96.6 us; the launch traced here: 96.3 us
  Pallas kernels  46.1 us (48%)
  starting transfers between devices  39.1 us (40%)
  waiting for transfers between devices  7.53 us (8%)
  local copies, waits for them, and re-layouts  2.62 us (3%)
    pallas_call x9, Pallas kernels, kernel(): pl.pallas_call(wrapped, out_shape=tuple(out_shapes), in_specs=in_specs, o...  46.1 us
    ppermute x3, starting transfers between devices, swap(): second = lax.ppermute(second, 'cells', far_pairs)  22.1 us
    all_to_all x1, starting transfers between devices, local(): asked = lax.all_to_all(request, 'cells', 0, 0, tiled=True)  11.1 us
    all_to_all x1, starting transfers between devices, local(): lax.all_to_all(answer.reshape(DEVS, CAP, HID), 'cells', 0, 0, tiled=True)  5.62 us
    all_to_all x1, waiting for transfers between devices, local(): asked = lax.all_to_all(request, 'cells', 0, 0, tiled=True)  4.15 us
    ppermute x3, waiting for transfers between devices, swap(): second = lax.ppermute(second, 'cells', far_pairs)  3.37 us
    unnamed x12, local copies, waits for them, and re-layouts  2.62 us
  transfers between devices with their start and end apart: 8, of which 3 were waited for; matrix products, arithmetic and copies ran while one was open for 0% of the time, Pallas kernels for 22%

profile of v2, /device:TPU:0, one launch (start us, length us, event | category | flops | bytes accessed | tf_op | source)
XLA Modules:
  0.0 96.3 jit_solution(9396384443444670077)
XLA Ops:
  0.6 0.0 copy-start
  0.6 0.7 copy-done
  1.3 1.2 %route.1 = (f32[128,1,128]{2,1,0:T(1,128)}, s32[1,512]{1,0:T(1,128)}) custom-call(s32[1,512]{1,0:T(1,128)S(1)} %copy-done), custom_call_target="tpu_custom_call" | custom-call | flops 10000000 | bytes 69632 | tf_op jit(solution)/shard_map/route/pallas_call | solution.py:123
  2.5 11.1 %all-to-all-start = ((f32[128,1,128]{2,1,0:T(1,128)}), f32[128,1,128]{2,1,0:T(1,128)S(1)}, u32[]{:S(2)}, u32[]{:S(2)}) async-start(f32[128,1,128]{2,1,0:T(1,128)} %get-tuple-element.35), calls=%async_computation | async-start | bytes 131072 | tf_op jit(solution)/shard_map/all_to_all | solution.py:426
  13.7 5.3 %prepare.1 = (bf16[512,2048]{1,0:T(8,128)(2,1)}, f32[256,512]{1,0:T(8,128)}, bf16[512,256]{1,0:T(8,128)(2,1)}, f32[1,512]{1,0:T(1,128)}) custom-call(s32[1,2048]{1,0:T(1,128)} %refs_0_.4, bf16[540,2048]{1,0:T(8,128)(2,1)} %refs_10_.1, bf16[540,256]{1,0:T(8,128)(2,1)} %refs_8_.1, bf16[540,512]{1,0:T(8,128)(2,1)} %refs_3_.3, f32[3,256]{1,0:T(4,128)} %refs_5_.3, ...), custom_call_target="tpu_custom_call" | custom-call | flops 2000000000 | bytes 5940736 | tf_op jit(solution)/shard_map/prepare/pallas_call | solution.py:123
  19.0 4.2 %all-to-all-done.refs_0_ = f32[128,1,128]{2,1,0:T(1,128)S(1)} async-done(((f32[128,1,128]{2,1,0:T(1,128)}), f32[128,1,128]{2,1,0:T(1,128)S(1)}, u32[]{:S(2)}, u32[]{:S(2)}) %all-to-all-start) | async-done | bytes 65568 | tf_op jit(solution)/shard_map/all_to_all | solution.py:426
  23.2 0.6 copy-done.5
  23.8 3.2 %answer.1 = (bf16[1024,256]{1,0:T(8,128)(2,1)}, f32[1,128]{1,0:T(1,128)S(1)}) custom-call(f32[128,1,128]{2,1,0:T(1,128)} %copy-done.5, bf16[512,256]{1,0:T(8,128)(2,1)} %get-tuple-element.36.refs_1_, f32[1,512]{1,0:T(1,128)} %get-tuple-element.37.refs_2_), custom_call_target="tpu_custom_call" | custom-call | flops 1000000000 | bytes 854528 | tf_op jit(solution)/shard_map/answer/pallas_call | solution.py:123
  27.0 0.5 copy-done.1
  27.5 5.6 %all-to-all-start.1 = ((bf16[128,8,256]{2,1,0:T(8,128)(2,1)}), bf16[128,8,256]{2,1,0:T(8,128)(2,1)S(1)}, u32[]{:S(2)}, u32[]{:S(2)}) async-start(bf16[128,8,256]{2,1,0:T(8,128)(2,1)} %bitcast.6), calls=%async_computation.1 | async-start | bytes 1048576 | tf_op jit(solution)/shard_map/all_to_all | solution.py:456
  33.2 9.0 %build.1 = (bf16[2560,2048]{1,0:T(8,128)(2,1)}, bf16[2048,512]{1,0:T(8,128)(2,1)}, f32[90,2048]{1,0:T(8,128)}, bf16[2,90,256]{2,1,0:T(8,128)(2,1)}, bf16[2,90,256]{2,1,0:T(8,128)(2,1)}) custom-call(s32[6,2048]{1,0:T(8,128)} %refs_0_.5, s32[2,256]{1,0:T(2,128)} %bitcast.9, bf16[90,2048]{1,0:T(8,128)(2,1)} %refs_9_.1, bf16[540,2048]{1,0:T(8,128)(2,1)} %refs_10_.1, ...), custom_call_target="tpu_custom_call" | custom-call | flops 3000000000 | bytes 16136704 | tf_op jit(solution)/shard_map/build/pallas_call | solution.py:123
  42.2 0.1 collective-permute-start
  42.2 7.4 %collective-permute-start.1 = (bf16[2,90,256]{2,1,0:T(8,128)(2,1)}, bf16[2,90,256]{2,1,0:T(8,128)(2,1)S(1)}, u32[]{:S(2)}, u32[]{:S(2)}) collective-permute-start(bf16[2,90,256]{2,1,0:T(8,128)(2,1)} %get-tuple-element.43), channel_id=1, source_target_pairs={{0,127},{1,2},{2,1},{3,4},{4,3},{5,6},{6,5},{7,8},{8,7},{9,10},{10... | collective-permute-start | bytes 276488 | tf_op jit(solution)/shard_map/ppermute | solution.py:416
  49.7 0.0 collective-permute-done.refs_6_
  49.7 2.5 %collective-permute-done.1.refs_7_ = bf16[2,90,256]{2,1,0:T(8,128)(2,1)S(1)} collective-permute-done((bf16[2,90,256]{2,1,0:T(8,128)(2,1)}, bf16[2,90,256]{2,1,0:T(8,128)(2,1)S(1)}, u32[]{:S(2)}, u32[]{:S(2)}) %collective-permute-start.1) | collective-permute-done | bytes 92192 | tf_op jit(solution)/shard_map/ppermute | solution.py:416
  52.2 0.0 all-to-all-done.1
  52.2 0.0 copy-done.3
  52.2 0.6 copy-done.4
  52.8 0.2 copy-done.2
  53.0 13.7 %middle.1 = (bf16[512,2048]{1,0:T(8,128)(2,1)S(1)}, bf16[2048,512]{1,0:T(8,128)(2,1)S(1)}, bf16[2560,2048]{1,0:T(8,128)(2,1)S(1)}, f32[90,2048]{1,0:T(8,128)S(1)...) custom-call(bf16[1024,256]{1,0:T(8,128)(2,1)} %bitcast.5, ...), custom_call_target="tpu_custom_call" | custom-call | flops 5000000000 | bytes 38930432 | tf_op jit(solution)/shard_map/middle/pallas_call | solution.py:123
  66.7 0.1 collective-permute-start.2
  66.8 7.2 %collective-permute-start.3 = (bf16[2,90,256]{2,1,0:T(8,128)(2,1)S(1)}, bf16[2,90,256]{2,1,0:T(8,128)(2,1)S(1)}, u32[]{:S(2)}, u32[]{:S(2)}) collective-permute-start(bf16[2,90,256]{2,1,0:T(8,128)(2,1)S(1)} %get-tuple-element.49), channel_id=1, source_target_pairs={{0,127},{1,2},{2,1},{3,4},{4,3},{5,6},{6,5},{7,8},{8,7},{9,10},{10... | collective-permute-start | bytes 276488 | tf_op jit(solution)/shard_map/ppermute | solution.py:416
  74.1 1.5 %inner.1.refs_6_ = f32[90,2048]{1,0:T(8,128)S(1)} custom-call(f32[90,2048]{1,0:T(8,128)S(1)} %get-tuple-element.54.refs_0_, f32[90,2048]{1,0:T(8,128)S(1)} %get-tuple-element.55.refs_1_, bf16[2560,2048]{1,0:T(8,128)(2,1)S(1)} %get-tuple-element.53.refs_2_.refs_5_.refs_4_), custom_call_target="tpu_custom_call" | custom-call | flops 1000000000 | bytes 12697600 | tf_op jit(solution)/shard_map/inner/pallas_call | solution.py:123
  75.5 0.0 collective-permute-done.2.refs_0_
  75.6 0.8 collective-permute-done.3.refs_1_
  76.4 4.6 %third.1 = (f32[90,2048]{1,0:T(8,128)S(1)}, bf16[90,2048]{1,0:T(8,128)(2,1)S(1)}, f32[90,2048]{1,0:T(8,128)S(1)}, bf16[2,90,256]{2,1,0:T(8,128)(2,1)S(1)}, bf16[2,90,256]{2,1,0:T(8,128)(2,1)S(1)}) custom-call(bf16[2,90,256]{2,1,0:T(8,128)(2,1)S(1)} %collective-permute-done.2.refs_0_, bf16[2,90,256]{2,1,0:T(8,128)(2,1)S(1)} %collective-permute-done.3.refs_1_, ...), custom_call_target="tpu_custom_call" | custom-call | flops 3000000000 | bytes 17006592 | tf_op jit(solution)/shard_map/third/pallas_call | solution.py:123
  81.0 0.1 collective-permute-start.4
  81.1 7.5 %collective-permute-start.5 = (bf16[2,90,256]{2,1,0:T(8,128)(2,1)S(1)}, bf16[2,90,256]{2,1,0:T(8,128)(2,1)S(1)}, u32[]{:S(2)}, u32[]{:S(2)}) collective-permute-start(bf16[2,90,256]{2,1,0:T(8,128)(2,1)S(1)} %get-tuple-element.57), channel_id=1, source_target_pairs={{0,127},{1,2},{2,1},{3,4},{4,3},{5,6},{6,5},{7,8},{8,7},{9,10},{10... | collective-permute-start | bytes 276488 | tf_op jit(solution)/shard_map/ppermute | solution.py:416
  88.6 5.7 %window.1 = (bf16[540,2048]{1,0:T(8,128)(2,1)}, f32[96,2048]{1,0:T(8,128)S(1)}, f32[90,2048]{1,0:T(8,128)S(1)}) custom-call(f32[90,2048]{1,0:T(8,128)S(1)} %get-tuple-element.59.refs_0_, f32[90,2048]{1,0:T(8,128)S(1)} %get-tuple-element.55.refs_1_, bf16[2560,2048]{1,0:T(8,128)(2,1)S(1)} %get-tuple-element.53.refs_2_.refs_5_.refs_4_, ...), custom_call_target="tpu_custom_call" | custom-call | flops 3000000000 | bytes 20319232 | tf_op jit(solution)/shard_map/window/pallas_call | solution.py:123
  94.2 0.0 collective-permute-done.4.refs_0_
  94.2 0.0 collective-permute-done.5.refs_1_
  94.3 1.9 %finish.1 = (bf16[540,2048]{1,0:T(8,128)(2,1)}, f32[90,2048]{1,0:T(8,128)}) custom-call(bf16[2,90,256]{2,1,0:T(8,128)(2,1)S(1)} %collective-permute-done.4.refs_0_, bf16[2,90,256]{2,1,0:T(8,128)(2,1)S(1)} %collective-permute-done.5.refs_1_, bf16[2048,512]{1,0:T(8,128)(2,1)S(1)} %get-tuple-element.50.refs_2_, ...), custom_call_target="tpu_custom_call", output_to_operand_aliasing={{0}: (7, {})} | custom-call | flops 1000000000 | bytes 20189184 | tf_op jit(solution)/shard_map/finish/pallas_call | solution.py:123
  (5 shorter events, 0.0 us)
Async XLA Ops:
  0.6 0.7 copy-start
  2.5 20.6 %all-to-all-start = ((f32[128,1,128]{2,1,0:T(1,128)}), f32[128,1,128]{2,1,0:T(1,128)S(1)}, u32[]{:S(2)}, u32[]{:S(2)}) async-start(f32[128,1,128]{2,1,0:T(1,128)} %get-tuple-element.35), calls=%async_computation | async-start | bytes 131072 | tf_op jit(solution)/shard_map/all_to_all | solution.py:426
  23.2 0.6 copy-start.5
  27.0 0.5 copy-start.1
  27.5 24.7 %all-to-all-start.1 = ((bf16[128,8,256]{2,1,0:T(8,128)(2,1)}), bf16[128,8,256]{2,1,0:T(8,128)(2,1)S(1)}, u32[]{:S(2)}, u32[]{:S(2)}) async-start(bf16[128,8,256]{2,1,0:T(8,128)(2,1)} %bitcast.6), calls=%async_computation.1 | async-start | bytes 1048576 | tf_op jit(solution)/shard_map/all_to_all | solution.py:456
  42.2 7.5 %collective-permute-start = (bf16[2,90,256]{2,1,0:T(8,128)(2,1)}, bf16[2,90,256]{2,1,0:T(8,128)(2,1)S(1)}, u32[]{:S(2)}, u32[]{:S(2)}) collective-permute-start(bf16[2,90,256]{2,1,0:T(8,128)(2,1)} %get-tuple-element.42), channel_id=1, source_target_pairs={{0,1},{1,0},{2,3},{3,2},{4,5},{5,4},{6,7},{7,6},{8,9},{9,8},{10,11... | collective-permute-start | bytes 276488 | tf_op jit(solution)/shard_map/ppermute | solution.py:417
  42.2 9.9 %collective-permute-start.1 = (bf16[2,90,256]{2,1,0:T(8,128)(2,1)}, bf16[2,90,256]{2,1,0:T(8,128)(2,1)S(1)}, u32[]{:S(2)}, u32[]{:S(2)}) collective-permute-start(bf16[2,90,256]{2,1,0:T(8,128)(2,1)} %get-tuple-element.43), channel_id=1, source_target_pairs={{0,127},{1,2},{2,1},{3,4},{4,3},{5,6},{6,5},{7,8},{8,7},{9,10},{10... | collective-permute-start | bytes 276488 | tf_op jit(solution)/shard_map/ppermute | solution.py:416
  49.7 2.5 %copy-start.3 = (bf16[2,90,256]{2,1,0:T(8,128)(2,1)}, bf16[2,90,256]{2,1,0:T(8,128)(2,1)S(1)}, u32[]{:S(2)}) copy-start(bf16[2,90,256]{2,1,0:T(8,128)(2,1)S(1)} %collective-permute-done.refs_6_) | copy-start | bytes 276484
  52.2 0.6 copy-start.4
  52.2 0.8 copy-start.2
  66.7 8.8 %collective-permute-start.2 = (bf16[2,90,256]{2,1,0:T(8,128)(2,1)S(1)}, bf16[2,90,256]{2,1,0:T(8,128)(2,1)S(1)}, u32[]{:S(2)}, u32[]{:S(2)}) collective-permute-start(bf16[2,90,256]{2,1,0:T(8,128)(2,1)S(1)} %get-tuple-element.48), channel_id=1, source_target_pairs={{0,1},{1,0},{2,3},{3,2},{4,5},{5,4},{6,7},{7,6},{8,9},{9,8},{10,11... | collective-permute-start | bytes 276488 | tf_op jit(solution)/shard_map/ppermute | solution.py:417
  66.8 9.6 %collective-permute-start.3 = (bf16[2,90,256]{2,1,0:T(8,128)(2,1)S(1)}, bf16[2,90,256]{2,1,0:T(8,128)(2,1)S(1)}, u32[]{:S(2)}, u32[]{:S(2)}) collective-permute-start(bf16[2,90,256]{2,1,0:T(8,128)(2,1)S(1)} %get-tuple-element.49), channel_id=1, source_target_pairs={{0,127},{1,2},{2,1},{3,4},{4,3},{5,6},{6,5},{7,8},{8,7},{9,10},{10... | collective-permute-start | bytes 276488 | tf_op jit(solution)/shard_map/ppermute | solution.py:416
  81.0 13.2 %collective-permute-start.4 = (bf16[2,90,256]{2,1,0:T(8,128)(2,1)S(1)}, bf16[2,90,256]{2,1,0:T(8,128)(2,1)S(1)}, u32[]{:S(2)}, u32[]{:S(2)}) collective-permute-start(bf16[2,90,256]{2,1,0:T(8,128)(2,1)S(1)} %get-tuple-element.56), channel_id=1, source_target_pairs={{0,1},{1,0},{2,3},{3,2},{4,5},{5,4},{6,7},{7,6},{8,9},{9,8},{10,11... | collective-permute-start | bytes 276488 | tf_op jit(solution)/shard_map/ppermute | solution.py:417
  81.1 13.1 %collective-permute-start.5 = (bf16[2,90,256]{2,1,0:T(8,128)(2,1)S(1)}, bf16[2,90,256]{2,1,0:T(8,128)(2,1)S(1)}, u32[]{:S(2)}, u32[]{:S(2)}) collective-permute-start(bf16[2,90,256]{2,1,0:T(8,128)(2,1)S(1)} %get-tuple-element.57), channel_id=1, source_target_pairs={{0,127},{1,2},{2,1},{3,4},{4,3},{5,6},{6,5},{7,8},{8,7},{9,10},{10... | collective-permute-start | bytes 276488 | tf_op jit(solution)/shard_map/ppermute | solution.py:416

commit v3 on v2

--- a/solution.py
+++ b/solution.py
@@ -149,6 +149,12 @@
     return jnp.where(mask, 1.0, 0.0).astype(bf16)
 
 
+def pick_rows(index, block, columns):
+    here = jnp.where(index >> 8 == block, index & 255, -1).astype(f32).astype(bf16)
+    place = row_iota(256, columns).astype(f32).astype(bf16)
+    return jnp.where(place == here, jnp.ones((), bf16), jnp.zeros((), bf16))
+
+
 def to_column(row):
     return jnp.broadcast_to(row, (128, row.shape[1])).T[:, :1]
 
@@ -183,7 +189,8 @@
     group = order_ref()[...] >> 2
     for c in range(8):
         sl = slice(c * 256, (c + 1) * 256)
-        groups_ref.ref[:, sl] = onehot(row_iota(COLS, 256) == group[:, sl])
+        for b in range(2):
+            groups_ref.ref[b * 256 : (b + 1) * 256, sl] = pick_rows(group[:, sl], b, 256)
     groups_ref.put()
     z = dot(traj_ref()[...], w_in_ref()[...], TN) + bias_ref()[0:1, :]
     decay = jnp.exp(-2.0 * jnp.minimum(jnp.abs(z), 30.0))
@@ -199,14 +206,16 @@
 
 
 def answer_kernel(request_ref, u_ref, number_ref, answer_ref, token_ref, left_ref, right_ref):
-    request = request_ref()[...].reshape(DEVS, 128)
-    number, u = number_ref()[...], u_ref()
-    token_ref[...] = number[:, :128]
+    request = request_ref[...].reshape(DEVS, 128)
+    number = number_ref()[...]
+    token_ref.ref[...] = number[:, :128]
+    token_ref.put()
+    chosen = [onehot(request[:, k : k + 1] == number) for k in range(CAP)]
+    rows = dot(jnp.concatenate(chosen, axis=0), u_ref()[...], NN)
     for k in range(CAP):
-        chosen = onehot(request[:, k : k + 1] == number)
-        rows = dot(chosen, u[...], NN)
-        left_ref[pl.ds(k, DEVS, stride=CAP), :] = rows[:, :128]
-        right_ref[pl.ds(k, DEVS, stride=CAP), :] = rows[:, 128:]
+        block = slice(k * DEVS, (k + 1) * DEVS)
+        left_ref[pl.ds(k, DEVS, stride=CAP), :] = rows[block, :128]
+        right_ref[pl.ds(k, DEVS, stride=CAP), :] = rows[block, 128:]
     answer_ref.ref[:, :128] = left_ref[...].astype(bf16)
     answer_ref.ref[:, 128:] = right_ref[...].astype(bf16)
     answer_ref.put()
@@ -232,38 +241,48 @@
 
     def fill(jb):
         here = jnp.where(high == jb, low, -1).astype(f32).astype(bf16)
-        rows = slice(jb * 256, (jb + 1) * 256)
         for c in range(8):
             sl = slice(c * 256, (c + 1) * 256)
             place = row_iota(256, 256).astype(f32).astype(bf16)
             count = jnp.zeros((256, 256), bf16)
             for k in range(6):
                 count = jnp.where(here[k : k + 1, sl] == place, times[k : k + 1, sl], count)
-            links[rows, sl] = count
-        out(jb).start()
-        return SPREAD * dot(forcing[...], links[rows, :], NT)
+            links[jb * 256 : (jb + 1) * 256, sl] = count
+
+    def share(jb):
+        return SPREAD * dot(forcing[...], links[jb * 256 : (jb + 1) * 256, :], NT)
 
     def out(jb):
         rows = pl.ds(jb * 256, 256)
         return pltpu.make_async_copy(links.at[rows], links_ref.at[rows], sems.at[jb])
 
-    first_ref.ref[0] = fill(8).astype(bf16)
-    second_ref.ref[0] = fill(9).astype(bf16)
-    state = state_ref()
+    def consume(jb):
+        if jb == 8:
+            first_ref.ref[0] = share(jb).astype(bf16)
+        elif jb == 9:
+            second_ref.ref[0] = share(jb).astype(bf16)
+        else:
+            sl = slice(jb * 256, (jb + 1) * 256)
+            part_ref.ref[:, sl] = KEEP * forcing[:, sl].astype(f32) + share(jb)
+
     for b in range(8):
         sl = slice(b * 256, (b + 1) * 256)
-        cell = row_iota(256, 256) + b * 256
-        border_ref.ref[sl, :HALO] = onehot(cell == near)
-        border_ref.ref[sl, HALO:] = onehot(cell == far)
+        border_ref.ref[sl, :HALO] = pick_rows(near, b, 256)
+        border_ref.ref[sl, HALO:] = pick_rows(far, b, 256)
     border_ref.put()
+    state = state_ref()
     border = dot(state[:LEV, :], border_ref.ref[...], NN)
     first_ref.ref[1] = border[:, :HALO].astype(bf16)
     second_ref.ref[1] = border[:, HALO:].astype(bf16)
+    order = (8, 9, *range(8))
+    fill(order[0])
+    for now, later in zip(order, order[1:] + (None,)):
+        if later is not None:
+            fill(later)
+        consume(now)
+        out(now).start()
     first_ref.put()
     second_ref.put()
-    for jb in range(8):
-        sl = slice(jb * 256, (jb + 1) * 256)
-        part_ref.ref[:, sl] = KEEP * forcing[:, sl].astype(f32) + fill(jb)
     part_ref.put()
     for jb in range(10):
         out(jb).wait()
@@ -273,16 +292,17 @@
     return dot(first, border[:, :HALO], NT) + dot(second, border[:, HALO:], NT)
 
 
-def pull(adjoint, links, wait, part_ref, first_ref, second_ref):
-    rounded = adjoint.astype(bf16)
-    wait(OWN)
+def push(rounded, links, first_ref, second_ref):
     share = SPREAD * dot(rounded, links[CELLS:, :], NT)
     first_ref[0] = share[:, :HALO].astype(bf16)
     second_ref[0] = share[:, HALO:].astype(bf16)
+
+
+def pull(adjoint_ref, links, part_ref):
+    rounded = adjoint_ref[...].astype(bf16)
     for i in range(OWN):
         sl = slice(i * PIECE, (i + 1) * PIECE)
-        wait(i)
-        part_ref[:, sl] = KEEP * adjoint[:, sl] + SPREAD * dot(rounded, links[sl, :], NT)
+        part_ref[:, sl] = KEEP * adjoint_ref[:, sl] + SPREAD * dot(rounded, links[sl, :], NT)
 
 
 def send_border(temp, border, first_ref, second_ref):
@@ -291,10 +311,10 @@
     second_ref[1] = values[:, HALO:].astype(bf16)
 
 
-def middle_kernel(
-    answer_ref, slot_ref, drive_ref, w_hidden_ref, w_out_ref, bias_ref, first_in, second_in, part_in,
-    forcing_ref, state_ref, groups_far, border_far, links_far,
-    groups, border, links, heat_ref, temp_ref, slope_ref, part_ref, heat_back_ref, first_ref, second_ref,
+def network_kernel(
+    answer_ref, slot_ref, drive_ref, w_hidden_ref, w_out_ref, bias_ref, state_ref,
+    groups_far, border_far, links_far,
+    groups, border, links, heat_ref, slope_ref, ahead_ref,
     sems,
 ):
     groups_copy = pltpu.make_async_copy(groups_far, groups, sems.at[5])
@@ -305,11 +325,12 @@
         return pltpu.make_async_copy(links_far.at[rows], links.at[rows], sems.at[i])
 
     groups_copy.start()
+    for i in range(OWN + 1):
+        piece(i).start()
     border_copy.start()
-    for i in (OWN, *range(OWN)):
-        piece(i).start()
-
-    chosen = onehot(row_iota(SLOTS, COLS) == slot_ref()[...])
+
+    slots = slot_ref()[...]
+    chosen = jnp.concatenate([pick_rows(slots, b, COLS) for b in range(SLOTS // 256)], axis=0)
     u = dot(answer_ref()[...], chosen, TN)
     size = jnp.abs(u)
     inverse = 1.0 / (1.0 + size)
@@ -328,29 +349,32 @@
     heating = dot(w_out_ref()[...], tangent, NN).astype(bf16)
     groups_copy.wait()
     heat_ref[...] = dot(heating, groups[...], NN)
-
+    for i in range(OWN):
+        piece(i).wait()
+    inner(state_ref(), heat_ref, links, ahead_ref)
+    piece(OWN).wait()
     border_copy.wait()
-    adjoint = part_in()[...] + received(first_in()[0], second_in()[0], border)
+
+
+def second_kernel(
+    first_in, second_in, border, part_in, forcing_ref, links, ahead_ref,
+    adjoint_ref, heat_back_ref, temp_ref, first_ref, second_ref,
+):
+    adjoint = part_in()[...] + received(first_in[0], second_in[0], border)
+    adjoint_ref[...] = adjoint
+    push(adjoint.astype(bf16), links, first_ref, second_ref)
+    temp = outer(ahead_ref, first_in[1], second_in[1], links)
+    temp_ref[...] = temp
+    send_border(temp, border, first_ref, second_ref)
     heat_back_ref[...] = forcing_ref()[...].astype(f32) + adjoint
-    pull(adjoint, links, lambda i: piece(i).wait(), part_ref, first_ref, second_ref)
-    state = state_ref()
-    sides = jnp.concatenate([state[:LEV, :], first_in.ref[1], second_in.ref[1]], axis=1)
-    for i in range(OWN):
-        sl = slice(i * PIECE, (i + 1) * PIECE)
-        temp_ref[:, sl] = (
-            KEEP * state[:LEV, sl].astype(f32)
-            + heat_ref[:, sl]
-            + SPREAD * dot(sides, links[:, sl], NN)
-        )
-    send_border(temp_ref[...], border, first_ref, second_ref)
 
 
 def inner(temp_ref, heat_ref, links, part_ref):
-    rounded = temp_ref[...].astype(bf16)
+    rounded = temp_ref[:LEV, :].astype(bf16)
     for i in range(OWN):
         sl = slice(i * PIECE, (i + 1) * PIECE)
         part_ref[:, sl] = (
-            KEEP * temp_ref[:, sl]
+            KEEP * temp_ref[:LEV, sl].astype(f32)
             + heat_ref[:, sl]
             + SPREAD * dot(rounded, links[:CELLS, sl], NN)
         )
@@ -361,21 +385,27 @@
     return part_ref[...] + SPREAD * dot(sides, links[CELLS:, :], NN)
 
 
+def between_kernel(adjoint_ref, temp_ref, heat_ref, links, part_ref, ahead_ref):
+    pull(adjoint_ref, links, part_ref)
+    inner(temp_ref, heat_ref, links, ahead_ref)
+
+
 def third_kernel(
     first_in, second_in, border, part_in, heat_back_ref, links, ahead_ref,
-    part_ref, back_ref, temp_ref, first_ref, second_ref,
+    adjoint_ref, back_ref, temp_ref, first_ref, second_ref,
 ):
     adjoint = part_in[...] + received(first_in[0], second_in[0], border)
-    back_ref[...] = (heat_back_ref[...] + adjoint).astype(bf16)
-    pull(adjoint, links, lambda i: None, part_ref, first_ref, second_ref)
+    adjoint_ref[...] = adjoint
+    push(adjoint.astype(bf16), links, first_ref, second_ref)
     temp = outer(ahead_ref, first_in[1], second_in[1], links)
     temp_ref[...] = temp
     send_border(temp, border, first_ref, second_ref)
+    back_ref[...] = (heat_back_ref[...] + adjoint).astype(bf16)
 
 
 def window_kernel(
-    temp_ref, heat_ref, links, slope_ref, back_ref, groups, w_out_ref, w_hidden_ref, w_in_ref,
-    sens_far, top_ref, part_ref, low_ref, sem,
+    adjoint_ref, temp_ref, heat_ref, links, slope_ref, back_ref, groups, w_out_ref, w_hidden_ref,
+    w_in_ref, sens_far, top_ref, part_ref, ahead_ref, low_ref, sem,
 ):
     inputs = dot(back_ref[...], groups[...], NT).astype(bf16)
     weights = w_hidden_ref()
@@ -387,7 +417,8 @@
     copy = pltpu.make_async_copy(low_ref, sens_far.at[pl.ds(TOP, FEAT - TOP)], sem)
     copy.start()
     top_ref[...] = dot(sens[:TOP], groups[...], NN)
-    inner(temp_ref, heat_ref, links, part_ref)
+    inner(temp_ref, heat_ref, links, ahead_ref)
+    pull(adjoint_ref, links, part_ref)
     copy.wait()
 
 
@@ -449,8 +480,8 @@
     answer, token = kernel(
         answer_kernel,
         "answer",
-        [whole(asked), whole(u), whole(number)],
-        [(shape((SLOTS, HID), bf16), True), (shape((1, 128), f32), False)],
+        [asked, whole(u), whole(number)],
+        [(shape((SLOTS, HID), bf16), True), (shape((1, 128), f32), True)],
         scratch=[pltpu.VMEM((SLOTS, 128), f32)] * 2,
     )
     got = lax.all_to_all(answer.reshape(DEVS, CAP, HID), "cells", 0, 0, tiled=True)
@@ -468,43 +499,50 @@
     )
     first, second = swap(first, second)
 
-    groups, border, links, heat, temp, slope, part, heat_back, first, second = kernel(
-        middle_kernel,
-        "middle",
+    near = (field, False)
+    groups, border, links, heat, slope, ahead = kernel(
+        network_kernel,
+        "network",
         [
             whole(got), whole(slot), whole(drive), whole(w_hidden), whole(w_out.T), whole(biases),
-            whole(first), whole(second), whole(part), whole(forcing), state_rows,
-            ("raw", groups), ("raw", border), ("raw", links),
-        ],
-        [
-            (all_groups, False), (all_border, False), (all_links, False), (field, False),
-            (field, False), (shape((3, HID, COLS), f32), False), (field, False), (field, False),
-            (side, False), (side, False),
+            state_rows, ("raw", groups), ("raw", border), ("raw", links),
+        ],
+        [
+            (all_groups, False), (all_border, False), (all_links, False), near,
+            (shape((3, HID, COLS), f32), False), near,
         ],
         scratch=[pltpu.SemaphoreType.DMA((7,))],
         limit=32,
         flops=5 * 10**9,
     )
+    adjoint, heat_back, temp, first, second = kernel(
+        second_kernel,
+        "second",
+        [first, second, border, whole(part), whole(forcing), links, ahead],
+        [near, near, near, (side, False), (side, False)],
+        limit=32,
+    )
     first, second = swap(first, second)
-    (ahead,) = kernel(inner, "inner", [temp, heat, links], [(field, False)], limit=32)
-    part, back, temp, first, second = kernel(
+    part, ahead = kernel(
+        between_kernel, "between", [adjoint, temp, heat, links], [near, near], limit=32
+    )
+    adjoint, back, temp, first, second = kernel(
         third_kernel,
         "third",
         [first, second, border, part, heat_back, links, ahead],
-        [
-            (field, False), (shape((LEV, CELLS), bf16), False), (field, False), (side, False),
-            (side, False),
-        ],
+        [near, (shape((LEV, CELLS), bf16), False), near, (side, False), (side, False)],
         limit=32,
-        flops=3 * 10**9,
     )
     first, second = swap(first, second)
-    sens, top, ahead = kernel(
+    sens, top, part, ahead = kernel(
         window_kernel,
         "window",
-        [temp, heat, links, slope, back, groups, whole(w_out.T), whole(w_hidden), whole(w_in)],
-        [
-            (shape((FEAT, CELLS), bf16), "raw"), (shape((TOP, CELLS), f32), False), (field, False),
+        [
+            adjoint, temp, heat, links, slope, back, groups, whole(w_out.T), whole(w_hidden),
+            whole(w_in),
+        ],
+        [
+            (shape((FEAT, CELLS), bf16), "raw"), (shape((TOP, CELLS), f32), False), near, near,
         ],
         scratch=[pltpu.VMEM((FEAT - TOP, CELLS), bf16), pltpu.SemaphoreType.DMA],
         limit=32,

time: 96.6 us -> 85.5 us (0.89)
  starting transfers between devices: 39.1 us -> 27.2 us
  waiting for transfers between devices: 7.53 us -> 8.99 us
  local copies, waits for them, and re-layouts: 2.62 us -> 1.48 us
    ppermute x3, starting transfers between devices: 22.1 us -> 10.2 us  [swap(): second = lax.ppermute(second, 'cells', far_pairs)]
    ppermute x3, waiting for transfers between devices: 3.37 us -> 4.8 us  [swap(): second = lax.ppermute(second, 'cells', far_pairs)]
    unnamed x12 -> x4, local copies, waits for them, and re-layouts: 2.62 us -> 1.48 us
    pallas_call x9 -> x10, Pallas kernels: 46.1 us -> 46.6 us  [kernel(): pl.pallas_call(wrapped, out_shape=tuple(out_shapes), in_specs=in_specs, o...]
  transfers between devices with their start and end apart: 8 -> 8, of which waited for: 3 -> 2; matrix products, arithmetic and copies ran while one was open for 0% -> 0% of each run, Pallas kernels for 22% -> 41%
where the time goes in v3:
time: 85.5 us; the launch traced here: 85.2 us
  Pallas kernels  46.6 us (55%)
  starting transfers between devices  27.2 us (32%)
  waiting for transfers between devices  8.99 us (11%)
  local copies, waits for them, and re-layouts  1.48 us (2%)
  between operations  0.96 us (1%)
    pallas_call x10, Pallas kernels, kernel(): pl.pallas_call(wrapped, out_shape=tuple(out_shapes), in_specs=in_specs, o...  46.6 us
    all_to_all x1, starting transfers between devices, local(): asked = lax.all_to_all(request, 'cells', 0, 0, tiled=True)  11.1 us
    ppermute x3, starting transfers between devices, swap(): second = lax.ppermute(second, 'cells', far_pairs)  10.2 us
    all_to_all x1, starting transfers between devices, local(): lax.all_to_all(answer.reshape(DEVS, CAP, HID), 'cells', 0, 0, tiled=True)  5.61 us
    ppermute x3, waiting for transfers between devices, swap(): second = lax.ppermute(second, 'cells', far_pairs)  4.8 us
    all_to_all x1, waiting for transfers between devices, local(): asked = lax.all_to_all(request, 'cells', 0, 0, tiled=True)  4.17 us
  transfers between devices with their start and end apart: 8, of which 2 were waited for; matrix products, arithmetic and copies ran while one was open for 0% of the time, Pallas kernels for 41%

profile of v3, /device:TPU:0, one launch (start us, length us, event | category | flops | bytes accessed | tf_op | source)
XLA Modules:
  0.0 85.2 jit_solution(3506678301418533265)
XLA Ops:
  0.6 0.0 copy-start
  0.6 0.7 copy-done
  1.3 1.2 %route.1 = (f32[128,1,128]{2,1,0:T(1,128)}, s32[1,512]{1,0:T(1,128)}) custom-call(s32[1,512]{1,0:T(1,128)S(1)} %copy-done), custom_call_target="tpu_custom_call" | custom-call | flops 10000000 | bytes 69632 | tf_op jit(solution)/shard_map/route/pallas_call | solution.py:123
  2.5 11.1 %all-to-all-start = ((f32[128,1,128]{2,1,0:T(1,128)}), f32[128,1,128]{2,1,0:T(1,128)S(1)}, u32[]{:S(2)}, u32[]{:S(2)}) async-start(f32[128,1,128]{2,1,0:T(1,128)} %get-tuple-element.39), calls=%async_computation | async-start | bytes 131072 | tf_op jit(solution)/shard_map/all_to_all | solution.py:457
  13.7 5.3 %prepare.1 = (bf16[512,2048]{1,0:T(8,128)(2,1)}, f32[256,512]{1,0:T(8,128)}, bf16[512,256]{1,0:T(8,128)(2,1)}, f32[1,512]{1,0:T(1,128)}) custom-call(s32[1,2048]{1,0:T(1,128)} %refs_0_.4, bf16[540,2048]{1,0:T(8,128)(2,1)} %refs_6_.1, bf16[540,256]{1,0:T(8,128)(2,1)} %refs_9_.1, bf16[540,512]{1,0:T(8,128)(2,1)} %refs_3_.3, f32[3,256]{1,0:T(4,128)} %refs_5_.3, ...), custom_call_target="tpu_custom_call" | custom-call | flops 2000000000 | bytes 5940736 | tf_op jit(solution)/shard_map/prepare/pallas_call | solution.py:123
  19.0 4.2 %all-to-all-done.refs_0_ = f32[128,1,128]{2,1,0:T(1,128)S(1)} async-done(((f32[128,1,128]{2,1,0:T(1,128)}), f32[128,1,128]{2,1,0:T(1,128)S(1)}, u32[]{:S(2)}, u32[]{:S(2)}) %all-to-all-start) | async-done | bytes 65568 | tf_op jit(solution)/shard_map/all_to_all | solution.py:457
  23.2 3.3 %answer.1 = (bf16[1024,256]{1,0:T(8,128)(2,1)}, f32[1,128]{1,0:T(1,128)}) custom-call(f32[128,1,128]{2,1,0:T(1,128)S(1)} %all-to-all-done.refs_0_, bf16[512,256]{1,0:T(8,128)(2,1)} %get-tuple-element.40.refs_1_, f32[1,512]{1,0:T(1,128)} %get-tuple-element.41.refs_2_), custom_call_target="tpu_custom_call" | custom-call | flops 1000000000 | bytes 854528 | tf_op jit(solution)/shard_map/answer/pallas_call | solution.py:123
  26.5 5.6 %all-to-all-start.1 = ((bf16[128,8,256]{2,1,0:T(8,128)(2,1)}), bf16[128,8,256]{2,1,0:T(8,128)(2,1)S(1)}, u32[]{:S(2)}, u32[]{:S(2)}) async-start(bf16[128,8,256]{2,1,0:T(8,128)(2,1)} %bitcast.6), calls=%async_computation.1 | async-start | bytes 1048576 | tf_op jit(solution)/shard_map/all_to_all | solution.py:487
  32.1 9.1 %build.1 = (bf16[2560,2048]{1,0:T(8,128)(2,1)}, bf16[2048,512]{1,0:T(8,128)(2,1)}, f32[90,2048]{1,0:T(8,128)}, bf16[2,90,256]{2,1,0:T(8,128)(2,1)}, bf16[2,90,256]{2,1,0:T(8,128)(2,1)}) custom-call(s32[6,2048]{1,0:T(8,128)} %refs_0_.5, s32[2,256]{1,0:T(2,128)} %bitcast.9, bf16[90,2048]{1,0:T(8,128)(2,1)} %refs_4_.3, bf16[540,2048]{1,0:T(8,128)(2,1)} %refs_6_.1, ...), custom_call_target="tpu_custom_call" | custom-call | flops 3000000000 | bytes 16136704 | tf_op jit(solution)/shard_map/build/pallas_call | solution.py:123
  41.3 0.1 collective-permute-start
  41.3 7.4 %collective-permute-start.1 = (bf16[2,90,256]{2,1,0:T(8,128)(2,1)}, bf16[2,90,256]{2,1,0:T(8,128)(2,1)S(1)}, u32[]{:S(2)}, u32[]{:S(2)}) collective-permute-start(bf16[2,90,256]{2,1,0:T(8,128)(2,1)} %get-tuple-element.44), channel_id=1, source_target_pairs={{0,127},{1,2},{2,1},{3,4},{4,3},{5,6},{6,5},{7,8},{8,7},{9,10},{10... | collective-permute-start | bytes 276488 | tf_op jit(solution)/shard_map/ppermute | solution.py:447
  48.7 0.0 all-to-all-done.1
  48.8 0.0 copy-start.1
  48.8 0.8 copy-done.1
  49.6 8.2 %network.1 = (bf16[512,2048]{1,0:T(8,128)(2,1)S(1)}, bf16[2048,512]{1,0:T(8,128)(2,1)S(1)}, bf16[2560,2048]{1,0:T(8,128)(2,1)S(1)}, f32[90,2048]{1,0:T(8,128)S(1...) custom-call(bf16[1024,256]{1,0:T(8,128)(2,1)} %bitcast.5, s32[1,512]{1,0:T(1,128)} %get-tuple-element.46.refs_1_, ...), custom_call_target="tpu_custom_call" | custom-call | flops 5000000000 | bytes 35981312 | tf_op jit(solution)/shard_map/network/pallas_call | solution.py:123
  57.7 0.0 collective-permute-done.refs_0_
  57.8 0.0 collective-permute-done.1.refs_1_
  57.8 3.3 %second.1 = (f32[90,2048]{1,0:T(8,128)S(1)}, f32[90,2048]{1,0:T(8,128)S(1)}, f32[90,2048]{1,0:T(8,128)S(1)}, bf16[2,90,256]{2,1,0:T(8,128)(2,1)S(1)}, bf16[2,90,256]{2,1,0:T(8,128)(2,1)S(1)}) custom-call(bf16[2,90,256]{2,1,0:T(8,128)(2,1)S(1)} %collective-permute-done.refs_0_, bf16[2,90,256]{2,1,0:T(8,128)(2,1)S(1)} %collective-permute-done.1.refs_1_, ...), custom_call_target="tpu_custom_call" | custom-call | flops 1000000000 | bytes 17006592 | tf_op jit(solution)/shard_map/second/pallas_call | solution.py:123
  61.1 0.1 collective-permute-start.2
  61.2 0.7 collective-permute-start.3
  61.9 4.0 %between.1 = (f32[90,2048]{1,0:T(8,128)S(1)}, f32[90,2048]{1,0:T(8,128)S(1)}) custom-call(f32[90,2048]{1,0:T(8,128)S(1)} %get-tuple-element.57.refs_0_, f32[90,2048]{1,0:T(8,128)S(1)} %get-tuple-element.58.refs_1_, f32[90,2048]{1,0:T(8,128)S(1)} %get-tuple-element.59.refs_2_, bf16[2560,2048]{1,0:T(8,128)(2,1)S(1)} %get-tuple-element.53.refs_5_.refs_3_.refs_4_), custom_call_target="tpu_custom_call" | custom-call | flops 1000000000 | bytes 14172160 | tf_op jit(solution)/shard_map/between/pallas_call | solution.py:123
  65.9 0.0 collective-permute-done.2.refs_0_
  65.9 4.8 %collective-permute-done.3.refs_1_ = bf16[2,90,256]{2,1,0:T(8,128)(2,1)S(1)} collective-permute-done((bf16[2,90,256]{2,1,0:T(8,128)(2,1)S(1)}, bf16[2,90,256]{2,1,0:T(8,128)(2,1)S(1)}, u32[]{:S(2)}, u32[]{:S(2)}) %collective-permute-start.3) | collective-permute-done | bytes 92192 | tf_op jit(solution)/shard_map/ppermute | solution.py:447
  70.7 2.1 %third.1 = (f32[90,2048]{1,0:T(8,128)S(1)}, bf16[90,2048]{1,0:T(8,128)(2,1)S(1)}, f32[90,2048]{1,0:T(8,128)S(1)}, bf16[2,90,256]{2,1,0:T(8,128)(2,1)S(1)}, bf16[2,90,256]{2,1,0:T(8,128)(2,1)S(1)}) custom-call(bf16[2,90,256]{2,1,0:T(8,128)(2,1)S(1)} %collective-permute-done.2.refs_0_, bf16[2,90,256]{2,1,0:T(8,128)(2,1)S(1)} %collective-permute-done.3.refs_1_, ...), custom_call_target="tpu_custom_call" | custom-call | flops 1000000000 | bytes 17006592 | tf_op jit(solution)/shard_map/third/pallas_call | solution.py:123
  72.8 0.1 collective-permute-start.4
  72.9 2.0 %collective-permute-start.5 = (bf16[2,90,256]{2,1,0:T(8,128)(2,1)S(1)}, bf16[2,90,256]{2,1,0:T(8,128)(2,1)S(1)}, u32[]{:S(2)}, u32[]{:S(2)}) collective-permute-start(bf16[2,90,256]{2,1,0:T(8,128)(2,1)S(1)} %get-tuple-element.64), channel_id=1, source_target_pairs={{0,127},{1,2},{2,1},{3,4},{4,3},{5,6},{6,5},{7,8},{8,7},{9,10},{10... | collective-permute-start | bytes 276488 | tf_op jit(solution)/shard_map/ppermute | solution.py:447
  74.9 8.2 %window.1 = (bf16[540,2048]{1,0:T(8,128)(2,1)}, f32[96,2048]{1,0:T(8,128)S(1)}, f32[90,2048]{1,0:T(8,128)S(1)}, f32[90,2048]{1,0:T(8,128)S(1)}) custom-call(f32[90,2048]{1,0:T(8,128)S(1)} %get-tuple-element.65.refs_0_, f32[90,2048]{1,0:T(8,128)S(1)} %get-tuple-element.66.refs_1_, f32[90,2048]{1,0:T(8,128)S(1)} %get-tuple-element.59.refs_2_, ...), custom_call_target="tpu_custom_call" | custom-call | flops 3000000000 | bytes 21793792 | tf_op jit(solution)/shard_map/window/pallas_call | solution.py:123
  83.1 0.0 collective-permute-done.4.refs_0_
  83.1 0.0 collective-permute-done.5.refs_1_
  83.1 1.9 %finish.1 = (bf16[540,2048]{1,0:T(8,128)(2,1)}, f32[90,2048]{1,0:T(8,128)}) custom-call(bf16[2,90,256]{2,1,0:T(8,128)(2,1)S(1)} %collective-permute-done.4.refs_0_, bf16[2,90,256]{2,1,0:T(8,128)(2,1)S(1)} %collective-permute-done.5.refs_1_, bf16[2048,512]{1,0:T(8,128)(2,1)S(1)} %get-tuple-element.51.refs_2_, ...), custom_call_target="tpu_custom_call", output_to_operand_aliasing={{0}: (7, {})} | custom-call | flops 1000000000 | bytes 20189184 | tf_op jit(solution)/shard_map/finish/pallas_call | solution.py:123
Async XLA Ops:
  0.6 0.7 copy-start
  2.5 20.7 %all-to-all-start = ((f32[128,1,128]{2,1,0:T(1,128)}), f32[128,1,128]{2,1,0:T(1,128)S(1)}, u32[]{:S(2)}, u32[]{:S(2)}) async-start(f32[128,1,128]{2,1,0:T(1,128)} %get-tuple-element.39), calls=%async_computation | async-start | bytes 131072 | tf_op jit(solution)/shard_map/all_to_all | solution.py:457
  26.5 22.3 %all-to-all-start.1 = ((bf16[128,8,256]{2,1,0:T(8,128)(2,1)}), bf16[128,8,256]{2,1,0:T(8,128)(2,1)S(1)}, u32[]{:S(2)}, u32[]{:S(2)}) async-start(bf16[128,8,256]{2,1,0:T(8,128)(2,1)} %bitcast.6), calls=%async_computation.1 | async-start | bytes 1048576 | tf_op jit(solution)/shard_map/all_to_all | solution.py:487
  41.3 16.5 %collective-permute-start = (bf16[2,90,256]{2,1,0:T(8,128)(2,1)}, bf16[2,90,256]{2,1,0:T(8,128)(2,1)S(1)}, u32[]{:S(2)}, u32[]{:S(2)}) collective-permute-start(bf16[2,90,256]{2,1,0:T(8,128)(2,1)} %get-tuple-element.43), channel_id=1, source_target_pairs={{0,1},{1,0},{2,3},{3,2},{4,5},{5,4},{6,7},{7,6},{8,9},{9,8},{10,11... | collective-permute-start | bytes 276488 | tf_op jit(solution)/shard_map/ppermute | solution.py:448
  41.3 16.4 %collective-permute-start.1 = (bf16[2,90,256]{2,1,0:T(8,128)(2,1)}, bf16[2,90,256]{2,1,0:T(8,128)(2,1)S(1)}, u32[]{:S(2)}, u32[]{:S(2)}) collective-permute-start(bf16[2,90,256]{2,1,0:T(8,128)(2,1)} %get-tuple-element.44), channel_id=1, source_target_pairs={{0,127},{1,2},{2,1},{3,4},{4,3},{5,6},{6,5},{7,8},{8,7},{9,10},{10... | collective-permute-start | bytes 276488 | tf_op jit(solution)/shard_map/ppermute | solution.py:447
  48.8 0.8 copy-start.1
  61.1 4.8 %collective-permute-start.2 = (bf16[2,90,256]{2,1,0:T(8,128)(2,1)S(1)}, bf16[2,90,256]{2,1,0:T(8,128)(2,1)S(1)}, u32[]{:S(2)}, u32[]{:S(2)}) collective-permute-start(bf16[2,90,256]{2,1,0:T(8,128)(2,1)S(1)} %get-tuple-element.55), channel_id=1, source_target_pairs={{0,1},{1,0},{2,3},{3,2},{4,5},{5,4},{6,7},{7,6},{8,9},{9,8},{10,11... | collective-permute-start | bytes 276488 | tf_op jit(solution)/shard_map/ppermute | solution.py:448
  61.2 9.6 %collective-permute-start.3 = (bf16[2,90,256]{2,1,0:T(8,128)(2,1)S(1)}, bf16[2,90,256]{2,1,0:T(8,128)(2,1)S(1)}, u32[]{:S(2)}, u32[]{:S(2)}) collective-permute-start(bf16[2,90,256]{2,1,0:T(8,128)(2,1)S(1)} %get-tuple-element.56), channel_id=1, source_target_pairs={{0,127},{1,2},{2,1},{3,4},{4,3},{5,6},{6,5},{7,8},{8,7},{9,10},{10... | collective-permute-start | bytes 276488 | tf_op jit(solution)/shard_map/ppermute | solution.py:447
  72.8 10.3 %collective-permute-start.4 = (bf16[2,90,256]{2,1,0:T(8,128)(2,1)S(1)}, bf16[2,90,256]{2,1,0:T(8,128)(2,1)S(1)}, u32[]{:S(2)}, u32[]{:S(2)}) collective-permute-start(bf16[2,90,256]{2,1,0:T(8,128)(2,1)S(1)} %get-tuple-element.63), channel_id=1, source_target_pairs={{0,1},{1,0},{2,3},{3,2},{4,5},{5,4},{6,7},{7,6},{8,9},{9,8},{10,11... | collective-permute-start | bytes 276488 | tf_op jit(solution)/shard_map/ppermute | solution.py:448
  72.9 10.2 %collective-permute-start.5 = (bf16[2,90,256]{2,1,0:T(8,128)(2,1)S(1)}, bf16[2,90,256]{2,1,0:T(8,128)(2,1)S(1)}, u32[]{:S(2)}, u32[]{:S(2)}) collective-permute-start(bf16[2,90,256]{2,1,0:T(8,128)(2,1)S(1)} %get-tuple-element.64), channel_id=1, source_target_pairs={{0,127},{1,2},{2,1},{3,4},{4,3},{5,6},{6,5},{7,8},{8,7},{9,10},{10... | collective-permute-start | bytes 276488 | tf_op jit(solution)/shard_map/ppermute | solution.py:447

commit v4 on v3

--- a/solution.py
+++ b/solution.py
@@ -155,6 +155,24 @@
     return jnp.where(place == here, jnp.ones((), bf16), jnp.zeros((), bf16))
 
 
+def make_groups(order_ref, groups_ref):
+    group = order_ref[...] >> 2
+    for c in range(8):
+        sl = slice(c * 256, (c + 1) * 256)
+        for b in range(2):
+            groups_ref[b * 256 : (b + 1) * 256, sl] = pick_rows(group[:, sl], b, 256)
+
+
+def make_border(lists_ref, border_ref):
+    even = (lax.axis_index("cells") & 1) == 0
+    near = jnp.where(even, lists_ref[1:2, :], lists_ref[0:1, :])
+    far = jnp.where(even, lists_ref[0:1, :], lists_ref[1:2, :])
+    for b in range(8):
+        sl = slice(b * 256, (b + 1) * 256)
+        border_ref[sl, :HALO] = pick_rows(near, b, 256)
+        border_ref[sl, HALO:] = pick_rows(far, b, 256)
+
+
 def to_column(row):
     return jnp.broadcast_to(row, (128, row.shape[1])).T[:, :1]
 
@@ -182,48 +200,61 @@
 
 
 def prepare_kernel(
-    order_ref, state_ref, w_in_ref, traj_ref, bias_ref, rank_ref, count_ref,
-    groups_ref, drive_ref, u_ref, number_ref,
+    order_ref, state_ref, w_in_ref, traj_ref, bias_ref, rank_ref, count_ref, drive_ref, u_ref, groups
 ):
     me = lax.axis_index("cells")
-    group = order_ref()[...] >> 2
-    for c in range(8):
-        sl = slice(c * 256, (c + 1) * 256)
-        for b in range(2):
-            groups_ref.ref[b * 256 : (b + 1) * 256, sl] = pick_rows(group[:, sl], b, 256)
-    groups_ref.put()
     z = dot(traj_ref()[...], w_in_ref()[...], TN) + bias_ref()[0:1, :]
     decay = jnp.exp(-2.0 * jnp.minimum(jnp.abs(z), 30.0))
-    u_ref.ref[...] = jnp.where(z < 0.0, -decay, decay).astype(bf16)
-    u_ref.put()
     mine = jnp.where(lane_iota(1, DEVS) == me, count_ref()[...], 0).astype(f32)
     daylit = rank_ref()[...].astype(f32) < jnp.sum(mine, axis=1, keepdims=True)
-    number_ref.ref[...] = jnp.where(daylit, lane_iota(1, COLS) + 1, -1).astype(f32)
-    number_ref.put()
-    mean = (0.25 * dot(state_ref()[...], groups_ref.ref[...], NT)).astype(bf16)
+    daylit = to_column(jnp.where(daylit, 1.0, 0.0)) > 0.5
+    u = jnp.where(z < 0.0, -decay, decay)
+    u_ref.ref[...] = jnp.where(daylit, u, 0.0).astype(bf16)
+    u_ref.put()
+    make_groups(order_ref(), groups)
+    mean = (0.25 * dot(state_ref()[...], groups[...], NT)).astype(bf16)
     drive_ref.ref[...] = dot(w_in_ref.ref[...], mean, TN)
     drive_ref.put()
 
 
-def answer_kernel(request_ref, u_ref, number_ref, answer_ref, token_ref, left_ref, right_ref):
+def answer_kernel(
+    request_ref, u_ref, answer_ref, token_ref, left_ref, right_ref, whole_ref, sems
+):
     request = request_ref[...].reshape(DEVS, 128)
-    number = number_ref()[...]
-    token_ref.ref[...] = number[:, :128]
+    token_ref.ref[...] = request[:1, :]
     token_ref.put()
-    chosen = [onehot(request[:, k : k + 1] == number) for k in range(CAP)]
-    rows = dot(jnp.concatenate(chosen, axis=0), u_ref()[...], NN)
-    for k in range(CAP):
-        block = slice(k * DEVS, (k + 1) * DEVS)
-        left_ref[pl.ds(k, DEVS, stride=CAP), :] = rows[block, :128]
-        right_ref[pl.ds(k, DEVS, stride=CAP), :] = rows[block, 128:]
-    answer_ref.ref[:, :128] = left_ref[...].astype(bf16)
-    answer_ref.ref[:, 128:] = right_ref[...].astype(bf16)
-    answer_ref.put()
+    number = (lane_iota(1, COLS) + 1).astype(f32)
+    half = DEVS // 2
+    chosen = [
+        jnp.concatenate(
+            [onehot(request[h * half : (h + 1) * half, k : k + 1] == number) for k in range(CAP)],
+            axis=0,
+        )
+        for h in range(2)
+    ]
+    u = u_ref()[...]
+    copies = []
+    for h in range(2):
+        rows = dot(chosen[h], u, NN)
+        for k in range(CAP):
+            block = slice(k * half, (k + 1) * half)
+            place = pl.ds(h * half * CAP + k, half, stride=CAP)
+            left_ref[place, :] = rows[block, :128]
+            right_ref[place, :] = rows[block, 128:]
+        part = slice(h * half * CAP, (h + 1) * half * CAP)
+        whole_ref[part, :128] = left_ref[part, :].astype(bf16)
+        whole_ref[part, 128:] = right_ref[part, :].astype(bf16)
+        window = pl.ds(h * half * CAP, half * CAP)
+        copy = pltpu.make_async_copy(whole_ref.at[window], answer_ref.at[window], sems.at[h])
+        copy.start()
+        copies.append(copy)
+    for copy in copies:
+        copy.wait()
 
 
 def build_kernel(
     slots_ref, lists_ref, forcing_ref, state_ref, token_ref,
-    links_ref, border_ref, part_ref, first_ref, second_ref, links, sems,
+    links_ref, part_ref, first_ref, second_ref, links, border_ref, sems,
 ):
     even = (lax.axis_index("cells") & 1) == 0
     slots = slots_ref()[...]
@@ -234,9 +265,6 @@
     for k in range(6):
         times = times + jnp.where(slots == slots[k : k + 1, :], 1.0, 0.0)
     times = times.astype(bf16)
-    lists = lists_ref()
-    near = jnp.where(even, lists[1:2, :], lists[0:1, :])
-    far = jnp.where(even, lists[0:1, :], lists[1:2, :])
     forcing = forcing_ref()
 
     def fill(jb):
@@ -265,13 +293,9 @@
             sl = slice(jb * 256, (jb + 1) * 256)
             part_ref.ref[:, sl] = KEEP * forcing[:, sl].astype(f32) + share(jb)
 
-    for b in range(8):
-        sl = slice(b * 256, (b + 1) * 256)
-        border_ref.ref[sl, :HALO] = pick_rows(near, b, 256)
-        border_ref.ref[sl, HALO:] = pick_rows(far, b, 256)
-    border_ref.put()
+    make_border(lists_ref(), border_ref)
     state = state_ref()
-    border = dot(state[:LEV, :], border_ref.ref[...], NN)
+    border = dot(state[:LEV, :], border_ref[...], NN)
     first_ref.ref[1] = border[:, :HALO].astype(bf16)
     second_ref.ref[1] = border[:, HALO:].astype(bf16)
     order = (8, 9, *range(8))
@@ -312,26 +336,29 @@
 
 
 def network_kernel(
-    answer_ref, slot_ref, drive_ref, w_hidden_ref, w_out_ref, bias_ref, state_ref,
-    groups_far, border_far, links_far,
-    groups, border, links, heat_ref, slope_ref, ahead_ref,
+    answer_ref, slot_ref, drive_ref, w_hidden_ref, w_out_ref, bias_ref, order_ref, lists_ref,
+    state_ref, links_far, part_far, forcing_far,
+    groups, border, links, heat_ref, slope_ref, ahead_ref, part_ref, forcing_ref,
     sems,
 ):
-    groups_copy = pltpu.make_async_copy(groups_far, groups, sems.at[5])
-    border_copy = pltpu.make_async_copy(border_far, border, sems.at[6])
-
     def piece(i):
         rows = pl.ds(i * PIECE, PIECE)
         return pltpu.make_async_copy(links_far.at[rows], links.at[rows], sems.at[i])
 
-    groups_copy.start()
+    later = [
+        pltpu.make_async_copy(part_far, part_ref, sems.at[OWN + 1]),
+        pltpu.make_async_copy(forcing_far, forcing_ref, sems.at[OWN + 2]),
+    ]
     for i in range(OWN + 1):
         piece(i).start()
-    border_copy.start()
-
+    for copy in later:
+        copy.start()
+
+    make_groups(order_ref(), groups)
+    make_border(lists_ref(), border)
     slots = slot_ref()[...]
     chosen = jnp.concatenate([pick_rows(slots, b, COLS) for b in range(SLOTS // 256)], axis=0)
-    u = dot(answer_ref()[...], chosen, TN)
+    u = dot(answer_ref[...], chosen, TN)
     size = jnp.abs(u)
     inverse = 1.0 / (1.0 + size)
     act = jnp.where(u < 0.0, size - 1.0, 1.0 - size) * inverse
@@ -347,26 +374,29 @@
         slope_ref[layer + 1] = slope
         tangent = (slope * dot(weight, tangent, TN)).astype(bf16)
     heating = dot(w_out_ref()[...], tangent, NN).astype(bf16)
-    groups_copy.wait()
     heat_ref[...] = dot(heating, groups[...], NN)
+    state = state_ref()
+    ahead_ref[...] = KEEP * state[:LEV, :].astype(f32) + heat_ref[...]
     for i in range(OWN):
         piece(i).wait()
-    inner(state_ref(), heat_ref, links, ahead_ref)
+        sl = slice(i * PIECE, (i + 1) * PIECE)
+        ahead_ref[...] += SPREAD * dot(state[:LEV, sl], links[sl, :], NN)
     piece(OWN).wait()
-    border_copy.wait()
+    for copy in later:
+        copy.wait()
 
 
 def second_kernel(
     first_in, second_in, border, part_in, forcing_ref, links, ahead_ref,
     adjoint_ref, heat_back_ref, temp_ref, first_ref, second_ref,
 ):
-    adjoint = part_in()[...] + received(first_in[0], second_in[0], border)
+    adjoint = part_in[...] + received(first_in[0], second_in[0], border)
     adjoint_ref[...] = adjoint
     push(adjoint.astype(bf16), links, first_ref, second_ref)
     temp = outer(ahead_ref, first_in[1], second_in[1], links)
     temp_ref[...] = temp
     send_border(temp, border, first_ref, second_ref)
-    heat_back_ref[...] = forcing_ref()[...].astype(f32) + adjoint
+    heat_back_ref[...] = forcing_ref[...].astype(f32) + adjoint
 
 
 def inner(temp_ref, heat_ref, links, part_ref):
@@ -407,6 +437,7 @@
     adjoint_ref, temp_ref, heat_ref, links, slope_ref, back_ref, groups, w_out_ref, w_hidden_ref,
     w_in_ref, sens_far, top_ref, part_ref, ahead_ref, low_ref, sem,
 ):
+    inner(temp_ref, heat_ref, links, ahead_ref)
     inputs = dot(back_ref[...], groups[...], NT).astype(bf16)
     weights = w_hidden_ref()
     back = (slope_ref[2] * dot(w_out_ref()[...], inputs, TN)).astype(bf16)
@@ -417,7 +448,6 @@
     copy = pltpu.make_async_copy(low_ref, sens_far.at[pl.ds(TOP, FEAT - TOP)], sem)
     copy.start()
     top_ref[...] = dot(sens[:TOP], groups[...], NN)
-    inner(temp_ref, heat_ref, links, ahead_ref)
     pull(adjoint_ref, links, part_ref)
     copy.wait()
 
@@ -462,54 +492,60 @@
     all_groups = shape((COLS, CELLS), bf16)
     state_rows = (state_deviation, TOP, TOP)
 
-    groups, drive, u, number = kernel(
+    drive, u = kernel(
         prepare_kernel,
         "prepare",
         [
             whole(fine_order), whole(state_deviation), whole(w_in), whole(trajectory), whole(biases),
             whole(sun_rank), whole(daylit_counts.reshape(1, DEVS)),
         ],
-        [
-            (all_groups, True),
-            (shape((HID, COLS), f32), True),
-            (shape((COLS, HID), bf16), True),
-            (shape((1, COLS), f32), True),
-        ],
+        [(shape((HID, COLS), f32), True), (shape((COLS, HID), bf16), True)],
+        scratch=[pltpu.VMEM((COLS, CELLS), bf16)],
         flops=2 * 10**9,
     )
     answer, token = kernel(
         answer_kernel,
         "answer",
-        [asked, whole(u), whole(number)],
-        [(shape((SLOTS, HID), bf16), True), (shape((1, 128), f32), True)],
-        scratch=[pltpu.VMEM((SLOTS, 128), f32)] * 2,
+        [asked, whole(u)],
+        [(shape((SLOTS, HID), bf16), "raw"), (shape((1, 128), f32), True)],
+        scratch=[
+            pltpu.VMEM((SLOTS, 128), f32),
+            pltpu.VMEM((SLOTS, 128), f32),
+            pltpu.VMEM((SLOTS, HID), bf16),
+            pltpu.SemaphoreType.DMA((2,)),
+        ],
     )
     got = lax.all_to_all(answer.reshape(DEVS, CAP, HID), "cells", 0, 0, tiled=True)
     got = got.reshape(SLOTS, HID)
-    links, border, part, first, second = kernel(
+    links, part, first, second = kernel(
         build_kernel,
         "build",
         [
             whole(adjacent_source_slots), whole(outgoing_local_lists[0]), whole(forcing), state_rows,
             ("raw", token),
         ],
-        [(all_links, "raw"), (all_border, True), (field, True), (side, True), (side, True)],
-        scratch=[pltpu.VMEM((EXT, CELLS), bf16), pltpu.SemaphoreType.DMA((10,))],
+        [(all_links, "raw"), (field, True), (side, True), (side, True)],
+        scratch=[
+            pltpu.VMEM((EXT, CELLS), bf16),
+            pltpu.VMEM((CELLS, 2 * HALO), bf16),
+            pltpu.SemaphoreType.DMA((10,)),
+        ],
         flops=3 * 10**9,
     )
     first, second = swap(first, second)
 
     near = (field, False)
-    groups, border, links, heat, slope, ahead = kernel(
+    groups, border, links, heat, slope, ahead, part, late_forcing = kernel(
         network_kernel,
         "network",
         [
-            whole(got), whole(slot), whole(drive), whole(w_hidden), whole(w_out.T), whole(biases),
-            state_rows, ("raw", groups), ("raw", border), ("raw", links),
+            got, whole(slot), whole(drive), whole(w_hidden), whole(w_out.T), whole(biases),
+            whole(fine_order), whole(outgoing_local_lists[0]), state_rows,
+            ("raw", links), ("raw", part), ("raw", forcing),
         ],
         [
             (all_groups, False), (all_border, False), (all_links, False), near,
-            (shape((3, HID, COLS), f32), False), near,
+            (shape((3, HID, COLS), f32), False), near, near, (shape((LEV, CELLS), bf16), False),
         ],
         scratch=[pltpu.SemaphoreType.DMA((7,))],
         limit=32,
@@ -518,7 +554,7 @@
     adjoint, heat_back, temp, first, second = kernel(
         second_kernel,
         "second",
-        [first, second, border, whole(part), whole(forcing), links, ahead],
+        [first, second, border, part, late_forcing, links, ahead],
         [near, near, near, (side, False), (side, False)],
         limit=32,
     )

time: 85.5 us -> 84.3 us (0.986)
  transfers between devices with their start and end apart: 8 -> 8, of which waited for: 2 -> 2; matrix products, arithmetic and copies ran while one was open for 0% -> 0% of each run, Pallas kernels for 41% -> 42%
where the time goes in v4:
time: 84.3 us; the launch traced here: 84 us
  Pallas kernels  46.2 us (55%)
  starting transfers between devices  27.8 us (33%)
  waiting for transfers between devices  8.4 us (10%)
  between operations  0.95 us (1%)
    pallas_call x10, Pallas kernels, kernel(): pl.pallas_call(wrapped, out_shape=tuple(out_shapes), in_specs=in_specs, o...  46.2 us
    all_to_all x1, starting transfers between devices, local(): asked = lax.all_to_all(request, 'cells', 0, 0, tiled=True)  11.1 us
    ppermute x3, starting transfers between devices, swap(): second = lax.ppermute(second, 'cells', far_pairs)  10.4 us
    all_to_all x1, starting transfers between devices, local(): lax.all_to_all(answer.reshape(DEVS, CAP, HID), 'cells', 0, 0, tiled=True)  5.94 us
    ppermute x3, waiting for transfers between devices, swap(): second = lax.ppermute(second, 'cells', far_pairs)  4.56 us
    all_to_all x1, waiting for transfers between devices, local(): asked = lax.all_to_all(request, 'cells', 0, 0, tiled=True)  3.83 us
  transfers between devices with their start and end apart: 8, of which 2 were waited for; matrix products, arithmetic and copies ran while one was open for 0% of the time, Pallas kernels for 42%

profile of v4, /device:TPU:0, one launch (start us, length us, event | category | flops | bytes accessed | tf_op | source)
XLA Modules:
  0.0 84.0 jit_solution(4103819626892707118)
XLA Ops:
  0.6 0.0 copy-start
  0.6 0.7 copy-done
  1.3 1.2 %route.1 = (f32[128,1,128]{2,1,0:T(1,128)}, s32[1,512]{1,0:T(1,128)}) custom-call(s32[1,512]{1,0:T(1,128)S(1)} %copy-done), custom_call_target="tpu_custom_call" | custom-call | flops 10000000 | bytes 69632 | tf_op jit(solution)/shard_map/route/pallas_call | solution.py:123
  2.5 11.1 %all-to-all-start = ((f32[128,1,128]{2,1,0:T(1,128)}), f32[128,1,128]{2,1,0:T(1,128)S(1)}, u32[]{:S(2)}, u32[]{:S(2)}) async-start(f32[128,1,128]{2,1,0:T(1,128)} %get-tuple-element.38), calls=%async_computation | async-start | bytes 131072 | tf_op jit(solution)/shard_map/all_to_all | solution.py:487
  13.7 5.7 %prepare.1 = (f32[256,512]{1,0:T(8,128)}, bf16[512,256]{1,0:T(8,128)(2,1)}) custom-call(s32[1,2048]{1,0:T(1,128)} %refs_6_.1, bf16[540,2048]{1,0:T(8,128)(2,1)} %refs_8_.2, bf16[540,256]{1,0:T(8,128)(2,1)} %refs_9_.1, bf16[540,512]{1,0:T(8,128)(2,1)} %refs_3_.3, f32[3,256]{1,0:T(4,128)} %refs_5_.3, s32[1,512]{1,0:T(1,128)} %refs_5_.2, s32[1,128]{1,0:T(1,128)} %bitcast.11), custom_call_target="tpu_custom_call" | custom-call | flops 2000000000 | bytes 3841536 | tf_op jit(solution)/shard_map/prepare/pallas_call | solution.py:123
  19.3 3.8 %all-to-all-done.refs_0_ = f32[128,1,128]{2,1,0:T(1,128)S(1)} async-done(((f32[128,1,128]{2,1,0:T(1,128)}), f32[128,1,128]{2,1,0:T(1,128)S(1)}, u32[]{:S(2)}, u32[]{:S(2)}) %all-to-all-start) | async-done | bytes 65568 | tf_op jit(solution)/shard_map/all_to_all | solution.py:487
  23.2 3.5 %answer.1 = (bf16[1024,256]{1,0:T(8,128)(2,1)}, f32[1,128]{1,0:T(1,128)}) custom-call(f32[128,1,128]{2,1,0:T(1,128)S(1)} %all-to-all-done.refs_0_, bf16[512,256]{1,0:T(8,128)(2,1)} %get-tuple-element.39.refs_1_), custom_call_target="tpu_custom_call" | custom-call | flops 1000000000 | bytes 852480 | tf_op jit(solution)/shard_map/answer/pallas_call | solution.py:123
  26.7 5.9 %all-to-all-start.1 = ((bf16[128,8,256]{2,1,0:T(8,128)(2,1)}), bf16[128,8,256]{2,1,0:T(8,128)(2,1)S(1)}, u32[]{:S(2)}, u32[]{:S(2)}) async-start(bf16[128,8,256]{2,1,0:T(8,128)(2,1)} %bitcast.6), calls=%async_computation.1 | async-start | bytes 1048576 | tf_op jit(solution)/shard_map/all_to_all | solution.py:518
  32.6 9.1 %build.1 = (bf16[2560,2048]{1,0:T(8,128)(2,1)}, f32[90,2048]{1,0:T(8,128)}, bf16[2,90,256]{2,1,0:T(8,128)(2,1)}, bf16[2,90,256]{2,1,0:T(8,128)(2,1)}) custom-call(s32[6,2048]{1,0:T(8,128)} %refs_0_.5, s32[2,256]{1,0:T(2,128)} %bitcast.9, bf16[90,2048]{1,0:T(8,128)(2,1)} %refs_11_.1, bf16[540,2048]{1,0:T(8,128)(2,1)} %refs_8_.2, ...), custom_call_target="tpu_custom_call" | custom-call | flops 3000000000 | bytes 14039552 | tf_op jit(solution)/shard_map/build/pallas_call | solution.py:123
  41.7 0.1 collective-permute-start
  41.8 7.4 %collective-permute-start.1 = (bf16[2,90,256]{2,1,0:T(8,128)(2,1)}, bf16[2,90,256]{2,1,0:T(8,128)(2,1)S(1)}, u32[]{:S(2)}, u32[]{:S(2)}) collective-permute-start(bf16[2,90,256]{2,1,0:T(8,128)(2,1)} %get-tuple-element.42), channel_id=1, source_target_pairs={{0,127},{1,2},{2,1},{3,4},{4,3},{5,6},{6,5},{7,8},{8,7},{9,10},{10... | collective-permute-start | bytes 276488 | tf_op jit(solution)/shard_map/ppermute | solution.py:477
  49.2 0.0 all-to-all-done.1
  49.2 8.7 %network.1 = (bf16[512,2048]{1,0:T(8,128)(2,1)S(1)}, bf16[2048,512]{1,0:T(8,128)(2,1)S(1)}, bf16[2560,2048]{1,0:T(8,128)(2,1)S(1)}, f32[90,2048]{1,0:T(8,128)S(1...) custom-call(bf16[1024,256]{1,0:T(8,128)(2,1)S(1)} %bitcast.5, ...), custom_call_target="tpu_custom_call" | custom-call | flops 5000000000 | bytes 34009088 | tf_op jit(solution)/shard_map/network/pallas_call | solution.py:123
  58.0 0.0 collective-permute-done.refs_0_
  58.0 0.0 collective-permute-done.1.refs_1_
  58.0 2.1 %second.1 = (f32[90,2048]{1,0:T(8,128)S(1)}, f32[90,2048]{1,0:T(8,128)S(1)}, f32[90,2048]{1,0:T(8,128)S(1)}, bf16[2,90,256]{2,1,0:T(8,128)(2,1)S(1)}, bf16[2,90,256]{2,1,0:T(8,128)(2,1)S(1)}) custom-call(bf16[2,90,256]{2,1,0:T(8,128)(2,1)S(1)} %collective-permute-done.refs_0_, bf16[2,90,256]{2,1,0:T(8,128)(2,1)S(1)} %collective-permute-done.1.refs_1_, ...), custom_call_target="tpu_custom_call" | custom-call | flops 1000000000 | bytes 17006592 | tf_op jit(solution)/shard_map/second/pallas_call | solution.py:123
  60.1 0.1 collective-permute-start.2
  60.2 1.0 %collective-permute-start.3 = (bf16[2,90,256]{2,1,0:T(8,128)(2,1)S(1)}, bf16[2,90,256]{2,1,0:T(8,128)(2,1)S(1)}, u32[]{:S(2)}, u32[]{:S(2)}) collective-permute-start(bf16[2,90,256]{2,1,0:T(8,128)(2,1)S(1)} %get-tuple-element.54), channel_id=1, source_target_pairs={{0,127},{1,2},{2,1},{3,4},{4,3},{5,6},{6,5},{7,8},{8,7},{9,10},{10... | collective-permute-start | bytes 276488 | tf_op jit(solution)/shard_map/ppermute | solution.py:477
  61.2 4.0 %between.1 = (f32[90,2048]{1,0:T(8,128)S(1)}, f32[90,2048]{1,0:T(8,128)S(1)}) custom-call(f32[90,2048]{1,0:T(8,128)S(1)} %get-tuple-element.55.refs_0_, f32[90,2048]{1,0:T(8,128)S(1)} %get-tuple-element.56.refs_1_, f32[90,2048]{1,0:T(8,128)S(1)} %get-tuple-element.57.refs_2_, bf16[2560,2048]{1,0:T(8,128)(2,1)S(1)} %get-tuple-element.51.refs_5_.refs_3_.refs_4_), custom_call_target="tpu_custom_call" | custom-call | flops 1000000000 | bytes 14172160 | tf_op jit(solution)/shard_map/between/pallas_call | solution.py:123
  65.2 0.0 collective-permute-done.2.refs_0_
  65.2 4.6 %collective-permute-done.3.refs_1_ = bf16[2,90,256]{2,1,0:T(8,128)(2,1)S(1)} collective-permute-done((bf16[2,90,256]{2,1,0:T(8,128)(2,1)S(1)}, bf16[2,90,256]{2,1,0:T(8,128)(2,1)S(1)}, u32[]{:S(2)}, u32[]{:S(2)}) %collective-permute-start.3) | collective-permute-done | bytes 92192 | tf_op jit(solution)/shard_map/ppermute | solution.py:477
  69.7 2.1 %third.1 = (f32[90,2048]{1,0:T(8,128)S(1)}, bf16[90,2048]{1,0:T(8,128)(2,1)S(1)}, f32[90,2048]{1,0:T(8,128)S(1)}, bf16[2,90,256]{2,1,0:T(8,128)(2,1)S(1)}, bf16[2,90,256]{2,1,0:T(8,128)(2,1)S(1)}) custom-call(bf16[2,90,256]{2,1,0:T(8,128)(2,1)S(1)} %collective-permute-done.2.refs_0_, bf16[2,90,256]{2,1,0:T(8,128)(2,1)S(1)} %collective-permute-done.3.refs_1_, ...), custom_call_target="tpu_custom_call" | custom-call | flops 1000000000 | bytes 17006592 | tf_op jit(solution)/shard_map/third/pallas_call | solution.py:123
  71.8 0.1 collective-permute-start.4
  71.9 2.0 %collective-permute-start.5 = (bf16[2,90,256]{2,1,0:T(8,128)(2,1)S(1)}, bf16[2,90,256]{2,1,0:T(8,128)(2,1)S(1)}, u32[]{:S(2)}, u32[]{:S(2)}) collective-permute-start(bf16[2,90,256]{2,1,0:T(8,128)(2,1)S(1)} %get-tuple-element.62), channel_id=1, source_target_pairs={{0,127},{1,2},{2,1},{3,4},{4,3},{5,6},{6,5},{7,8},{8,7},{9,10},{10... | collective-permute-start | bytes 276488 | tf_op jit(solution)/shard_map/ppermute | solution.py:477
  73.9 8.0 %window.1 = (bf16[540,2048]{1,0:T(8,128)(2,1)}, f32[96,2048]{1,0:T(8,128)S(1)}, f32[90,2048]{1,0:T(8,128)S(1)}, f32[90,2048]{1,0:T(8,128)S(1)}) custom-call(f32[90,2048]{1,0:T(8,128)S(1)} %get-tuple-element.63.refs_0_, f32[90,2048]{1,0:T(8,128)S(1)} %get-tuple-element.64.refs_1_, f32[90,2048]{1,0:T(8,128)S(1)} %get-tuple-element.57.refs_2_, ...), custom_call_target="tpu_custom_call" | custom-call | flops 3000000000 | bytes 21793792 | tf_op jit(solution)/shard_map/window/pallas_call | solution.py:123
  81.9 0.0 collective-permute-done.4.refs_0_
  81.9 0.0 collective-permute-done.5.refs_1_
  81.9 1.9 %finish.1 = (bf16[540,2048]{1,0:T(8,128)(2,1)}, f32[90,2048]{1,0:T(8,128)}) custom-call(bf16[2,90,256]{2,1,0:T(8,128)(2,1)S(1)} %collective-permute-done.4.refs_0_, bf16[2,90,256]{2,1,0:T(8,128)(2,1)S(1)} %collective-permute-done.5.refs_1_, bf16[2048,512]{1,0:T(8,128)(2,1)S(1)} %get-tuple-element.48.refs_2_, ...), custom_call_target="tpu_custom_call", output_to_operand_aliasing={{0}: (7, {})} | custom-call | flops 1000000000 | bytes 20189184 | tf_op jit(solution)/shard_map/finish/pallas_call | solution.py:123
Async XLA Ops:
  0.6 0.7 copy-start
  2.5 20.7 %all-to-all-start = ((f32[128,1,128]{2,1,0:T(1,128)}), f32[128,1,128]{2,1,0:T(1,128)S(1)}, u32[]{:S(2)}, u32[]{:S(2)}) async-start(f32[128,1,128]{2,1,0:T(1,128)} %get-tuple-element.38), calls=%async_computation | async-start | bytes 131072 | tf_op jit(solution)/shard_map/all_to_all | solution.py:487
  26.7 22.5 %all-to-all-start.1 = ((bf16[128,8,256]{2,1,0:T(8,128)(2,1)}), bf16[128,8,256]{2,1,0:T(8,128)(2,1)S(1)}, u32[]{:S(2)}, u32[]{:S(2)}) async-start(bf16[128,8,256]{2,1,0:T(8,128)(2,1)} %bitcast.6), calls=%async_computation.1 | async-start | bytes 1048576 | tf_op jit(solution)/shard_map/all_to_all | solution.py:518
  41.7 16.3 %collective-permute-start = (bf16[2,90,256]{2,1,0:T(8,128)(2,1)}, bf16[2,90,256]{2,1,0:T(8,128)(2,1)S(1)}, u32[]{:S(2)}, u32[]{:S(2)}) collective-permute-start(bf16[2,90,256]{2,1,0:T(8,128)(2,1)} %get-tuple-element.41), channel_id=1, source_target_pairs={{0,1},{1,0},{2,3},{3,2},{4,5},{5,4},{6,7},{7,6},{8,9},{9,8},{10,11... | collective-permute-start | bytes 276488 | tf_op jit(solution)/shard_map/ppermute | solution.py:478
  41.8 16.2 %collective-permute-start.1 = (bf16[2,90,256]{2,1,0:T(8,128)(2,1)}, bf16[2,90,256]{2,1,0:T(8,128)(2,1)S(1)}, u32[]{:S(2)}, u32[]{:S(2)}) collective-permute-start(bf16[2,90,256]{2,1,0:T(8,128)(2,1)} %get-tuple-element.42), channel_id=1, source_target_pairs={{0,127},{1,2},{2,1},{3,4},{4,3},{5,6},{6,5},{7,8},{8,7},{9,10},{10... | collective-permute-start | bytes 276488 | tf_op jit(solution)/shard_map/ppermute | solution.py:477
  60.1 5.1 %collective-permute-start.2 = (bf16[2,90,256]{2,1,0:T(8,128)(2,1)S(1)}, bf16[2,90,256]{2,1,0:T(8,128)(2,1)S(1)}, u32[]{:S(2)}, u32[]{:S(2)}) collective-permute-start(bf16[2,90,256]{2,1,0:T(8,128)(2,1)S(1)} %get-tuple-element.53), channel_id=1, source_target_pairs={{0,1},{1,0},{2,3},{3,2},{4,5},{5,4},{6,7},{7,6},{8,9},{9,8},{10,11... | collective-permute-start | bytes 276488 | tf_op jit(solution)/shard_map/ppermute | solution.py:478
  60.2 9.6 %collective-permute-start.3 = (bf16[2,90,256]{2,1,0:T(8,128)(2,1)S(1)}, bf16[2,90,256]{2,1,0:T(8,128)(2,1)S(1)}, u32[]{:S(2)}, u32[]{:S(2)}) collective-permute-start(bf16[2,90,256]{2,1,0:T(8,128)(2,1)S(1)} %get-tuple-element.54), channel_id=1, source_target_pairs={{0,127},{1,2},{2,1},{3,4},{4,3},{5,6},{6,5},{7,8},{8,7},{9,10},{10... | collective-permute-start | bytes 276488 | tf_op jit(solution)/shard_map/ppermute | solution.py:477
  71.8 10.1 %collective-permute-start.4 = (bf16[2,90,256]{2,1,0:T(8,128)(2,1)S(1)}, bf16[2,90,256]{2,1,0:T(8,128)(2,1)S(1)}, u32[]{:S(2)}, u32[]{:S(2)}) collective-permute-start(bf16[2,90,256]{2,1,0:T(8,128)(2,1)S(1)} %get-tuple-element.61), channel_id=1, source_target_pairs={{0,1},{1,0},{2,3},{3,2},{4,5},{5,4},{6,7},{7,6},{8,9},{9,8},{10,11... | collective-permute-start | bytes 276488 | tf_op jit(solution)/shard_map/ppermute | solution.py:478
  71.9 10.0 %collective-permute-start.5 = (bf16[2,90,256]{2,1,0:T(8,128)(2,1)S(1)}, bf16[2,90,256]{2,1,0:T(8,128)(2,1)S(1)}, u32[]{:S(2)}, u32[]{:S(2)}) collective-permute-start(bf16[2,90,256]{2,1,0:T(8,128)(2,1)S(1)} %get-tuple-element.62), channel_id=1, source_target_pairs={{0,127},{1,2},{2,1},{3,4},{4,3},{5,6},{6,5},{7,8},{8,7},{9,10},{10... | collective-permute-start | bytes 276488 | tf_op jit(solution)/shard_map/ppermute | solution.py:477

commit v5 on v4

--- a/solution.py
+++ b/solution.py
@@ -191,11 +191,10 @@
     slot_ref.ref[...] = target * CAP + rank
     slot_ref.put()
     owners = onehot(row_iota(DEVS, COLS) == target)
-    ranked = row_iota(DEVS, COLS) == rank
-    high = jnp.where(ranked, (column >> 4).astype(f32), 0.0).astype(bf16)
-    low = jnp.where(ranked, (column & 15).astype(f32), 0.0).astype(bf16)
-    request = dot(owners, high, NT) * 16.0 + dot(owners, low, NT)
-    request_ref.ref[...] = request.reshape(DEVS, 1, 128)
+    high, low = (column >> 4).astype(f32), (column & 15).astype(f32)
+    lane = row_iota(DEVS, COLS)
+    digits = jnp.where(lane == rank, high, jnp.where(lane == rank + CAP, low, 0.0))
+    request_ref.ref[...] = dot(owners, digits.astype(bf16), NT).reshape(DEVS, 1, 128)
     request_ref.put()
 
 
@@ -217,34 +216,24 @@
     drive_ref.put()
 
 
-def answer_kernel(
-    request_ref, u_ref, answer_ref, token_ref, left_ref, right_ref, whole_ref, sems
-):
+def answer_kernel(request_ref, u_ref, answer_ref, token_ref, whole_ref, sems):
     request = request_ref[...].reshape(DEVS, 128)
     token_ref.ref[...] = request[:1, :]
     token_ref.put()
-    number = (lane_iota(1, COLS) + 1).astype(f32)
-    half = DEVS // 2
-    chosen = [
-        jnp.concatenate(
-            [onehot(request[h * half : (h + 1) * half, k : k + 1] == number) for k in range(CAP)],
-            axis=0,
-        )
-        for h in range(2)
-    ]
-    u = u_ref()[...]
-    copies = []
+    digits = request.astype(bf16)
+    number = (lane_iota(1, 128) + 1).astype(f32)
+    ones = jnp.ones((128, 128), bf16)
+    rows, copies = SLOTS // 2, []
     for h in range(2):
-        rows = dot(chosen[h], u, NN)
-        for k in range(CAP):
-            block = slice(k * half, (k + 1) * half)
-            place = pl.ds(h * half * CAP + k, half, stride=CAP)
-            left_ref[place, :] = rows[block, :128]
-            right_ref[place, :] = rows[block, 128:]
-        part = slice(h * half * CAP, (h + 1) * half * CAP)
-        whole_ref[part, :128] = left_ref[part, :].astype(bf16)
-        whole_ref[part, 128:] = right_ref[part, :].astype(bf16)
-        window = pl.ds(h * half * CAP, half * CAP)
+        row, lane = row_iota(rows, 128), lane_iota(rows, 128)
+        asker = onehot((row >> 3) + h * (DEVS // 2) == lane)
+        weight = jnp.where(lane == (row & 7), 16.0, jnp.where(lane == (row & 7) + CAP, 1.0, 0.0))
+        wanted = dot((dot(asker, digits, NN) * weight).astype(bf16), ones, NN)
+        chosen = [onehot(wanted == number + 128.0 * c) for c in range(COLS // 128)]
+        part = slice(h * rows, (h + 1) * rows)
+        u = u_ref()[...]
+        whole_ref[part, :] = dot(jnp.concatenate(chosen, axis=1), u, NN).astype(bf16)
+        window = pl.ds(h * rows, rows)
         copy = pltpu.make_async_copy(whole_ref.at[window], answer_ref.at[window], sems.at[h])
         copy.start()
         copies.append(copy)
@@ -349,6 +338,9 @@
         pltpu.make_async_copy(part_far, part_ref, sems.at[OWN + 1]),
         pltpu.make_async_copy(forcing_far, forcing_ref, sems.at[OWN + 2]),
     ]
+    small = (slot_ref, drive_ref, w_hidden_ref, w_out_ref, bias_ref, order_ref, lists_ref, state_ref)
+    for operand in small:
+        operand()
     for i in range(OWN + 1):
         piece(i).start()
     for copy in later:
@@ -509,8 +501,6 @@
         [asked, whole(u)],
         [(shape((SLOTS, HID), bf16), "raw"), (shape((1, 128), f32), True)],
         scratch=[
-            pltpu.VMEM((SLOTS, 128), f32),
-            pltpu.VMEM((SLOTS, 128), f32),
             pltpu.VMEM((SLOTS, HID), bf16),
             pltpu.SemaphoreType.DMA((2,)),
         ],

time: 84.3 us -> 82.4 us (0.977)
  starting transfers between devices: 27.8 us -> 32.6 us
  Pallas kernels: 46.2 us -> 42.3 us
  waiting for transfers between devices: 8.4 us -> 5.58 us
    ppermute x3, starting transfers between devices: 10.4 us -> 15.2 us  [swap(): second = lax.ppermute(second, 'cells', far_pairs)]
    pallas_call x10, Pallas kernels: 46.2 us -> 42.3 us  [kernel(): pl.pallas_call(wrapped, out_shape=tuple(out_shapes), in_specs=in_specs, o...]
    ppermute x3, waiting for transfers between devices: 4.56 us -> 1.74 us  [swap(): second = lax.ppermute(second, 'cells', far_pairs)]
  transfers between devices with their start and end apart: 8 -> 8, of which waited for: 2 -> 2; matrix products, arithmetic and copies ran while one was open for 0% -> 0% of each run, Pallas kernels for 42% -> 40%
where the time goes in v5:
time: 82.4 us; the launch traced here: 82.1 us
  Pallas kernels  42.3 us (51%)
  starting transfers between devices  32.6 us (40%)
  waiting for transfers between devices  5.58 us (7%)
  between operations  0.95 us (1%)
    pallas_call x10, Pallas kernels, kernel(): pl.pallas_call(wrapped, out_shape=tuple(out_shapes), in_specs=in_specs, o...  42.3 us
    ppermute x3, starting transfers between devices, swap(): second = lax.ppermute(second, 'cells', far_pairs)  15.2 us
    all_to_all x1, starting transfers between devices, local(): asked = lax.all_to_all(request, 'cells', 0, 0, tiled=True)  11.1 us
    all_to_all x1, starting transfers between devices, local(): lax.all_to_all(answer.reshape(DEVS, CAP, HID), 'cells', 0, 0, tiled=True)  5.95 us
    all_to_all x1, waiting for transfers between devices, local(): asked = lax.all_to_all(request, 'cells', 0, 0, tiled=True)  3.82 us
    ppermute x3, waiting for transfers between devices, swap(): second = lax.ppermute(second, 'cells', far_pairs)  1.74 us
  transfers between devices with their start and end apart: 8, of which 2 were waited for; matrix products, arithmetic and copies ran while one was open for 0% of the time, Pallas kernels for 40%

profile of v5, /device:TPU:0, one launch (start us, length us, event | category | flops | bytes accessed | tf_op | source)
XLA Modules:
  0.0 82.1 jit_solution(9038757491257816140)
XLA Ops:
  0.6 0.0 copy-start
  0.6 0.7 copy-done
  1.3 1.2 %route.1 = (f32[128,1,128]{2,1,0:T(1,128)}, s32[1,512]{1,0:T(1,128)}) custom-call(s32[1,512]{1,0:T(1,128)S(1)} %copy-done), custom_call_target="tpu_custom_call" | custom-call | flops 10000000 | bytes 69632 | tf_op jit(solution)/shard_map/route/pallas_call | solution.py:123
  2.5 11.1 %all-to-all-start = ((f32[128,1,128]{2,1,0:T(1,128)}), f32[128,1,128]{2,1,0:T(1,128)S(1)}, u32[]{:S(2)}, u32[]{:S(2)}) async-start(f32[128,1,128]{2,1,0:T(1,128)} %get-tuple-element.38), calls=%async_computation | async-start | bytes 131072 | tf_op jit(solution)/shard_map/all_to_all | solution.py:479
  13.6 5.7 %prepare.1 = (f32[256,512]{1,0:T(8,128)}, bf16[512,256]{1,0:T(8,128)(2,1)}) custom-call(s32[1,2048]{1,0:T(1,128)} %refs_6_.1, bf16[540,2048]{1,0:T(8,128)(2,1)} %refs_8_.2, bf16[540,256]{1,0:T(8,128)(2,1)} %refs_9_.1, bf16[540,512]{1,0:T(8,128)(2,1)} %refs_3_.3, f32[3,256]{1,0:T(4,128)} %refs_5_.3, s32[1,512]{1,0:T(1,128)} %refs_5_.2, s32[1,128]{1,0:T(1,128)} %bitcast.11), custom_call_target="tpu_custom_call" | custom-call | flops 2000000000 | bytes 3841536 | tf_op jit(solution)/shard_map/prepare/pallas_call | solution.py:123
  19.3 3.8 %all-to-all-done.refs_0_ = f32[128,1,128]{2,1,0:T(1,128)S(1)} async-done(((f32[128,1,128]{2,1,0:T(1,128)}), f32[128,1,128]{2,1,0:T(1,128)S(1)}, u32[]{:S(2)}, u32[]{:S(2)}) %all-to-all-start) | async-done | bytes 65568 | tf_op jit(solution)/shard_map/all_to_all | solution.py:479
  23.1 2.4 %answer.1 = (bf16[1024,256]{1,0:T(8,128)(2,1)}, f32[1,128]{1,0:T(1,128)}) custom-call(f32[128,1,128]{2,1,0:T(1,128)S(1)} %all-to-all-done.refs_0_, bf16[512,256]{1,0:T(8,128)(2,1)} %get-tuple-element.39.refs_1_), custom_call_target="tpu_custom_call" | custom-call | flops 1000000000 | bytes 852480 | tf_op jit(solution)/shard_map/answer/pallas_call | solution.py:123
  25.6 6.0 %all-to-all-start.1 = ((bf16[128,8,256]{2,1,0:T(8,128)(2,1)}), bf16[128,8,256]{2,1,0:T(8,128)(2,1)S(1)}, u32[]{:S(2)}, u32[]{:S(2)}) async-start(bf16[128,8,256]{2,1,0:T(8,128)(2,1)} %bitcast.6), calls=%async_computation.1 | async-start | bytes 1048576 | tf_op jit(solution)/shard_map/all_to_all | solution.py:508
  31.6 9.1 %build.1 = (bf16[2560,2048]{1,0:T(8,128)(2,1)}, f32[90,2048]{1,0:T(8,128)}, bf16[2,90,256]{2,1,0:T(8,128)(2,1)}, bf16[2,90,256]{2,1,0:T(8,128)(2,1)}) custom-call(s32[6,2048]{1,0:T(8,128)} %refs_0_.5, s32[2,256]{1,0:T(2,128)} %bitcast.9, bf16[90,2048]{1,0:T(8,128)(2,1)} %refs_11_.1, bf16[540,2048]{1,0:T(8,128)(2,1)} %refs_8_.2, ...), custom_call_target="tpu_custom_call" | custom-call | flops 3000000000 | bytes 14039552 | tf_op jit(solution)/shard_map/build/pallas_call | solution.py:123
  40.6 0.1 collective-permute-start
  40.7 7.4 %collective-permute-start.1 = (bf16[2,90,256]{2,1,0:T(8,128)(2,1)}, bf16[2,90,256]{2,1,0:T(8,128)(2,1)S(1)}, u32[]{:S(2)}, u32[]{:S(2)}) collective-permute-start(bf16[2,90,256]{2,1,0:T(8,128)(2,1)} %get-tuple-element.42), channel_id=1, source_target_pairs={{0,127},{1,2},{2,1},{3,4},{4,3},{5,6},{6,5},{7,8},{8,7},{9,10},{10... | collective-permute-start | bytes 276488 | tf_op jit(solution)/shard_map/ppermute | solution.py:469
  48.1 0.0 all-to-all-done.1
  48.1 5.9 %network.1 = (bf16[512,2048]{1,0:T(8,128)(2,1)S(1)}, bf16[2048,512]{1,0:T(8,128)(2,1)S(1)}, bf16[2560,2048]{1,0:T(8,128)(2,1)S(1)}, f32[90,2048]{1,0:T(8,128)S(1...) custom-call(bf16[1024,256]{1,0:T(8,128)(2,1)S(1)} %bitcast.5, ...), custom_call_target="tpu_custom_call" | custom-call | flops 5000000000 | bytes 34009088 | tf_op jit(solution)/shard_map/network/pallas_call | solution.py:123
  54.1 0.0 collective-permute-done.refs_0_
  54.1 0.0 collective-permute-done.1.refs_1_
  54.1 2.1 %second.1 = (f32[90,2048]{1,0:T(8,128)S(1)}, f32[90,2048]{1,0:T(8,128)S(1)}, f32[90,2048]{1,0:T(8,128)S(1)}, bf16[2,90,256]{2,1,0:T(8,128)(2,1)S(1)}, bf16[2,90,256]{2,1,0:T(8,128)(2,1)S(1)}) custom-call(bf16[2,90,256]{2,1,0:T(8,128)(2,1)S(1)} %collective-permute-done.refs_0_, bf16[2,90,256]{2,1,0:T(8,128)(2,1)S(1)} %collective-permute-done.1.refs_1_, ...), custom_call_target="tpu_custom_call" | custom-call | flops 1000000000 | bytes 17006592 | tf_op jit(solution)/shard_map/second/pallas_call | solution.py:123
  56.2 0.1 collective-permute-start.2
  56.3 3.8 %collective-permute-start.3 = (bf16[2,90,256]{2,1,0:T(8,128)(2,1)S(1)}, bf16[2,90,256]{2,1,0:T(8,128)(2,1)S(1)}, u32[]{:S(2)}, u32[]{:S(2)}) collective-permute-start(bf16[2,90,256]{2,1,0:T(8,128)(2,1)S(1)} %get-tuple-element.54), channel_id=1, source_target_pairs={{0,127},{1,2},{2,1},{3,4},{4,3},{5,6},{6,5},{7,8},{8,7},{9,10},{10... | collective-permute-start | bytes 276488 | tf_op jit(solution)/shard_map/ppermute | solution.py:469
  60.1 4.0 %between.1 = (f32[90,2048]{1,0:T(8,128)S(1)}, f32[90,2048]{1,0:T(8,128)S(1)}) custom-call(f32[90,2048]{1,0:T(8,128)S(1)} %get-tuple-element.55.refs_0_, f32[90,2048]{1,0:T(8,128)S(1)} %get-tuple-element.56.refs_1_, f32[90,2048]{1,0:T(8,128)S(1)} %get-tuple-element.57.refs_2_, bf16[2560,2048]{1,0:T(8,128)(2,1)S(1)} %get-tuple-element.51.refs_5_.refs_3_.refs_4_), custom_call_target="tpu_custom_call" | custom-call | flops 1000000000 | bytes 14172160 | tf_op jit(solution)/shard_map/between/pallas_call | solution.py:123
  64.1 0.0 collective-permute-done.2.refs_0_
  64.1 1.7 %collective-permute-done.3.refs_1_ = bf16[2,90,256]{2,1,0:T(8,128)(2,1)S(1)} collective-permute-done((bf16[2,90,256]{2,1,0:T(8,128)(2,1)S(1)}, bf16[2,90,256]{2,1,0:T(8,128)(2,1)S(1)}, u32[]{:S(2)}, u32[]{:S(2)}) %collective-permute-start.3) | collective-permute-done | bytes 92192 | tf_op jit(solution)/shard_map/ppermute | solution.py:469
  65.8 2.1 %third.1 = (f32[90,2048]{1,0:T(8,128)S(1)}, bf16[90,2048]{1,0:T(8,128)(2,1)S(1)}, f32[90,2048]{1,0:T(8,128)S(1)}, bf16[2,90,256]{2,1,0:T(8,128)(2,1)S(1)}, bf16[2,90,256]{2,1,0:T(8,128)(2,1)S(1)}) custom-call(bf16[2,90,256]{2,1,0:T(8,128)(2,1)S(1)} %collective-permute-done.2.refs_0_, bf16[2,90,256]{2,1,0:T(8,128)(2,1)S(1)} %collective-permute-done.3.refs_1_, ...), custom_call_target="tpu_custom_call" | custom-call | flops 1000000000 | bytes 17006592 | tf_op jit(solution)/shard_map/third/pallas_call | solution.py:123
  67.9 0.1 collective-permute-start.4
  68.0 4.0 %collective-permute-start.5 = (bf16[2,90,256]{2,1,0:T(8,128)(2,1)S(1)}, bf16[2,90,256]{2,1,0:T(8,128)(2,1)S(1)}, u32[]{:S(2)}, u32[]{:S(2)}) collective-permute-start(bf16[2,90,256]{2,1,0:T(8,128)(2,1)S(1)} %get-tuple-element.62), channel_id=1, source_target_pairs={{0,127},{1,2},{2,1},{3,4},{4,3},{5,6},{6,5},{7,8},{8,7},{9,10},{10... | collective-permute-start | bytes 276488 | tf_op jit(solution)/shard_map/ppermute | solution.py:469
  72.0 8.0 %window.1 = (bf16[540,2048]{1,0:T(8,128)(2,1)}, f32[96,2048]{1,0:T(8,128)S(1)}, f32[90,2048]{1,0:T(8,128)S(1)}, f32[90,2048]{1,0:T(8,128)S(1)}) custom-call(f32[90,2048]{1,0:T(8,128)S(1)} %get-tuple-element.63.refs_0_, f32[90,2048]{1,0:T(8,128)S(1)} %get-tuple-element.64.refs_1_, f32[90,2048]{1,0:T(8,128)S(1)} %get-tuple-element.57.refs_2_, ...), custom_call_target="tpu_custom_call" | custom-call | flops 3000000000 | bytes 21793792 | tf_op jit(solution)/shard_map/window/pallas_call | solution.py:123
  80.0 0.0 collective-permute-done.4.refs_0_
  80.0 0.0 collective-permute-done.5.refs_1_
  80.0 1.9 %finish.1 = (bf16[540,2048]{1,0:T(8,128)(2,1)}, f32[90,2048]{1,0:T(8,128)}) custom-call(bf16[2,90,256]{2,1,0:T(8,128)(2,1)S(1)} %collective-permute-done.4.refs_0_, bf16[2,90,256]{2,1,0:T(8,128)(2,1)S(1)} %collective-permute-done.5.refs_1_, bf16[2048,512]{1,0:T(8,128)(2,1)S(1)} %get-tuple-element.48.refs_2_, ...), custom_call_target="tpu_custom_call", output_to_operand_aliasing={{0}: (7, {})} | custom-call | flops 1000000000 | bytes 20189184 | tf_op jit(solution)/shard_map/finish/pallas_call | solution.py:123
Async XLA Ops:
  0.6 0.7 copy-start
  2.5 20.7 %all-to-all-start = ((f32[128,1,128]{2,1,0:T(1,128)}), f32[128,1,128]{2,1,0:T(1,128)S(1)}, u32[]{:S(2)}, u32[]{:S(2)}) async-start(f32[128,1,128]{2,1,0:T(1,128)} %get-tuple-element.38), calls=%async_computation | async-start | bytes 131072 | tf_op jit(solution)/shard_map/all_to_all | solution.py:479
  25.6 22.5 %all-to-all-start.1 = ((bf16[128,8,256]{2,1,0:T(8,128)(2,1)}), bf16[128,8,256]{2,1,0:T(8,128)(2,1)S(1)}, u32[]{:S(2)}, u32[]{:S(2)}) async-start(bf16[128,8,256]{2,1,0:T(8,128)(2,1)} %bitcast.6), calls=%async_computation.1 | async-start | bytes 1048576 | tf_op jit(solution)/shard_map/all_to_all | solution.py:508
  40.6 13.4 %collective-permute-start = (bf16[2,90,256]{2,1,0:T(8,128)(2,1)}, bf16[2,90,256]{2,1,0:T(8,128)(2,1)S(1)}, u32[]{:S(2)}, u32[]{:S(2)}) collective-permute-start(bf16[2,90,256]{2,1,0:T(8,128)(2,1)} %get-tuple-element.41), channel_id=1, source_target_pairs={{0,1},{1,0},{2,3},{3,2},{4,5},{5,4},{6,7},{7,6},{8,9},{9,8},{10,11... | collective-permute-start | bytes 276488 | tf_op jit(solution)/shard_map/ppermute | solution.py:470
  40.7 13.4 %collective-permute-start.1 = (bf16[2,90,256]{2,1,0:T(8,128)(2,1)}, bf16[2,90,256]{2,1,0:T(8,128)(2,1)S(1)}, u32[]{:S(2)}, u32[]{:S(2)}) collective-permute-start(bf16[2,90,256]{2,1,0:T(8,128)(2,1)} %get-tuple-element.42), channel_id=1, source_target_pairs={{0,127},{1,2},{2,1},{3,4},{4,3},{5,6},{6,5},{7,8},{8,7},{9,10},{10... | collective-permute-start | bytes 276488 | tf_op jit(solution)/shard_map/ppermute | solution.py:469
  56.2 7.9 %collective-permute-start.2 = (bf16[2,90,256]{2,1,0:T(8,128)(2,1)S(1)}, bf16[2,90,256]{2,1,0:T(8,128)(2,1)S(1)}, u32[]{:S(2)}, u32[]{:S(2)}) collective-permute-start(bf16[2,90,256]{2,1,0:T(8,128)(2,1)S(1)} %get-tuple-element.53), channel_id=1, source_target_pairs={{0,1},{1,0},{2,3},{3,2},{4,5},{5,4},{6,7},{7,6},{8,9},{9,8},{10,11... | collective-permute-start | bytes 276488 | tf_op jit(solution)/shard_map/ppermute | solution.py:470
  56.3 9.6 %collective-permute-start.3 = (bf16[2,90,256]{2,1,0:T(8,128)(2,1)S(1)}, bf16[2,90,256]{2,1,0:T(8,128)(2,1)S(1)}, u32[]{:S(2)}, u32[]{:S(2)}) collective-permute-start(bf16[2,90,256]{2,1,0:T(8,128)(2,1)S(1)} %get-tuple-element.54), channel_id=1, source_target_pairs={{0,127},{1,2},{2,1},{3,4},{4,3},{5,6},{6,5},{7,8},{8,7},{9,10},{10... | collective-permute-start | bytes 276488 | tf_op jit(solution)/shard_map/ppermute | solution.py:469
  67.9 12.1 %collective-permute-start.4 = (bf16[2,90,256]{2,1,0:T(8,128)(2,1)S(1)}, bf16[2,90,256]{2,1,0:T(8,128)(2,1)S(1)}, u32[]{:S(2)}, u32[]{:S(2)}) collective-permute-start(bf16[2,90,256]{2,1,0:T(8,128)(2,1)S(1)} %get-tuple-element.61), channel_id=1, source_target_pairs={{0,1},{1,0},{2,3},{3,2},{4,5},{5,4},{6,7},{7,6},{8,9},{9,8},{10,11... | collective-permute-start | bytes 276488 | tf_op jit(solution)/shard_map/ppermute | solution.py:470
  68.0 12.0 %collective-permute-start.5 = (bf16[2,90,256]{2,1,0:T(8,128)(2,1)S(1)}, bf16[2,90,256]{2,1,0:T(8,128)(2,1)S(1)}, u32[]{:S(2)}, u32[]{:S(2)}) collective-permute-start(bf16[2,90,256]{2,1,0:T(8,128)(2,1)S(1)} %get-tuple-element.62), channel_id=1, source_target_pairs={{0,127},{1,2},{2,1},{3,4},{4,3},{5,6},{6,5},{7,8},{8,7},{9,10},{10... | collective-permute-start | bytes 276488 | tf_op jit(solution)/shard_map/ppermute | solution.py:469

commit v6 on v5

--- a/solution.py
+++ b/solution.py
@@ -182,7 +182,7 @@
 
 
 def route_kernel(parent_ref, request_ref, slot_ref):
-    parents = parent_ref[...]
+    parents = parent_ref()[...]
     target = parents >> 9
     column = (parents & (COLS - 1)) + 1
     target_column = to_column(target.astype(f32))
@@ -243,7 +243,7 @@
 
 def build_kernel(
     slots_ref, lists_ref, forcing_ref, state_ref, token_ref,
-    links_ref, part_ref, first_ref, second_ref, links, border_ref, sems,
+    links_ref, part_ref, first_ref, second_ref, ahead_ref, links, border_ref, sems,
 ):
     even = (lax.axis_index("cells") & 1) == 0
     slots = slots_ref()[...]
@@ -281,6 +281,11 @@
         else:
             sl = slice(jb * 256, (jb + 1) * 256)
             part_ref.ref[:, sl] = KEEP * forcing[:, sl].astype(f32) + share(jb)
+            total = SPREAD * dot(state[:LEV, sl], links[sl, :], NN)
+            if jb == 0:
+                ahead_ref.ref[...] = KEEP * state[:LEV, :].astype(f32) + total
+            else:
+                ahead_ref.ref[...] += total
 
     make_border(lists_ref(), border_ref)
     state = state_ref()
@@ -297,6 +302,7 @@
     first_ref.put()
     second_ref.put()
     part_ref.put()
+    ahead_ref.put()
     for jb in range(10):
         out(jb).wait()
 
@@ -305,16 +311,18 @@
     return dot(first, border[:, :HALO], NT) + dot(second, border[:, HALO:], NT)
 
 
-def push(rounded, links, first_ref, second_ref):
-    share = SPREAD * dot(rounded, links[CELLS:, :], NT)
+def push(rounded, halo, first_ref, second_ref):
+    share = SPREAD * dot(rounded, halo[...], NT)
     first_ref[0] = share[:, :HALO].astype(bf16)
     second_ref[0] = share[:, HALO:].astype(bf16)
 
 
-def pull(adjoint_ref, links, part_ref):
+def pull(adjoint_ref, links, part_ref, wait=None):
     rounded = adjoint_ref[...].astype(bf16)
     for i in range(OWN):
         sl = slice(i * PIECE, (i + 1) * PIECE)
+        if wait is not None:
+            wait(i)
         part_ref[:, sl] = KEEP * adjoint_ref[:, sl] + SPREAD * dot(rounded, links[sl, :], NT)
 
 
@@ -326,23 +334,18 @@
 
 def network_kernel(
     answer_ref, slot_ref, drive_ref, w_hidden_ref, w_out_ref, bias_ref, order_ref, lists_ref,
-    state_ref, links_far, part_far, forcing_far,
-    groups, border, links, heat_ref, slope_ref, ahead_ref, part_ref, forcing_ref,
+    own_ref, links_far, part_far, forcing_far,
+    groups, border, halo, heat_ref, slope_ref, ahead_ref, part_ref, forcing_ref,
     sems,
 ):
-    def piece(i):
-        rows = pl.ds(i * PIECE, PIECE)
-        return pltpu.make_async_copy(links_far.at[rows], links.at[rows], sems.at[i])
-
     later = [
-        pltpu.make_async_copy(part_far, part_ref, sems.at[OWN + 1]),
-        pltpu.make_async_copy(forcing_far, forcing_ref, sems.at[OWN + 2]),
+        pltpu.make_async_copy(part_far, part_ref, sems.at[0]),
+        pltpu.make_async_copy(forcing_far, forcing_ref, sems.at[1]),
+        pltpu.make_async_copy(links_far.at[pl.ds(CELLS, 2 * HALO)], halo, sems.at[2]),
     ]
-    small = (slot_ref, drive_ref, w_hidden_ref, w_out_ref, bias_ref, order_ref, lists_ref, state_ref)
+    small = (slot_ref, drive_ref, w_hidden_ref, w_out_ref, bias_ref, order_ref, lists_ref, own_ref)
     for operand in small:
         operand()
-    for i in range(OWN + 1):
-        piece(i).start()
     for copy in later:
         copy.start()
 
@@ -366,26 +369,21 @@
         slope_ref[layer + 1] = slope
         tangent = (slope * dot(weight, tangent, TN)).astype(bf16)
     heating = dot(w_out_ref()[...], tangent, NN).astype(bf16)
-    heat_ref[...] = dot(heating, groups[...], NN)
-    state = state_ref()
-    ahead_ref[...] = KEEP * state[:LEV, :].astype(f32) + heat_ref[...]
-    for i in range(OWN):
-        piece(i).wait()
-        sl = slice(i * PIECE, (i + 1) * PIECE)
-        ahead_ref[...] += SPREAD * dot(state[:LEV, sl], links[sl, :], NN)
-    piece(OWN).wait()
+    heat = dot(heating, groups[...], NN)
+    heat_ref[...] = heat
+    ahead_ref[...] = own_ref()[...] + heat
     for copy in later:
         copy.wait()
 
 
 def second_kernel(
-    first_in, second_in, border, part_in, forcing_ref, links, ahead_ref,
+    first_in, second_in, border, part_in, forcing_ref, halo, ahead_ref,
     adjoint_ref, heat_back_ref, temp_ref, first_ref, second_ref,
 ):
     adjoint = part_in[...] + received(first_in[0], second_in[0], border)
     adjoint_ref[...] = adjoint
-    push(adjoint.astype(bf16), links, first_ref, second_ref)
-    temp = outer(ahead_ref, first_in[1], second_in[1], links)
+    push(adjoint.astype(bf16), halo, first_ref, second_ref)
+    temp = outer(ahead_ref, first_in[1], second_in[1], halo)
     temp_ref[...] = temp
     send_border(temp, border, first_ref, second_ref)
     heat_back_ref[...] = forcing_ref[...].astype(f32) + adjoint
@@ -398,28 +396,36 @@
         part_ref[:, sl] = (
             KEEP * temp_ref[:LEV, sl].astype(f32)
             + heat_ref[:, sl]
-            + SPREAD * dot(rounded, links[:CELLS, sl], NN)
+            + SPREAD * dot(rounded, links[:, sl], NN)
         )
 
 
-def outer(part_ref, first, second, links):
+def outer(part_ref, first, second, halo):
     sides = jnp.concatenate([first, second], axis=1)
-    return part_ref[...] + SPREAD * dot(sides, links[CELLS:, :], NN)
-
-
-def between_kernel(adjoint_ref, temp_ref, heat_ref, links, part_ref, ahead_ref):
-    pull(adjoint_ref, links, part_ref)
+    return part_ref[...] + SPREAD * dot(sides, halo[...], NN)
+
+
+def between_kernel(
+    adjoint_ref, temp_ref, heat_ref, links_far, links, part_ref, ahead_ref, sems
+):
+    def piece(i):
+        rows = pl.ds(i * PIECE, PIECE)
+        return pltpu.make_async_copy(links_far.at[rows], links.at[rows], sems.at[i])
+
+    for i in range(OWN):
+        piece(i).start()
+    pull(adjoint_ref, links, part_ref, lambda i: piece(i).wait())
     inner(temp_ref, heat_ref, links, ahead_ref)
 
 
 def third_kernel(
-    first_in, second_in, border, part_in, heat_back_ref, links, ahead_ref,
+    first_in, second_in, border, part_in, heat_back_ref, halo, ahead_ref,
     adjoint_ref, back_ref, temp_ref, first_ref, second_ref,
 ):
     adjoint = part_in[...] + received(first_in[0], second_in[0], border)
     adjoint_ref[...] = adjoint
-    push(adjoint.astype(bf16), links, first_ref, second_ref)
-    temp = outer(ahead_ref, first_in[1], second_in[1], links)
+    push(adjoint.astype(bf16), halo, first_ref, second_ref)
+    temp = outer(ahead_ref, first_in[1], second_in[1], halo)
     temp_ref[...] = temp
     send_border(temp, border, first_ref, second_ref)
     back_ref[...] = (heat_back_ref[...] + adjoint).astype(bf16)
@@ -445,10 +451,10 @@
 
 
 def finish_kernel(
-    first_in, second_in, border, part_in, links, ahead_ref, top_in, sens_in,
+    first_in, second_in, border, part_in, halo, ahead_ref, top_in, sens_in,
     sens_far, temp_far, top_ref, sem,
 ):
-    temp_far.ref[...] = outer(ahead_ref, first_in[1], second_in[1], links)
+    temp_far.ref[...] = outer(ahead_ref, first_in[1], second_in[1], halo)
     temp_far.put()
     adjoint = part_in[...] + received(first_in[0], second_in[0], border)
     top_ref[:LEV] = (top_in[:LEV] + adjoint).astype(bf16)
@@ -472,7 +478,7 @@
     request, slot = kernel(
         route_kernel,
         "route",
-        [group_parent],
+        [whole(group_parent)],
         [(shape((DEVS, 1, 128), f32), True), (shape((1, COLS), i32), True)],
         flops=10**7,
     )
@@ -507,14 +513,14 @@
     )
     got = lax.all_to_all(answer.reshape(DEVS, CAP, HID), "cells", 0, 0, tiled=True)
     got = got.reshape(SLOTS, HID)
-    links, part, first, second = kernel(
+    links, part, first, second, own = kernel(
         build_kernel,
         "build",
         [
             whole(adjacent_source_slots), whole(outgoing_local_lists[0]), whole(forcing), state_rows,
             ("raw", token),
         ],
-        [(all_links, "raw"), (field, True), (side, True), (side, True)],
+        [(all_links, "raw"), (field, True), (side, True), (side, True), (field, True)],
         scratch=[
             pltpu.VMEM((EXT, CELLS), bf16),
             pltpu.VMEM((CELLS, 2 * HALO), bf16),
@@ -525,37 +531,42 @@
     first, second = swap(first, second)
 
     near = (field, False)
-    groups, border, links, heat, slope, ahead, part, late_forcing = kernel(
+    groups, border, halo, heat, slope, ahead, part, late_forcing = kernel(
         network_kernel,
         "network",
         [
             got, whole(slot), whole(drive), whole(w_hidden), whole(w_out.T), whole(biases),
-            whole(fine_order), whole(outgoing_local_lists[0]), state_rows,
+            whole(fine_order), whole(outgoing_local_lists[0]), whole(own),
             ("raw", links), ("raw", part), ("raw", forcing),
         ],
         [
-            (all_groups, False), (all_border, False), (all_links, False), near,
+            (all_groups, False), (all_border, False), (shape((2 * HALO, CELLS), bf16), False), near,
             (shape((3, HID, COLS), f32), False), near, near, (shape((LEV, CELLS), bf16), False),
         ],
-        scratch=[pltpu.SemaphoreType.DMA((7,))],
+        scratch=[pltpu.SemaphoreType.DMA((3,))],
         limit=32,
         flops=5 * 10**9,
     )
     adjoint, heat_back, temp, first, second = kernel(
         second_kernel,
         "second",
-        [first, second, border, part, late_forcing, links, ahead],
+        [first, second, border, part, late_forcing, halo, ahead],
         [near, near, near, (side, False), (side, False)],
         limit=32,
     )
     first, second = swap(first, second)
-    part, ahead = kernel(
-        between_kernel, "between", [adjoint, temp, heat, links], [near, near], limit=32
+    links, part, ahead = kernel(
+        between_kernel,
+        "between",
+        [adjoint, temp, heat, ("raw", links)],
+        [(shape((CELLS, CELLS), bf16), False), near, near],
+        scratch=[pltpu.SemaphoreType.DMA((OWN,))],
+        limit=32,
     )
     adjoint, back, temp, first, second = kernel(
         third_kernel,
         "third",
-        [first, second, border, part, heat_back, links, ahead],
+        [first, second, border, part, heat_back, halo, ahead],
         [near, (shape((LEV, CELLS), bf16), False), near, (side, False), (side, False)],
         limit=32,
     )
@@ -577,7 +588,7 @@
     sens, temp = kernel(
         finish_kernel,
         "finish",
-        [first, second, border, part, links, ahead, top, ("raw", sens)],
+        [first, second, border, part, halo, ahead, top, ("raw", sens)],
         [(shape((FEAT, CELLS), bf16), "raw"), (field, True)],
         scratch=[pltpu.VMEM((TOP, CELLS), bf16), pltpu.SemaphoreType.DMA],
         limit=32,

time: 82.4 us -> 83 us (level)
  starting transfers between devices: 32.6 us -> 34.7 us
  waiting for transfers between devices: 5.58 us -> 3.77 us
  Pallas kernels: 42.3 us -> 43.3 us
    ppermute x3, starting transfers between devices: 15.2 us -> 17.3 us  [swap(): second = lax.ppermute(second, 'cells', far_pairs)]
    ppermute x3, waiting for transfers between devices: 1.74 us -> 0.01 us  [swap(): second = lax.ppermute(second, 'cells', far_pairs)]
    pallas_call x10, Pallas kernels: 42.3 us -> 43.3 us  [kernel(): pl.pallas_call(wrapped, out_shape=tuple(out_shapes), in_specs=in_specs, o...]
  transfers between devices with their start and end apart: 8 -> 8, of which waited for: 2 -> 1; matrix products, arithmetic and copies ran while one was open for 0% -> 0% of each run, Pallas kernels for 40% -> 40%
where the time goes in v6:
time: 83 us; the launch traced here: 82.7 us
  Pallas kernels  43.3 us (52%)
  starting transfers between devices  34.7 us (42%)
  waiting for transfers between devices  3.77 us (5%)
  between operations  0.96 us (1%)
    pallas_call x10, Pallas kernels, kernel(): pl.pallas_call(wrapped, out_shape=tuple(out_shapes), in_specs=in_specs, o...  43.3 us
    ppermute x3, starting transfers between devices, swap(): second = lax.ppermute(second, 'cells', far_pairs)  17.3 us
    all_to_all x1, starting transfers between devices, local(): asked = lax.all_to_all(request, 'cells', 0, 0, tiled=True)  11.1 us
    all_to_all x1, starting transfers between devices, local(): lax.all_to_all(answer.reshape(DEVS, CAP, HID), 'cells', 0, 0, tiled=True)  6.01 us
    all_to_all x1, waiting for transfers between devices, local(): asked = lax.all_to_all(request, 'cells', 0, 0, tiled=True)  3.75 us
  transfers between devices with their start and end apart: 8, of which 1 were waited for; matrix products, arithmetic and copies ran while one was open for 0% of the time, Pallas kernels for 40%

profile of v6, /device:TPU:0, one launch (start us, length us, event | category | flops | bytes accessed | tf_op | source)
XLA Modules:
  0.0 82.7 jit_solution(2172352986653980266)
XLA Ops:
  0.6 1.9 %route.1 = (f32[128,1,128]{2,1,0:T(1,128)}, s32[1,512]{1,0:T(1,128)}) custom-call(s32[1,512]{1,0:T(1,128)} %refs_0_.3), custom_call_target="tpu_custom_call" | custom-call | flops 10000000 | bytes 69632 | tf_op jit(solution)/shard_map/route/pallas_call | solution.py:123
  2.5 11.1 %all-to-all-start = ((f32[128,1,128]{2,1,0:T(1,128)}), f32[128,1,128]{2,1,0:T(1,128)S(1)}, u32[]{:S(2)}, u32[]{:S(2)}) async-start(f32[128,1,128]{2,1,0:T(1,128)} %get-tuple-element.40), calls=%async_computation | async-start | bytes 131072 | tf_op jit(solution)/shard_map/all_to_all | solution.py:485
  13.7 5.7 %prepare.1 = (f32[256,512]{1,0:T(8,128)}, bf16[512,256]{1,0:T(8,128)(2,1)}) custom-call(s32[1,2048]{1,0:T(1,128)} %refs_6_.1, bf16[540,2048]{1,0:T(8,128)(2,1)} %refs_3_.4, bf16[540,256]{1,0:T(8,128)(2,1)} %refs_9_.1, bf16[540,512]{1,0:T(8,128)(2,1)} %refs_3_.3, f32[3,256]{1,0:T(4,128)} %refs_5_.3, s32[1,512]{1,0:T(1,128)} %refs_5_.2, s32[1,128]{1,0:T(1,128)} %bitcast.11), custom_call_target="tpu_custom_call" | custom-call | flops 2000000000 | bytes 3841536 | tf_op jit(solution)/shard_map/prepare/pallas_call | solution.py:123
  19.3 3.8 %all-to-all-done.refs_0_ = f32[128,1,128]{2,1,0:T(1,128)S(1)} async-done(((f32[128,1,128]{2,1,0:T(1,128)}), f32[128,1,128]{2,1,0:T(1,128)S(1)}, u32[]{:S(2)}, u32[]{:S(2)}) %all-to-all-start) | async-done | bytes 65568 | tf_op jit(solution)/shard_map/all_to_all | solution.py:485
  23.1 2.4 %answer.1 = (bf16[1024,256]{1,0:T(8,128)(2,1)}, f32[1,128]{1,0:T(1,128)}) custom-call(f32[128,1,128]{2,1,0:T(1,128)S(1)} %all-to-all-done.refs_0_, bf16[512,256]{1,0:T(8,128)(2,1)} %get-tuple-element.41.refs_1_), custom_call_target="tpu_custom_call" | custom-call | flops 1000000000 | bytes 852480 | tf_op jit(solution)/shard_map/answer/pallas_call | solution.py:123
  25.5 6.0 %all-to-all-start.1 = ((bf16[128,8,256]{2,1,0:T(8,128)(2,1)}), bf16[128,8,256]{2,1,0:T(8,128)(2,1)S(1)}, u32[]{:S(2)}, u32[]{:S(2)}) async-start(bf16[128,8,256]{2,1,0:T(8,128)(2,1)} %bitcast.6), calls=%async_computation.1 | async-start | bytes 1048576 | tf_op jit(solution)/shard_map/all_to_all | solution.py:514
  31.5 9.7 %build.1 = (bf16[2560,2048]{1,0:T(8,128)(2,1)}, f32[90,2048]{1,0:T(8,128)}, bf16[2,90,256]{2,1,0:T(8,128)(2,1)}, bf16[2,90,256]{2,1,0:T(8,128)(2,1)}, f32[90,2048]{1,0:T(8,128)}) custom-call(s32[6,2048]{1,0:T(8,128)} %refs_0_.5, s32[2,256]{1,0:T(2,128)} %bitcast.9, bf16[90,2048]{1,0:T(8,128)(2,1)} %refs_11_.1, bf16[540,2048]{1,0:T(8,128)(2,1)} %refs_3_.4, ...), custom_call_target="tpu_custom_call" | custom-call | flops 3000000000 | bytes 14776832 | tf_op jit(solution)/shard_map/build/pallas_call | solution.py:123
  41.2 0.1 collective-permute-start
  41.3 7.4 %collective-permute-start.1 = (bf16[2,90,256]{2,1,0:T(8,128)(2,1)}, bf16[2,90,256]{2,1,0:T(8,128)(2,1)S(1)}, u32[]{:S(2)}, u32[]{:S(2)}) collective-permute-start(bf16[2,90,256]{2,1,0:T(8,128)(2,1)} %get-tuple-element.44), channel_id=1, source_target_pairs={{0,127},{1,2},{2,1},{3,4},{4,3},{5,6},{6,5},{7,8},{8,7},{9,10},{10... | collective-permute-start | bytes 276488 | tf_op jit(solution)/shard_map/ppermute | solution.py:475
  48.7 0.0 all-to-all-done.1
  48.7 3.6 %network.1 = (bf16[512,2048]{1,0:T(8,128)(2,1)S(1)}, bf16[2048,512]{1,0:T(8,128)(2,1)S(1)}, bf16[512,2048]{1,0:T(8,128)(2,1)S(1)}, f32[90,2048]{1,0:T(8,128)S(1)...) custom-call(bf16[1024,256]{1,0:T(8,128)(2,1)S(1)} %bitcast.5, ...), custom_call_target="tpu_custom_call" | custom-call | flops 5000000000 | bytes 24145920 | tf_op jit(solution)/shard_map/network/pallas_call | solution.py:123
  52.3 0.0 collective-permute-done.refs_0_
  52.3 0.0 collective-permute-done.1.refs_1_
  52.3 2.1 %second.1 = (f32[90,2048]{1,0:T(8,128)S(1)}, f32[90,2048]{1,0:T(8,128)S(1)}, f32[90,2048]{1,0:T(8,128)S(1)}, bf16[2,90,256]{2,1,0:T(8,128)(2,1)S(1)}, bf16[2,90,256]{2,1,0:T(8,128)(2,1)S(1)}) custom-call(bf16[2,90,256]{2,1,0:T(8,128)(2,1)S(1)} %collective-permute-done.refs_0_, bf16[2,90,256]{2,1,0:T(8,128)(2,1)S(1)} %collective-permute-done.1.refs_1_, ...), custom_call_target="tpu_custom_call" | custom-call | flops 1000000000 | bytes 8617984 | tf_op jit(solution)/shard_map/second/pallas_call | solution.py:123
  54.4 0.1 collective-permute-start.2
  54.5 6.1 %collective-permute-start.3 = (bf16[2,90,256]{2,1,0:T(8,128)(2,1)S(1)}, bf16[2,90,256]{2,1,0:T(8,128)(2,1)S(1)}, u32[]{:S(2)}, u32[]{:S(2)}) collective-permute-start(bf16[2,90,256]{2,1,0:T(8,128)(2,1)S(1)} %get-tuple-element.57), channel_id=1, source_target_pairs={{0,127},{1,2},{2,1},{3,4},{4,3},{5,6},{6,5},{7,8},{8,7},{9,10},{10... | collective-permute-start | bytes 276488 | tf_op jit(solution)/shard_map/ppermute | solution.py:475
  60.6 6.0 %between.1 = (bf16[2048,2048]{1,0:T(8,128)(2,1)S(1)}, f32[90,2048]{1,0:T(8,128)S(1)}, f32[90,2048]{1,0:T(8,128)S(1)}) custom-call(f32[90,2048]{1,0:T(8,128)S(1)} %get-tuple-element.58.refs_0_, f32[90,2048]{1,0:T(8,128)S(1)} %get-tuple-element.59.refs_1_, f32[90,2048]{1,0:T(8,128)S(1)} %get-tuple-element.60.refs_2_, ...), custom_call_target="tpu_custom_call" | custom-call | flops 1000000000 | bytes 22560768 | tf_op jit(solution)/shard_map/between/pallas_call | solution.py:123
  66.7 0.0 collective-permute-done.2.refs_0_
  66.7 0.0 collective-permute-done.3.refs_1_
  66.7 2.1 %third.1 = (f32[90,2048]{1,0:T(8,128)S(1)}, bf16[90,2048]{1,0:T(8,128)(2,1)S(1)}, f32[90,2048]{1,0:T(8,128)S(1)}, bf16[2,90,256]{2,1,0:T(8,128)(2,1)S(1)}, bf16[2,90,256]{2,1,0:T(8,128)(2,1)S(1)}) custom-call(bf16[2,90,256]{2,1,0:T(8,128)(2,1)S(1)} %collective-permute-done.2.refs_0_, bf16[2,90,256]{2,1,0:T(8,128)(2,1)S(1)} %collective-permute-done.3.refs_1_, ...), custom_call_target="tpu_custom_call" | custom-call | flops 1000000000 | bytes 8617984 | tf_op jit(solution)/shard_map/third/pallas_call | solution.py:123
  68.8 0.1 collective-permute-start.4
  68.9 3.7 %collective-permute-start.5 = (bf16[2,90,256]{2,1,0:T(8,128)(2,1)S(1)}, bf16[2,90,256]{2,1,0:T(8,128)(2,1)S(1)}, u32[]{:S(2)}, u32[]{:S(2)}) collective-permute-start(bf16[2,90,256]{2,1,0:T(8,128)(2,1)S(1)} %get-tuple-element.65), channel_id=1, source_target_pairs={{0,127},{1,2},{2,1},{3,4},{4,3},{5,6},{6,5},{7,8},{8,7},{9,10},{10... | collective-permute-start | bytes 276488 | tf_op jit(solution)/shard_map/ppermute | solution.py:475
  72.6 8.0 %window.1 = (bf16[540,2048]{1,0:T(8,128)(2,1)}, f32[96,2048]{1,0:T(8,128)S(1)}, f32[90,2048]{1,0:T(8,128)S(1)}, f32[90,2048]{1,0:T(8,128)S(1)}) custom-call(f32[90,2048]{1,0:T(8,128)S(1)} %get-tuple-element.66.refs_0_, f32[90,2048]{1,0:T(8,128)S(1)} %get-tuple-element.67.refs_1_, f32[90,2048]{1,0:T(8,128)S(1)} %get-tuple-element.60.refs_2_, ...), custom_call_target="tpu_custom_call" | custom-call | flops 3000000000 | bytes 19696640 | tf_op jit(solution)/shard_map/window/pallas_call | solution.py:123
  80.6 0.0 collective-permute-done.4.refs_0_
  80.6 0.0 collective-permute-done.5.refs_1_
  80.6 1.9 %finish.1 = (bf16[540,2048]{1,0:T(8,128)(2,1)}, f32[90,2048]{1,0:T(8,128)}) custom-call(bf16[2,90,256]{2,1,0:T(8,128)(2,1)S(1)} %collective-permute-done.4.refs_0_, bf16[2,90,256]{2,1,0:T(8,128)(2,1)S(1)} %collective-permute-done.5.refs_1_, bf16[2048,512]{1,0:T(8,128)(2,1)S(1)} %get-tuple-element.51.refs_2_, ...), custom_call_target="tpu_custom_call", output_to_operand_aliasing={{0}: (7, {})} | custom-call | flops 1000000000 | bytes 11800576 | tf_op jit(solution)/shard_map/finish/pallas_call | solution.py:123
Async XLA Ops:
  2.5 20.6 %all-to-all-start = ((f32[128,1,128]{2,1,0:T(1,128)}), f32[128,1,128]{2,1,0:T(1,128)S(1)}, u32[]{:S(2)}, u32[]{:S(2)}) async-start(f32[128,1,128]{2,1,0:T(1,128)} %get-tuple-element.40), calls=%async_computation | async-start | bytes 131072 | tf_op jit(solution)/shard_map/all_to_all | solution.py:485
  25.5 23.2 %all-to-all-start.1 = ((bf16[128,8,256]{2,1,0:T(8,128)(2,1)}), bf16[128,8,256]{2,1,0:T(8,128)(2,1)S(1)}, u32[]{:S(2)}, u32[]{:S(2)}) async-start(bf16[128,8,256]{2,1,0:T(8,128)(2,1)} %bitcast.6), calls=%async_computation.1 | async-start | bytes 1048576 | tf_op jit(solution)/shard_map/all_to_all | solution.py:514
  41.2 11.1 %collective-permute-start = (bf16[2,90,256]{2,1,0:T(8,128)(2,1)}, bf16[2,90,256]{2,1,0:T(8,128)(2,1)S(1)}, u32[]{:S(2)}, u32[]{:S(2)}) collective-permute-start(bf16[2,90,256]{2,1,0:T(8,128)(2,1)} %get-tuple-element.43), channel_id=1, source_target_pairs={{0,1},{1,0},{2,3},{3,2},{4,5},{5,4},{6,7},{7,6},{8,9},{9,8},{10,11... | collective-permute-start | bytes 276488 | tf_op jit(solution)/shard_map/ppermute | solution.py:476
  41.3 11.0 %collective-permute-start.1 = (bf16[2,90,256]{2,1,0:T(8,128)(2,1)}, bf16[2,90,256]{2,1,0:T(8,128)(2,1)S(1)}, u32[]{:S(2)}, u32[]{:S(2)}) collective-permute-start(bf16[2,90,256]{2,1,0:T(8,128)(2,1)} %get-tuple-element.44), channel_id=1, source_target_pairs={{0,127},{1,2},{2,1},{3,4},{4,3},{5,6},{6,5},{7,8},{8,7},{9,10},{10... | collective-permute-start | bytes 276488 | tf_op jit(solution)/shard_map/ppermute | solution.py:475
  54.4 12.3 %collective-permute-start.2 = (bf16[2,90,256]{2,1,0:T(8,128)(2,1)S(1)}, bf16[2,90,256]{2,1,0:T(8,128)(2,1)S(1)}, u32[]{:S(2)}, u32[]{:S(2)}) collective-permute-start(bf16[2,90,256]{2,1,0:T(8,128)(2,1)S(1)} %get-tuple-element.56), channel_id=1, source_target_pairs={{0,1},{1,0},{2,3},{3,2},{4,5},{5,4},{6,7},{7,6},{8,9},{9,8},{10,11... | collective-permute-start | bytes 276488 | tf_op jit(solution)/shard_map/ppermute | solution.py:476
  54.5 12.2 %collective-permute-start.3 = (bf16[2,90,256]{2,1,0:T(8,128)(2,1)S(1)}, bf16[2,90,256]{2,1,0:T(8,128)(2,1)S(1)}, u32[]{:S(2)}, u32[]{:S(2)}) collective-permute-start(bf16[2,90,256]{2,1,0:T(8,128)(2,1)S(1)} %get-tuple-element.57), channel_id=1, source_target_pairs={{0,127},{1,2},{2,1},{3,4},{4,3},{5,6},{6,5},{7,8},{8,7},{9,10},{10... | collective-permute-start | bytes 276488 | tf_op jit(solution)/shard_map/ppermute | solution.py:475
  68.8 11.8 %collective-permute-start.4 = (bf16[2,90,256]{2,1,0:T(8,128)(2,1)S(1)}, bf16[2,90,256]{2,1,0:T(8,128)(2,1)S(1)}, u32[]{:S(2)}, u32[]{:S(2)}) collective-permute-start(bf16[2,90,256]{2,1,0:T(8,128)(2,1)S(1)} %get-tuple-element.64), channel_id=1, source_target_pairs={{0,1},{1,0},{2,3},{3,2},{4,5},{5,4},{6,7},{7,6},{8,9},{9,8},{10,11... | collective-permute-start | bytes 276488 | tf_op jit(solution)/shard_map/ppermute | solution.py:476
  68.9 11.7 %collective-permute-start.5 = (bf16[2,90,256]{2,1,0:T(8,128)(2,1)S(1)}, bf16[2,90,256]{2,1,0:T(8,128)(2,1)S(1)}, u32[]{:S(2)}, u32[]{:S(2)}) collective-permute-start(bf16[2,90,256]{2,1,0:T(8,128)(2,1)S(1)} %get-tuple-element.65), channel_id=1, source_target_pairs={{0,127},{1,2},{2,1},{3,4},{4,3},{5,6},{6,5},{7,8},{8,7},{9,10},{10... | collective-permute-start | bytes 276488 | tf_op jit(solution)/shard_map/ppermute | solution.py:475

commit v7 on v5

--- a/solution.py
+++ b/solution.py
@@ -173,6 +173,18 @@
         border_ref[sl, HALO:] = pick_rows(far, b, 256)
 
 
+def make_landing(lists_ref, landing_ref):
+    even = (lax.axis_index("cells") & 1) == 0
+    near = jnp.where(even, lists_ref[1:2, :], lists_ref[0:1, :]).astype(f32)
+    far = jnp.where(even, lists_ref[0:1, :], lists_ref[1:2, :]).astype(f32)
+    for side, row in enumerate((near, far)):
+        cell = to_column(row)
+        rows = slice(side * HALO, (side + 1) * HALO)
+        for c in range(8):
+            lane = (lane_iota(1, 256) + c * 256).astype(f32)
+            landing_ref[rows, c * 256 : (c + 1) * 256] = onehot(cell == lane)
+
+
 def to_column(row):
     return jnp.broadcast_to(row, (128, row.shape[1])).T[:, :1]
 
@@ -301,8 +313,8 @@
         out(jb).wait()
 
 
-def received(first, second, border):
-    return dot(first, border[:, :HALO], NT) + dot(second, border[:, HALO:], NT)
+def received(first, second, landing):
+    return dot(jnp.concatenate([first, second], axis=1), landing[...], NN)
 
 
 def push(rounded, links, first_ref, second_ref):
@@ -327,7 +339,7 @@
 def network_kernel(
     answer_ref, slot_ref, drive_ref, w_hidden_ref, w_out_ref, bias_ref, order_ref, lists_ref,
     state_ref, links_far, part_far, forcing_far,
-    groups, border, links, heat_ref, slope_ref, ahead_ref, part_ref, forcing_ref,
+    groups, border, landing, links, heat_ref, slope_ref, ahead_ref, part_ref, forcing_ref,
     sems,
 ):
     def piece(i):
@@ -348,6 +360,7 @@
 
     make_groups(order_ref(), groups)
     make_border(lists_ref(), border)
+    make_landing(lists_ref(), landing)
     slots = slot_ref()[...]
     chosen = jnp.concatenate([pick_rows(slots, b, COLS) for b in range(SLOTS // 256)], axis=0)
     u = dot(answer_ref[...], chosen, TN)
@@ -379,10 +392,10 @@
 
 
 def second_kernel(
-    first_in, second_in, border, part_in, forcing_ref, links, ahead_ref,
+    first_in, second_in, border, landing, part_in, forcing_ref, links, ahead_ref,
     adjoint_ref, heat_back_ref, temp_ref, first_ref, second_ref,
 ):
-    adjoint = part_in[...] + received(first_in[0], second_in[0], border)
+    adjoint = part_in[...] + received(first_in[0], second_in[0], landing)
     adjoint_ref[...] = adjoint
     push(adjoint.astype(bf16), links, first_ref, second_ref)
     temp = outer(ahead_ref, first_in[1], second_in[1], links)
@@ -413,10 +426,10 @@
 
 
 def third_kernel(
-    first_in, second_in, border, part_in, heat_back_ref, links, ahead_ref,
+    first_in, second_in, border, landing, part_in, heat_back_ref, links, ahead_ref,
     adjoint_ref, back_ref, temp_ref, first_ref, second_ref,
 ):
-    adjoint = part_in[...] + received(first_in[0], second_in[0], border)
+    adjoint = part_in[...] + received(first_in[0], second_in[0], landing)
     adjoint_ref[...] = adjoint
     push(adjoint.astype(bf16), links, first_ref, second_ref)
     temp = outer(ahead_ref, first_in[1], second_in[1], links)
@@ -445,12 +458,12 @@
 
 
 def finish_kernel(
-    first_in, second_in, border, part_in, links, ahead_ref, top_in, sens_in,
+    first_in, second_in, landing, part_in, links, ahead_ref, top_in, sens_in,
     sens_far, temp_far, top_ref, sem,
 ):
     temp_far.ref[...] = outer(ahead_ref, first_in[1], second_in[1], links)
     temp_far.put()
-    adjoint = part_in[...] + received(first_in[0], second_in[0], border)
+    adjoint = part_in[...] + received(first_in[0], second_in[0], landing)
     top_ref[:LEV] = (top_in[:LEV] + adjoint).astype(bf16)
     top_ref[LEV:] = top_in[LEV:].astype(bf16)
     copy = pltpu.make_async_copy(top_ref, sens_far.at[pl.ds(0, TOP)], sem)
@@ -525,7 +538,7 @@
     first, second = swap(first, second)
 
     near = (field, False)
-    groups, border, links, heat, slope, ahead, part, late_forcing = kernel(
+    groups, border, landing, links, heat, slope, ahead, part, late_forcing = kernel(
         network_kernel,
         "network",
         [
@@ -534,7 +547,8 @@
             ("raw", links), ("raw", part), ("raw", forcing),
         ],
         [
-            (all_groups, False), (all_border, False), (all_links, False), near,
+            (all_groups, False), (all_border, False), (shape((2 * HALO, CELLS), bf16), False),
+            (all_links, False), near,
             (shape((3, HID, COLS), f32), False), near, near, (shape((LEV, CELLS), bf16), False),
         ],
         scratch=[pltpu.SemaphoreType.DMA((7,))],
@@ -544,7 +558,7 @@
     adjoint, heat_back, temp, first, second = kernel(
         second_kernel,
         "second",
-        [first, second, border, part, late_forcing, links, ahead],
+        [first, second, border, landing, part, late_forcing, links, ahead],
         [near, near, near, (side, False), (side, False)],
         limit=32,
     )
@@ -555,7 +569,7 @@
     adjoint, back, temp, first, second = kernel(
         third_kernel,
         "third",
-        [first, second, border, part, heat_back, links, ahead],
+        [first, second, border, landing, part, heat_back, links, ahead],
         [near, (shape((LEV, CELLS), bf16), False), near, (side, False), (side, False)],
         limit=32,
     )
@@ -577,7 +591,7 @@
     sens, temp = kernel(
         finish_kernel,
         "finish",
-        [first, second, border, part, links, ahead, top, ("raw", sens)],
+        [first, second, landing, part, links, ahead, top, ("raw", sens)],
         [(shape((FEAT, CELLS), bf16), "raw"), (field, True)],
         scratch=[pltpu.VMEM((TOP, CELLS), bf16), pltpu.SemaphoreType.DMA],
         limit=32,

time: 82.4 us -> 81.6 us (level)
  no operation moved by 1% of the time
where the time goes in v7:
time: 81.6 us; the launch traced here: 81.2 us
  Pallas kernels  41.6 us (51%)
  starting transfers between devices  32.3 us (40%)
  waiting for transfers between devices  5.74 us (7%)
  between operations  0.96 us (1%)
    pallas_call x10, Pallas kernels, kernel(): pl.pallas_call(wrapped, out_shape=tuple(out_shapes), in_specs=in_specs, o...  41.6 us
    ppermute x3, starting transfers between devices, swap(): second = lax.ppermute(second, 'cells', far_pairs)  14.9 us
    all_to_all x1, starting transfers between devices, local(): asked = lax.all_to_all(request, 'cells', 0, 0, tiled=True)  11.1 us
    all_to_all x1, starting transfers between devices, local(): lax.all_to_all(answer.reshape(DEVS, CAP, HID), 'cells', 0, 0, tiled=True)  5.95 us
    all_to_all x1, waiting for transfers between devices, local(): asked = lax.all_to_all(request, 'cells', 0, 0, tiled=True)  3.82 us
    ppermute x3, waiting for transfers between devices, swap(): second = lax.ppermute(second, 'cells', far_pairs)  1.9 us
  transfers between devices with their start and end apart: 8, of which 2 were waited for; matrix products, arithmetic and copies ran while one was open for 0% of the time, Pallas kernels for 40%

profile of v7, /device:TPU:0, one launch (start us, length us, event | category | flops | bytes accessed | tf_op | source)
XLA Modules:
  0.0 81.2 jit_solution(10773873524317774430)
XLA Ops:
  0.6 0.0 copy-start
  0.6 0.7 copy-done
  1.3 1.2 %route.1 = (f32[128,1,128]{2,1,0:T(1,128)}, s32[1,512]{1,0:T(1,128)}) custom-call(s32[1,512]{1,0:T(1,128)S(1)} %copy-done), custom_call_target="tpu_custom_call" | custom-call | flops 10000000 | bytes 69632 | tf_op jit(solution)/shard_map/route/pallas_call | solution.py:123
  2.5 11.1 %all-to-all-start = ((f32[128,1,128]{2,1,0:T(1,128)}), f32[128,1,128]{2,1,0:T(1,128)S(1)}, u32[]{:S(2)}, u32[]{:S(2)}) async-start(f32[128,1,128]{2,1,0:T(1,128)} %get-tuple-element.39), calls=%async_computation | async-start | bytes 131072 | tf_op jit(solution)/shard_map/all_to_all | solution.py:492
  13.6 5.7 %prepare.1 = (f32[256,512]{1,0:T(8,128)}, bf16[512,256]{1,0:T(8,128)(2,1)}) custom-call(s32[1,2048]{1,0:T(1,128)} %refs_6_.1, bf16[540,2048]{1,0:T(8,128)(2,1)} %refs_8_.2, bf16[540,256]{1,0:T(8,128)(2,1)} %refs_9_.1, bf16[540,512]{1,0:T(8,128)(2,1)} %refs_3_.3, f32[3,256]{1,0:T(4,128)} %refs_5_.3, s32[1,512]{1,0:T(1,128)} %refs_5_.2, s32[1,128]{1,0:T(1,128)} %bitcast.11), custom_call_target="tpu_custom_call" | custom-call | flops 2000000000 | bytes 3841536 | tf_op jit(solution)/shard_map/prepare/pallas_call | solution.py:123
  19.3 3.8 %all-to-all-done.refs_0_ = f32[128,1,128]{2,1,0:T(1,128)S(1)} async-done(((f32[128,1,128]{2,1,0:T(1,128)}), f32[128,1,128]{2,1,0:T(1,128)S(1)}, u32[]{:S(2)}, u32[]{:S(2)}) %all-to-all-start) | async-done | bytes 65568 | tf_op jit(solution)/shard_map/all_to_all | solution.py:492
  23.1 2.4 %answer.1 = (bf16[1024,256]{1,0:T(8,128)(2,1)}, f32[1,128]{1,0:T(1,128)}) custom-call(f32[128,1,128]{2,1,0:T(1,128)S(1)} %all-to-all-done.refs_0_, bf16[512,256]{1,0:T(8,128)(2,1)} %get-tuple-element.40.refs_1_), custom_call_target="tpu_custom_call" | custom-call | flops 1000000000 | bytes 852480 | tf_op jit(solution)/shard_map/answer/pallas_call | solution.py:123
  25.6 6.0 %all-to-all-start.1 = ((bf16[128,8,256]{2,1,0:T(8,128)(2,1)}), bf16[128,8,256]{2,1,0:T(8,128)(2,1)S(1)}, u32[]{:S(2)}, u32[]{:S(2)}) async-start(bf16[128,8,256]{2,1,0:T(8,128)(2,1)} %bitcast.6), calls=%async_computation.1 | async-start | bytes 1048576 | tf_op jit(solution)/shard_map/all_to_all | solution.py:521
  31.6 9.1 %build.1 = (bf16[2560,2048]{1,0:T(8,128)(2,1)}, f32[90,2048]{1,0:T(8,128)}, bf16[2,90,256]{2,1,0:T(8,128)(2,1)}, bf16[2,90,256]{2,1,0:T(8,128)(2,1)}) custom-call(s32[6,2048]{1,0:T(8,128)} %refs_0_.5, s32[2,256]{1,0:T(2,128)} %bitcast.9, bf16[90,2048]{1,0:T(8,128)(2,1)} %refs_11_.1, bf16[540,2048]{1,0:T(8,128)(2,1)} %refs_8_.2, ...), custom_call_target="tpu_custom_call" | custom-call | flops 3000000000 | bytes 14039552 | tf_op jit(solution)/shard_map/build/pallas_call | solution.py:123
  40.6 0.1 collective-permute-start
  40.7 7.4 %collective-permute-start.1 = (bf16[2,90,256]{2,1,0:T(8,128)(2,1)}, bf16[2,90,256]{2,1,0:T(8,128)(2,1)S(1)}, u32[]{:S(2)}, u32[]{:S(2)}) collective-permute-start(bf16[2,90,256]{2,1,0:T(8,128)(2,1)} %get-tuple-element.43), channel_id=1, source_target_pairs={{0,127},{1,2},{2,1},{3,4},{4,3},{5,6},{6,5},{7,8},{8,7},{9,10},{10... | collective-permute-start | bytes 276488 | tf_op jit(solution)/shard_map/ppermute | solution.py:482
  48.1 0.0 all-to-all-done.1
  48.1 6.1 %network.1 = (bf16[512,2048]{1,0:T(8,128)(2,1)S(1)}, bf16[2048,512]{1,0:T(8,128)(2,1)S(1)}, bf16[512,2048]{1,0:T(8,128)(2,1)S(1)}, bf16[2560,2048]{1,0:T(8,128)(...) custom-call(bf16[1024,256]{1,0:T(8,128)(2,1)S(1)} %bitcast.5, ...), custom_call_target="tpu_custom_call" | custom-call | flops 5000000000 | bytes 36106240 | tf_op jit(solution)/shard_map/network/pallas_call | solution.py:123
  54.2 0.0 collective-permute-done.refs_0_
  54.3 0.0 collective-permute-done.1.refs_1_
  54.3 1.8 %second.1 = (f32[90,2048]{1,0:T(8,128)S(1)}, f32[90,2048]{1,0:T(8,128)S(1)}, f32[90,2048]{1,0:T(8,128)S(1)}, bf16[2,90,256]{2,1,0:T(8,128)(2,1)S(1)}, bf16[2,90,256]{2,1,0:T(8,128)(2,1)S(1)}) custom-call(bf16[2,90,256]{2,1,0:T(8,128)(2,1)S(1)} %collective-permute-done.refs_0_, bf16[2,90,256]{2,1,0:T(8,128)(2,1)S(1)} %collective-permute-done.1.refs_1_, ...), custom_call_target="tpu_custom_call" | custom-call | flops 1000000000 | bytes 19103744 | tf_op jit(solution)/shard_map/second/pallas_call | solution.py:123
  56.1 0.1 collective-permute-start.2
  56.2 3.6 %collective-permute-start.3 = (bf16[2,90,256]{2,1,0:T(8,128)(2,1)S(1)}, bf16[2,90,256]{2,1,0:T(8,128)(2,1)S(1)}, u32[]{:S(2)}, u32[]{:S(2)}) collective-permute-start(bf16[2,90,256]{2,1,0:T(8,128)(2,1)S(1)} %get-tuple-element.56), channel_id=1, source_target_pairs={{0,127},{1,2},{2,1},{3,4},{4,3},{5,6},{6,5},{7,8},{8,7},{9,10},{10... | collective-permute-start | bytes 276488 | tf_op jit(solution)/shard_map/ppermute | solution.py:482
  59.8 4.0 %between.1 = (f32[90,2048]{1,0:T(8,128)S(1)}, f32[90,2048]{1,0:T(8,128)S(1)}) custom-call(f32[90,2048]{1,0:T(8,128)S(1)} %get-tuple-element.57.refs_0_, f32[90,2048]{1,0:T(8,128)S(1)} %get-tuple-element.58.refs_1_, f32[90,2048]{1,0:T(8,128)S(1)} %get-tuple-element.59.refs_2_, bf16[2560,2048]{1,0:T(8,128)(2,1)S(1)} %get-tuple-element.53.refs_6_.refs_3_.refs_4_), custom_call_target="tpu_custom_call" | custom-call | flops 1000000000 | bytes 14172160 | tf_op jit(solution)/shard_map/between/pallas_call | solution.py:123
  63.8 0.0 collective-permute-done.2.refs_0_
  63.8 1.9 %collective-permute-done.3.refs_1_ = bf16[2,90,256]{2,1,0:T(8,128)(2,1)S(1)} collective-permute-done((bf16[2,90,256]{2,1,0:T(8,128)(2,1)S(1)}, bf16[2,90,256]{2,1,0:T(8,128)(2,1)S(1)}, u32[]{:S(2)}, u32[]{:S(2)}) %collective-permute-start.3) | collective-permute-done | bytes 92192 | tf_op jit(solution)/shard_map/ppermute | solution.py:482
  65.7 1.8 %third.1 = (f32[90,2048]{1,0:T(8,128)S(1)}, bf16[90,2048]{1,0:T(8,128)(2,1)S(1)}, f32[90,2048]{1,0:T(8,128)S(1)}, bf16[2,90,256]{2,1,0:T(8,128)(2,1)S(1)}, bf16[2,90,256]{2,1,0:T(8,128)(2,1)S(1)}) custom-call(bf16[2,90,256]{2,1,0:T(8,128)(2,1)S(1)} %collective-permute-done.2.refs_0_, bf16[2,90,256]{2,1,0:T(8,128)(2,1)S(1)} %collective-permute-done.3.refs_1_, ...), custom_call_target="tpu_custom_call" | custom-call | flops 1000000000 | bytes 19103744 | tf_op jit(solution)/shard_map/third/pallas_call | solution.py:123
  67.5 0.1 collective-permute-start.4
  67.6 3.9 %collective-permute-start.5 = (bf16[2,90,256]{2,1,0:T(8,128)(2,1)S(1)}, bf16[2,90,256]{2,1,0:T(8,128)(2,1)S(1)}, u32[]{:S(2)}, u32[]{:S(2)}) collective-permute-start(bf16[2,90,256]{2,1,0:T(8,128)(2,1)S(1)} %get-tuple-element.64), channel_id=1, source_target_pairs={{0,127},{1,2},{2,1},{3,4},{4,3},{5,6},{6,5},{7,8},{8,7},{9,10},{10... | collective-permute-start | bytes 276488 | tf_op jit(solution)/shard_map/ppermute | solution.py:482
  71.5 8.0 %window.1 = (bf16[540,2048]{1,0:T(8,128)(2,1)}, f32[96,2048]{1,0:T(8,128)S(1)}, f32[90,2048]{1,0:T(8,128)S(1)}, f32[90,2048]{1,0:T(8,128)S(1)}) custom-call(f32[90,2048]{1,0:T(8,128)S(1)} %get-tuple-element.65.refs_0_, f32[90,2048]{1,0:T(8,128)S(1)} %get-tuple-element.66.refs_1_, f32[90,2048]{1,0:T(8,128)S(1)} %get-tuple-element.59.refs_2_, ...), custom_call_target="tpu_custom_call" | custom-call | flops 3000000000 | bytes 21793792 | tf_op jit(solution)/shard_map/window/pallas_call | solution.py:123
  79.4 0.0 collective-permute-done.4.refs_0_
  79.5 0.0 collective-permute-done.5.refs_1_
  79.5 1.6 %finish.1 = (bf16[540,2048]{1,0:T(8,128)(2,1)}, f32[90,2048]{1,0:T(8,128)}) custom-call(bf16[2,90,256]{2,1,0:T(8,128)(2,1)S(1)} %collective-permute-done.4.refs_0_, bf16[2,90,256]{2,1,0:T(8,128)(2,1)S(1)} %collective-permute-done.5.refs_1_, bf16[512,2048]{1,0:T(8,128)(2,1)S(1)} %get-tuple-element.50.refs_3_.refs_2_, ...), custom_call_target="tpu_custom_call", output_to_operand_aliasing={{0}: (7, {})} | custom-call | flops 1000000000 | bytes 20189184 | tf_op jit(solution)/shard_map/finish/pallas_call | solution.py:123
Async XLA Ops:
  0.6 0.7 copy-start
  2.5 20.7 %all-to-all-start = ((f32[128,1,128]{2,1,0:T(1,128)}), f32[128,1,128]{2,1,0:T(1,128)S(1)}, u32[]{:S(2)}, u32[]{:S(2)}) async-start(f32[128,1,128]{2,1,0:T(1,128)} %get-tuple-element.39), calls=%async_computation | async-start | bytes 131072 | tf_op jit(solution)/shard_map/all_to_all | solution.py:492
  25.6 22.5 %all-to-all-start.1 = ((bf16[128,8,256]{2,1,0:T(8,128)(2,1)}), bf16[128,8,256]{2,1,0:T(8,128)(2,1)S(1)}, u32[]{:S(2)}, u32[]{:S(2)}) async-start(bf16[128,8,256]{2,1,0:T(8,128)(2,1)} %bitcast.6), calls=%async_computation.1 | async-start | bytes 1048576 | tf_op jit(solution)/shard_map/all_to_all | solution.py:521
  40.6 13.6 %collective-permute-start = (bf16[2,90,256]{2,1,0:T(8,128)(2,1)}, bf16[2,90,256]{2,1,0:T(8,128)(2,1)S(1)}, u32[]{:S(2)}, u32[]{:S(2)}) collective-permute-start(bf16[2,90,256]{2,1,0:T(8,128)(2,1)} %get-tuple-element.42), channel_id=1, source_target_pairs={{0,1},{1,0},{2,3},{3,2},{4,5},{5,4},{6,7},{7,6},{8,9},{9,8},{10,11... | collective-permute-start | bytes 276488 | tf_op jit(solution)/shard_map/ppermute | solution.py:483
  40.7 13.5 %collective-permute-start.1 = (bf16[2,90,256]{2,1,0:T(8,128)(2,1)}, bf16[2,90,256]{2,1,0:T(8,128)(2,1)S(1)}, u32[]{:S(2)}, u32[]{:S(2)}) collective-permute-start(bf16[2,90,256]{2,1,0:T(8,128)(2,1)} %get-tuple-element.43), channel_id=1, source_target_pairs={{0,127},{1,2},{2,1},{3,4},{4,3},{5,6},{6,5},{7,8},{8,7},{9,10},{10... | collective-permute-start | bytes 276488 | tf_op jit(solution)/shard_map/ppermute | solution.py:482
  56.1 7.7 %collective-permute-start.2 = (bf16[2,90,256]{2,1,0:T(8,128)(2,1)S(1)}, bf16[2,90,256]{2,1,0:T(8,128)(2,1)S(1)}, u32[]{:S(2)}, u32[]{:S(2)}) collective-permute-start(bf16[2,90,256]{2,1,0:T(8,128)(2,1)S(1)} %get-tuple-element.55), channel_id=1, source_target_pairs={{0,1},{1,0},{2,3},{3,2},{4,5},{5,4},{6,7},{7,6},{8,9},{9,8},{10,11... | collective-permute-start | bytes 276488 | tf_op jit(solution)/shard_map/ppermute | solution.py:483
  56.2 9.6 %collective-permute-start.3 = (bf16[2,90,256]{2,1,0:T(8,128)(2,1)S(1)}, bf16[2,90,256]{2,1,0:T(8,128)(2,1)S(1)}, u32[]{:S(2)}, u32[]{:S(2)}) collective-permute-start(bf16[2,90,256]{2,1,0:T(8,128)(2,1)S(1)} %get-tuple-element.56), channel_id=1, source_target_pairs={{0,127},{1,2},{2,1},{3,4},{4,3},{5,6},{6,5},{7,8},{8,7},{9,10},{10... | collective-permute-start | bytes 276488 | tf_op jit(solution)/shard_map/ppermute | solution.py:482
  67.5 11.9 %collective-permute-start.4 = (bf16[2,90,256]{2,1,0:T(8,128)(2,1)S(1)}, bf16[2,90,256]{2,1,0:T(8,128)(2,1)S(1)}, u32[]{:S(2)}, u32[]{:S(2)}) collective-permute-start(bf16[2,90,256]{2,1,0:T(8,128)(2,1)S(1)} %get-tuple-element.63), channel_id=1, source_target_pairs={{0,1},{1,0},{2,3},{3,2},{4,5},{5,4},{6,7},{7,6},{8,9},{9,8},{10,11... | collective-permute-start | bytes 276488 | tf_op jit(solution)/shard_map/ppermute | solution.py:483
  67.6 11.9 %collective-permute-start.5 = (bf16[2,90,256]{2,1,0:T(8,128)(2,1)S(1)}, bf16[2,90,256]{2,1,0:T(8,128)(2,1)S(1)}, u32[]{:S(2)}, u32[]{:S(2)}) collective-permute-start(bf16[2,90,256]{2,1,0:T(8,128)(2,1)S(1)} %get-tuple-element.64), channel_id=1, source_target_pairs={{0,127},{1,2},{2,1},{3,4},{4,3},{5,6},{6,5},{7,8},{8,7},{9,10},{10... | collective-permute-start | bytes 276488 | tf_op jit(solution)/shard_map/ppermute | solution.py:482
